TPU v7x, 32 devices: a whole 2x2x4 slice. The times are simulated.
32 devices in a mesh: dp: 8 (over z, y), seq: 4 (over x, core).
Axes of the slice: x: 2, y: 2, z: 4, core: 2. Of those that a mesh axis runs over, the one named last changes fastest.
Arguments:
- patches: bfloat16 [8192, 768], P(('dp', 'seq')), may hold values from -6 to 6
- image_lengths: int32 [8, 3], P('dp'), may hold values from 193 to 576, as said below
- expert_ids: int32 [8192, 2], P(('dp', 'seq')), may hold values from 0 to 31, all different within a row; in each aligned block of 256 rows (0 to 255, 256 to 511, ...) at most 17 rows name the same one
- lower_norm_gain: float32 [768], P(('dp', 'seq')), may hold values from 0.5 to 1.5
- lower_norm_shift: float32 [768], P(('dp', 'seq')), may hold values from -1.25 to 1.25
- lower_project: float32 [768, 2304], P(('dp', 'seq')), may hold values from -0.21875 to 0.21875
- lower_query_bias: float32 [768], P(('dp', 'seq')), may hold values from -1.25 to 1.25
- lower_value_bias: float32 [768], P(('dp', 'seq')), may hold values from -1.25 to 1.25
- lower_merge: float32 [768, 768], P(('dp', 'seq')), may hold values from -1.75 to 1.75
- lower_merge_bias: float32 [768], P(('dp', 'seq')), may hold values from -1.25 to 1.25
- lower_second_gain: float32 [768], P(('dp', 'seq')), may hold values from 0.5 to 1.5
- lower_second_shift: float32 [768], P(('dp', 'seq')), may hold values from -1.25 to 1.25
- lower_expand: float32 [768, 3072], P(('dp', 'seq')), may hold values from -0.21875 to 0.21875
- lower_expand_bias: float32 [3072], P(('dp', 'seq')), may hold values from -1.25 to 1.25
- lower_shrink: float32 [3072, 768], P(('dp', 'seq')), may hold values from -0.109375 to 0.109375
- lower_shrink_bias: float32 [768], P(('dp', 'seq')), may hold values from -1.25 to 1.25
- upper_norm_gain: float32 [768], P(('dp', 'seq')), may hold values from 0.5 to 1.5
- upper_norm_shift: float32 [768], P(('dp', 'seq')), may hold values from -1.25 to 1.25
- upper_project: float32 [768, 2304], P(('dp', 'seq')), may hold values from -0.21875 to 0.21875
- upper_query_bias: float32 [768], P(('dp', 'seq')), may hold values from -1.25 to 1.25
- upper_value_bias: float32 [768], P(('dp', 'seq')), may hold values from -1.25 to 1.25
- upper_merge: float32 [768, 768], P(('dp', 'seq')), may hold values from -1.75 to 1.75
- upper_merge_bias: float32 [768], P(('dp', 'seq')), may hold values from -6 to 6
- upper_second_gain: float32 [768], P(('dp', 'seq')), may hold values from 0.5 to 1.5
- upper_second_shift: float32 [768], P(('dp', 'seq')), may hold values from -1.25 to 1.25
- router: float32 [768, 32], P(('dp', 'seq')), may hold values from -0.15625 to 0.15625
- expert_expand: float32 [768, 98304], P('seq', 'dp'), may hold values from -0.21875 to 0.21875
- expert_expand_bias: float32 [98304], P(('dp', 'seq')), may hold values from -1.25 to 1.25
- expert_shrink: float32 [98304, 768], P('dp', 'seq'), may hold values from -1.25 to 1.25
- expert_shrink_bias: float32 [32, 768], P(None, ('dp', 'seq')), may hold values from -3 to 3
- output_grad: float32 [8192, 768], P(('dp', 'seq')), may hold values from -6 to 6
Outputs:
- result: float32 [8192, 768], P(('dp', 'seq'))
- delta_patches: float32 [8192, 768], P(('dp', 'seq'))
- delta_lower_norm_gain: float32 [768], P(('dp', 'seq'))
- delta_lower_norm_shift: float32 [768], P(('dp', 'seq'))
- delta_lower_project: float32 [768, 2304], P(('dp', 'seq'))
- delta_lower_query_bias: float32 [768], P(('dp', 'seq'))
- delta_lower_value_bias: float32 [768], P(('dp', 'seq'))
- delta_lower_merge: float32 [768, 768], P(('dp', 'seq'))
- delta_lower_merge_bias: float32 [768], P(('dp', 'seq'))
- delta_lower_second_gain: float32 [768], P(('dp', 'seq'))
- delta_lower_second_shift: float32 [768], P(('dp', 'seq'))
- delta_lower_expand: float32 [768, 3072], P(('dp', 'seq'))
- delta_lower_expand_bias: float32 [3072], P(('dp', 'seq'))
- delta_lower_shrink: float32 [3072, 768], P(('dp', 'seq'))
- delta_lower_shrink_bias: float32 [768], P(('dp', 'seq'))
- delta_upper_norm_gain: float32 [768], P(('dp', 'seq'))
- delta_upper_norm_shift: float32 [768], P(('dp', 'seq'))
- delta_upper_project: float32 [768, 2304], P(('dp', 'seq'))
- delta_upper_query_bias: float32 [768], P(('dp', 'seq'))
- delta_upper_value_bias: float32 [768], P(('dp', 'seq'))
- delta_upper_merge: float32 [768, 768], P(('dp', 'seq'))
- delta_upper_merge_bias: float32 [768], P(('dp', 'seq'))
- delta_upper_second_gain: float32 [768], P(('dp', 'seq'))
- delta_upper_second_shift: float32 [768], P(('dp', 'seq'))
- delta_router: float32 [768, 32], P(('dp', 'seq'))
- delta_expert_expand: float32 [768, 98304], P('seq', 'dp')
- delta_expert_expand_bias: float32 [98304], P(('dp', 'seq'))
- delta_expert_shrink: float32 [98304, 768], P('dp', 'seq')
- delta_expert_shrink_bias: float32 [32, 768], P(None, ('dp', 'seq'))
Inputs may be any that keep to these rules, and one draw needn't show every extreme that they name: `image_lengths`: row g gives the patch counts of group g's three images, laid end to end in this order over the group's 1024 patches; they sum to 1024, and the second one has exactly 576 patches and holds patches of all 4 parts of the group. `expert_ids`: each row names 2 different experts. In the rows of one device (aligned blocks of 256 rows) no expert is named by more than 17 rows, a bound that some block reaches.
All inputs are finite; a program needn't handle non-finite values.
Results may differ from a plain program's by a relative error of at most 0.039.
Values may be sent and summed in bfloat16 or wider, within the bound.
No kernel may reach another device: no remote copies, remote signals or barrier semaphores. Data moves between devices by JAX's collectives and lax.ppermute only.
A program may use at most 216 MiB of HBM per device.

v0:
```python
import math

import jax
import jax.numpy as jnp
from jax import lax
from jax.sharding import PartitionSpec as P

HEADS = 12
CAP = 17


MASKED = -1000000000.0
EPSILON = 1e-06
LOWTYPE = jnp.bfloat16
WIDE = jnp.float32


def layer_norm(inputs, gain, shift):
    center = inputs - jnp.mean(inputs, axis=-1, keepdims=True)
    spread = jnp.mean(center * center, axis=-1, keepdims=True)
    return center * lax.rsqrt(spread + EPSILON) * gain + shift


def gelu_exact(values):
    return jax.nn.gelu(values, approximate=False)


def widen(vector):
    return vector.astype(WIDE)


def product(left, right):
    return jnp.dot(left, right, preferred_element_type=WIDE)


def over_rows(left, right):
    return lax.dot_general(left, right, (((0,), (0,)), ((), ())), preferred_element_type=WIDE)


def over_features(left, right):
    return lax.dot_general(left, right, (((1,), (1,)), ((), ())), preferred_element_type=WIDE)


def image_numbers(lengths, places):
    first_end = lengths[0]
    second_end = lengths[0] + lengths[1]
    return (places >= first_end).astype(jnp.int32) + (places >= second_end).astype(jnp.int32)


def masked_scores(query_heads, key_heads, query_numbers, key_numbers, scale):
    scores = jnp.einsum("qhd,khd->hqk", query_heads, key_heads, preferred_element_type=WIDE) * scale
    same_image = query_numbers[:, None] == key_numbers[None, :]
    return jnp.where(same_image[None], scores, MASKED)


def attend(query_heads, key_heads, value_heads, query_numbers, key_numbers, scale):
    scores = masked_scores(query_heads, key_heads, query_numbers, key_numbers, scale)
    highest = jnp.max(scores, axis=-1, keepdims=True)
    raised = jnp.exp(scores - highest)
    totals = jnp.sum(raised, axis=-1, keepdims=True)
    weights_low = (raised / totals).astype(LOWTYPE)
    attended = jnp.einsum("hqk,khd->qhd", weights_low, value_heads, preferred_element_type=WIDE)
    return (attended, highest + jnp.log(totals))


def attend_back(
    query_heads,
    key_heads,
    value_heads,
    grad_heads,
    attended_heads,
    log_totals,
    query_numbers,
    key_numbers,
    scale,
):
    row_delta = jnp.sum(grad_heads.astype(WIDE) * attended_heads, axis=-1).T[:, :, None]
    scores = masked_scores(query_heads, key_heads, query_numbers, key_numbers, scale)
    probs = jnp.exp(scores - log_totals)
    dprobs = jnp.einsum("qhd,khd->hqk", grad_heads, value_heads, preferred_element_type=WIDE)
    dscores = (probs * (dprobs - row_delta)).astype(LOWTYPE)
    dquery = scale * jnp.einsum("hqk,khd->qhd", dscores, key_heads, preferred_element_type=WIDE)
    dkey = scale * jnp.einsum("hqk,qhd->khd", dscores, query_heads, preferred_element_type=WIDE)
    dvalue = jnp.einsum(
        "hqk,qhd->khd", probs.astype(LOWTYPE), grad_heads, preferred_element_type=WIDE
    )
    return (dquery, dkey, dvalue)


def attention_forward(
    residual, lengths, gain, shift, project, query_bias, value_bias, merge, merge_bias
):
    rows, width = residual.shape
    head_dim = width // HEADS
    scale = 1.0 / math.sqrt(head_dim)
    lowered = layer_norm(residual, gain, shift).astype(LOWTYPE)
    query_numbers = image_numbers(
        lengths, lax.axis_index("seq") * rows + jnp.arange(rows, dtype=jnp.int32)
    )
    heads_here = width // head_dim
    packed = product(lowered, project)
    queries = (packed[:, :width] + query_bias).astype(LOWTYPE)
    key_rows = packed[:, width : 2 * width].astype(LOWTYPE)
    value_rows = (packed[:, 2 * width :] + value_bias).astype(LOWTYPE)
    all_keys, all_values = (
        lax.all_gather(key_rows, "seq", axis=0, tiled=True),
        lax.all_gather(value_rows, "seq", axis=0, tiled=True),
    )
    key_numbers = image_numbers(lengths, jnp.arange(all_keys.shape[0], dtype=jnp.int32))
    count = queries.shape[0]
    attended, log_totals = attend(
        queries.reshape(count, heads_here, head_dim),
        all_keys.reshape(-1, heads_here, head_dim),
        all_values.reshape(-1, heads_here, head_dim),
        query_numbers,
        key_numbers,
        scale,
    )
    attended = attended.reshape(count, width)
    attended_low = attended.astype(LOWTYPE)
    partial_value = product(attended_low, merge)
    saved = (
        lowered,
        queries,
        all_keys,
        all_values,
        log_totals,
        attended,
        attended_low,
        query_numbers,
        key_numbers,
    )
    return (residual + partial_value + merge_bias, saved)


def attention_backward(delta_resid, residual, saved, gain, shift, project, merge):
    (
        source,
        queries,
        all_keys,
        all_values,
        log_totals,
        attended,
        attended_low,
        query_numbers,
        key_numbers,
    ) = saved
    rows, width = delta_resid.shape
    head_dim = width // HEADS
    scale = 1.0 / math.sqrt(head_dim)
    share = attended.shape[1]
    heads_here = share // head_dim
    dmerged = delta_resid.astype(LOWTYPE)
    delta_merge_bias = jnp.sum(dmerged.astype(WIDE), axis=0)
    delta_merge = over_rows(attended_low, dmerged)
    dattended = over_features(dmerged, merge).astype(LOWTYPE)
    count = dattended.shape[0]
    dquery, dkey, dvalue = attend_back(
        queries.reshape(count, heads_here, head_dim),
        all_keys.reshape(-1, heads_here, head_dim),
        all_values.reshape(-1, heads_here, head_dim),
        dattended.reshape(count, heads_here, head_dim),
        attended.reshape(count, heads_here, head_dim),
        log_totals,
        query_numbers,
        key_numbers,
        scale,
    )
    keys_count = all_keys.shape[0]
    dpairs = jnp.concatenate(
        [dkey.reshape(keys_count, share), dvalue.reshape(keys_count, share)], axis=1
    )
    dpairs_low = (
        lax.psum_scatter(dpairs.astype(jnp.bfloat16), "seq", scatter_dimension=0, tiled=True)
        .astype(jnp.float32)
        .astype(LOWTYPE)
    )
    dquery_low = dquery.reshape(count, share).astype(LOWTYPE)
    dpacked = jnp.concatenate([dquery_low, dpairs_low], axis=1)
    delta_project = over_rows(source, dpacked)
    delta_query_bias = jnp.sum(dquery_low.astype(WIDE), axis=0)
    delta_value_bias = jnp.sum(dpairs_low[:, share:].astype(WIDE), axis=0)
    dnormed = over_features(dpacked, project)
    _, pullback = jax.vjp(layer_norm, residual, gain, shift)
    delta_input, delta_gain, delta_shift = pullback(dnormed)
    return (
        delta_resid + delta_input,
        (
            delta_gain,
            delta_shift,
            delta_project,
            delta_query_bias,
            delta_value_bias,
            delta_merge,
            delta_merge_bias,
        ),
    )


def mlp_forward(residual, gain, shift, expand, expand_bias, shrink, shrink_bias):
    lowered = layer_norm(residual, gain, shift).astype(LOWTYPE)
    before = product(lowered, expand) + expand_bias
    hidden = gelu_exact(before).astype(LOWTYPE)
    partial_value = product(hidden, shrink)
    return (residual + partial_value + shrink_bias, (lowered, before, hidden))


def mlp_backward(delta_resid, residual, saved, gain, shift, expand, shrink):
    source, before, hidden = saved
    delta_out = delta_resid.astype(LOWTYPE)
    delta_shrink_bias = jnp.sum(delta_out.astype(WIDE), axis=0)
    delta_shrink = over_rows(hidden, delta_out)
    _, gelu_back = jax.vjp(gelu_exact, before)
    dbefore = gelu_back(over_features(delta_out, shrink))[0].astype(LOWTYPE)
    delta_expand = over_rows(source, dbefore)
    delta_expand_bias = jnp.sum(dbefore.astype(WIDE), axis=0)
    dnormed = over_features(dbefore, expand)
    _, pullback = jax.vjp(layer_norm, residual, gain, shift)
    delta_input, delta_gain, delta_shift = pullback(dnormed)
    return (
        delta_resid + delta_input,
        (delta_gain, delta_shift, delta_expand, delta_expand_bias, delta_shrink, delta_shrink_bias),
    )


def routing(expert_rows, experts):
    chosen = (
        expert_rows[:, :, None] == jnp.arange(experts, dtype=jnp.int32)[None, None, :]
    ).astype(jnp.int32)
    per_row = jnp.sum(chosen, axis=1)
    earlier = jnp.cumsum(per_row, axis=0) - per_row
    slots = jnp.sum(chosen * earlier[:, None, :], axis=2)
    return (chosen, slots)


def send_places(expert_rows, slots, experts, devices):
    copies = max(devices // experts, 1)
    local_count = max(experts // devices, 1)
    places = []
    for replica in range(copies):
        target = expert_rows * copies + replica
        places.append(
            ((target % local_count * devices + target // local_count) * CAP + slots).reshape(-1)
        )
    return places


def fill_buffer(flat_rows, places, total, width):
    buffer = jnp.zeros((total, width), flat_rows.dtype)
    for place in places:
        buffer = buffer.at[place].set(flat_rows)
    return buffer


def collect_rows(buffer, places, tokens, chosen_count):
    summed = buffer[places[0]]
    for place in places[1:]:
        summed = summed + buffer[place]
    return summed.reshape(tokens, chosen_count, -1)


def to_experts(buffer):
    return lax.all_to_all(buffer, "dp", split_axis=1, concat_axis=1, tiled=True)


def to_patches(buffer):
    return lax.all_to_all(
        buffer.astype(jnp.bfloat16), "dp", split_axis=1, concat_axis=1, tiled=True
    ).astype(buffer.dtype)


def expert_forward(
    residual, expert_rows, gain, shift, router, expand_all, expand_bias_all, shrink_all, shrink_bias
):
    tokens, width = residual.shape
    chosen_count = expert_rows.shape[1]
    experts = router.shape[1]
    devices = lax.axis_size("dp")
    local_count = max(experts // devices, 1)
    hidden_each = expand_all.shape[1] // local_count
    total_slots = local_count * devices * CAP
    lowered = layer_norm(residual, gain, shift).astype(LOWTYPE)
    logits = product(lowered, router)
    raised = jnp.exp(logits - jnp.max(logits, axis=1, keepdims=True))
    probs = raised / jnp.sum(raised, axis=1, keepdims=True)
    chosen, slots = routing(expert_rows, experts)
    gating = jnp.sum(chosen.astype(WIDE) * probs[:, None, :], axis=2)
    places = send_places(expert_rows, slots, experts, devices)
    repeated = jnp.broadcast_to(lowered[:, None, :], (tokens, chosen_count, width)).reshape(
        -1, width
    )
    outgoing = fill_buffer(repeated, places, total_slots, width)
    arrived = to_experts(outgoing.reshape(local_count, devices, CAP, width)).reshape(
        local_count, devices * CAP, width
    )
    expand_parts = expand_all.reshape(width, local_count, hidden_each)
    shrink_parts = shrink_all.reshape(local_count, hidden_each, width)
    before = jnp.einsum("erd,def->erf", arrived, expand_parts, preferred_element_type=WIDE) + widen(
        expand_bias_all
    ).reshape(local_count, 1, hidden_each)
    hidden = gelu_exact(before).astype(LOWTYPE)
    partial_out = jnp.einsum("erf,efd->erd", hidden, shrink_parts, preferred_element_type=WIDE)
    returned = to_patches(partial_out.reshape(local_count, devices, CAP, width)).reshape(
        total_slots, width
    )
    picked = collect_rows(returned, places, tokens, chosen_count) + jnp.einsum(
        "tke,ed->tkd", chosen.astype(LOWTYPE), shrink_bias, preferred_element_type=WIDE
    )
    output = residual + jnp.sum(gating[:, :, None] * picked, axis=1)
    return (output, (lowered, probs, chosen, gating, places, arrived, before, hidden, picked))


def expert_backward(delta_resid, residual, saved, gain, shift, router, expand_all, shrink_all):
    lowered, probs, chosen, gating, places, arrived, before, hidden, picked = saved
    tokens, width = delta_resid.shape
    chosen_count = chosen.shape[1]
    experts = router.shape[1]
    devices = lax.axis_size("dp")
    local_count = max(experts // devices, 1)
    hidden_each = expand_all.shape[1] // local_count
    total_slots = local_count * devices * CAP
    delta_gate = jnp.sum(delta_resid[:, None, :] * picked, axis=2)
    dpicked = (gating[:, :, None] * delta_resid[:, None, :]).astype(LOWTYPE)
    delta_shrink_bias = jnp.einsum(
        "tke,tkd->ed", chosen.astype(LOWTYPE), dpicked, preferred_element_type=WIDE
    )
    outgoing = fill_buffer(dpicked.reshape(-1, width), places, total_slots, width)
    dpartial = to_experts(outgoing.reshape(local_count, devices, CAP, width)).reshape(
        local_count, devices * CAP, width
    )
    expand_parts = expand_all.reshape(width, local_count, hidden_each)
    shrink_parts = shrink_all.reshape(local_count, hidden_each, width)
    delta_shrink = jnp.einsum(
        "erf,erd->efd", hidden, dpartial, preferred_element_type=WIDE
    ).reshape(-1, width)
    _, gelu_back = jax.vjp(gelu_exact, before)
    dbefore = gelu_back(
        jnp.einsum("erd,efd->erf", dpartial, shrink_parts, preferred_element_type=WIDE)
    )[0].astype(LOWTYPE)
    delta_expand = jnp.einsum(
        "erd,erf->def", arrived, dbefore, preferred_element_type=WIDE
    ).reshape(width, -1)
    delta_expand_bias = jnp.sum(dbefore.astype(WIDE), axis=1).reshape(-1)
    darrived = jnp.einsum("erf,def->erd", dbefore, expand_parts, preferred_element_type=WIDE)
    dreturned = to_patches(darrived.reshape(local_count, devices, CAP, width)).reshape(
        total_slots, width
    )
    dnormed = jnp.sum(collect_rows(dreturned, places, tokens, chosen_count), axis=1)
    dprobs = jnp.sum(delta_gate[:, :, None] * chosen.astype(WIDE), axis=1)
    dlogits = (probs * (dprobs - jnp.sum(probs * dprobs, axis=1, keepdims=True))).astype(LOWTYPE)
    delta_router = over_rows(lowered, dlogits)
    dnormed = dnormed + over_features(dlogits, router)
    _, pullback = jax.vjp(layer_norm, residual, gain, shift)
    delta_input, delta_gain, delta_shift = pullback(dnormed)
    return (
        delta_resid + delta_input,
        (
            delta_gain,
            delta_shift,
            delta_router,
            delta_expand,
            delta_expand_bias,
            delta_shrink,
            delta_shrink_bias,
        ),
    )


def forward_pass(inputs, lengths, expert_ids, dense, expert):
    first, saved_first = attention_forward(
        inputs,
        lengths,
        widen(dense[0]),
        widen(dense[1]),
        dense[2],
        widen(dense[3]),
        widen(dense[4]),
        dense[5],
        widen(dense[6]),
    )
    second, saved_mlp = mlp_forward(
        first,
        widen(dense[7]),
        widen(dense[8]),
        dense[9],
        widen(dense[10]),
        dense[11],
        widen(dense[12]),
    )
    third, saved_second = attention_forward(
        second,
        lengths,
        widen(dense[13]),
        widen(dense[14]),
        dense[15],
        widen(dense[16]),
        widen(dense[17]),
        dense[18],
        widen(dense[19]),
    )
    output, saved_expert = expert_forward(
        third,
        expert_ids,
        widen(dense[20]),
        widen(dense[21]),
        dense[22],
        expert[0],
        expert[1],
        expert[2],
        dense[23],
    )
    return (
        output,
        (inputs, first, second, third, saved_first, saved_mlp, saved_second, saved_expert),
    )


def backward_pass(output_grad, dense, expert, saved):
    inputs, first, second, third, saved_first, saved_mlp, saved_second, saved_expert = saved
    delta_third, grads_expert = expert_backward(
        output_grad,
        third,
        saved_expert,
        widen(dense[20]),
        widen(dense[21]),
        dense[22],
        expert[0],
        expert[2],
    )
    delta_second, grads_upper = attention_backward(
        delta_third, second, saved_second, widen(dense[13]), widen(dense[14]), dense[15], dense[18]
    )
    delta_first, grads_mlp = mlp_backward(
        delta_second, first, saved_mlp, widen(dense[7]), widen(dense[8]), dense[9], dense[11]
    )
    delta_inputs, grads_lower = attention_backward(
        delta_first, inputs, saved_first, widen(dense[0]), widen(dense[1]), dense[2], dense[5]
    )
    return (delta_inputs, grads_lower + grads_mlp + grads_upper + grads_expert)


def local(
    patches,
    image_lengths,
    expert_ids,
    lower_norm_gain,
    lower_norm_shift,
    lower_project,
    lower_query_bias,
    lower_value_bias,
    lower_merge,
    lower_merge_bias,
    lower_second_gain,
    lower_second_shift,
    lower_expand,
    lower_expand_bias,
    lower_shrink,
    lower_shrink_bias,
    upper_norm_gain,
    upper_norm_shift,
    upper_project,
    upper_query_bias,
    upper_value_bias,
    upper_merge,
    upper_merge_bias,
    upper_second_gain,
    upper_second_shift,
    router,
    expert_expand,
    expert_expand_bias,
    expert_shrink,
    expert_shrink_bias,
    output_grad,
):
    lengths = image_lengths[0]

    def gather_weights():
        dense = (
            lax.all_gather(lower_norm_gain.astype(LOWTYPE), ("dp", "seq"), axis=0, tiled=True),
            lax.all_gather(lower_norm_shift.astype(LOWTYPE), ("dp", "seq"), axis=0, tiled=True),
            lax.all_gather(lower_project.astype(LOWTYPE), ("dp", "seq"), axis=0, tiled=True),
            lax.all_gather(lower_query_bias.astype(LOWTYPE), ("dp", "seq"), axis=0, tiled=True),
            lax.all_gather(lower_value_bias.astype(LOWTYPE), ("dp", "seq"), axis=0, tiled=True),
            lax.all_gather(lower_merge.astype(LOWTYPE), ("dp", "seq"), axis=0, tiled=True),
            lax.all_gather(lower_merge_bias.astype(LOWTYPE), ("dp", "seq"), axis=0, tiled=True),
            lax.all_gather(lower_second_gain.astype(LOWTYPE), ("dp", "seq"), axis=0, tiled=True),
            lax.all_gather(lower_second_shift.astype(LOWTYPE), ("dp", "seq"), axis=0, tiled=True),
            lax.all_gather(lower_expand.astype(LOWTYPE), ("dp", "seq"), axis=0, tiled=True),
            lax.all_gather(lower_expand_bias.astype(LOWTYPE), ("dp", "seq"), axis=0, tiled=True),
            lax.all_gather(lower_shrink.astype(LOWTYPE), ("dp", "seq"), axis=0, tiled=True),
            lax.all_gather(lower_shrink_bias.astype(LOWTYPE), ("dp", "seq"), axis=0, tiled=True),
            lax.all_gather(upper_norm_gain.astype(LOWTYPE), ("dp", "seq"), axis=0, tiled=True),
            lax.all_gather(upper_norm_shift.astype(LOWTYPE), ("dp", "seq"), axis=0, tiled=True),
            lax.all_gather(upper_project.astype(LOWTYPE), ("dp", "seq"), axis=0, tiled=True),
            lax.all_gather(upper_query_bias.astype(LOWTYPE), ("dp", "seq"), axis=0, tiled=True),
            lax.all_gather(upper_value_bias.astype(LOWTYPE), ("dp", "seq"), axis=0, tiled=True),
            lax.all_gather(upper_merge.astype(LOWTYPE), ("dp", "seq"), axis=0, tiled=True),
            lax.all_gather(upper_merge_bias.astype(LOWTYPE), ("dp", "seq"), axis=0, tiled=True),
            lax.all_gather(upper_second_gain.astype(LOWTYPE), ("dp", "seq"), axis=0, tiled=True),
            lax.all_gather(upper_second_shift.astype(LOWTYPE), ("dp", "seq"), axis=0, tiled=True),
            lax.all_gather(router.astype(LOWTYPE), ("dp", "seq"), axis=0, tiled=True),
            lax.all_gather(expert_shrink_bias.astype(LOWTYPE), ("dp", "seq"), axis=1, tiled=True),
        )
        expert = (
            lax.all_gather(expert_expand.astype(LOWTYPE), "seq", axis=0, tiled=True),
            lax.all_gather(expert_expand_bias.astype(LOWTYPE), "seq", axis=0, tiled=True),
            lax.all_gather(expert_shrink.astype(LOWTYPE), "seq", axis=1, tiled=True),
        )
        return (dense, expert)

    dense, expert = gather_weights()
    output, saved = forward_pass(patches.astype(WIDE), lengths, expert_ids, dense, expert)
    dense, expert = gather_weights()
    delta_inputs, gradients = backward_pass(output_grad, dense, expert, saved)
    expert_summed = (
        lax.psum_scatter(
            gradients[23].astype(jnp.bfloat16), "seq", scatter_dimension=0, tiled=True
        ).astype(jnp.float32),
        lax.psum_scatter(
            gradients[24].astype(jnp.bfloat16), "seq", scatter_dimension=0, tiled=True
        ).astype(jnp.float32),
        lax.psum_scatter(
            gradients[25].astype(jnp.bfloat16), "seq", scatter_dimension=1, tiled=True
        ).astype(jnp.float32),
    )
    summed = (
        lax.psum_scatter(gradients[0], ("dp", "seq"), scatter_dimension=0, tiled=True),
        lax.psum_scatter(gradients[1], ("dp", "seq"), scatter_dimension=0, tiled=True),
        lax.psum_scatter(gradients[2], ("dp", "seq"), scatter_dimension=0, tiled=True),
        lax.psum_scatter(gradients[3], ("dp", "seq"), scatter_dimension=0, tiled=True),
        lax.psum_scatter(gradients[4], ("dp", "seq"), scatter_dimension=0, tiled=True),
        lax.psum_scatter(gradients[5], ("dp", "seq"), scatter_dimension=0, tiled=True),
        lax.psum_scatter(gradients[6], ("dp", "seq"), scatter_dimension=0, tiled=True),
        lax.psum_scatter(gradients[7], ("dp", "seq"), scatter_dimension=0, tiled=True),
        lax.psum_scatter(gradients[8], ("dp", "seq"), scatter_dimension=0, tiled=True),
        lax.psum_scatter(gradients[9], ("dp", "seq"), scatter_dimension=0, tiled=True),
        lax.psum_scatter(gradients[10], ("dp", "seq"), scatter_dimension=0, tiled=True),
        lax.psum_scatter(gradients[11], ("dp", "seq"), scatter_dimension=0, tiled=True),
        lax.psum_scatter(gradients[12], ("dp", "seq"), scatter_dimension=0, tiled=True),
        lax.psum_scatter(gradients[13], ("dp", "seq"), scatter_dimension=0, tiled=True),
        lax.psum_scatter(gradients[14], ("dp", "seq"), scatter_dimension=0, tiled=True),
        lax.psum_scatter(gradients[15], ("dp", "seq"), scatter_dimension=0, tiled=True),
        lax.psum_scatter(gradients[16], ("dp", "seq"), scatter_dimension=0, tiled=True),
        lax.psum_scatter(gradients[17], ("dp", "seq"), scatter_dimension=0, tiled=True),
        lax.psum_scatter(gradients[18], ("dp", "seq"), scatter_dimension=0, tiled=True),
        lax.psum_scatter(gradients[19], ("dp", "seq"), scatter_dimension=0, tiled=True),
        lax.psum_scatter(gradients[20], ("dp", "seq"), scatter_dimension=0, tiled=True),
        lax.psum_scatter(gradients[21], ("dp", "seq"), scatter_dimension=0, tiled=True),
        lax.psum_scatter(gradients[22], ("dp", "seq"), scatter_dimension=0, tiled=True),
        lax.psum_scatter(gradients[26], ("dp", "seq"), scatter_dimension=1, tiled=True),
    )
    return (
        output,
        delta_inputs,
        summed[0],
        summed[1],
        summed[2],
        summed[3],
        summed[4],
        summed[5],
        summed[6],
        summed[7],
        summed[8],
        summed[9],
        summed[10],
        summed[11],
        summed[12],
        summed[13],
        summed[14],
        summed[15],
        summed[16],
        summed[17],
        summed[18],
        summed[19],
        summed[20],
        summed[21],
        summed[22],
        expert_summed[0],
        expert_summed[1],
        expert_summed[2],
        summed[23],
    )


def solution(mesh):
    in_specs = (
        P(("dp", "seq"), None),
        P("dp", None),
        P(("dp", "seq"), None),
        P(("dp", "seq")),
        P(("dp", "seq")),
        P(("dp", "seq"), None),
        P(("dp", "seq")),
        P(("dp", "seq")),
        P(("dp", "seq"), None),
        P(("dp", "seq")),
        P(("dp", "seq")),
        P(("dp", "seq")),
        P(("dp", "seq"), None),
        P(("dp", "seq")),
        P(("dp", "seq"), None),
        P(("dp", "seq")),
        P(("dp", "seq")),
        P(("dp", "seq")),
        P(("dp", "seq"), None),
        P(("dp", "seq")),
        P(("dp", "seq")),
        P(("dp", "seq"), None),
        P(("dp", "seq")),
        P(("dp", "seq")),
        P(("dp", "seq")),
        P(("dp", "seq"), None),
        P("seq", "dp"),
        P(("dp", "seq")),
        P("dp", "seq"),
        P(None, ("dp", "seq")),
        P(("dp", "seq"), None),
    )
    out_specs = (
        P(("dp", "seq"), None),
        P(("dp", "seq"), None),
        P(("dp", "seq")),
        P(("dp", "seq")),
        P(("dp", "seq"), None),
        P(("dp", "seq")),
        P(("dp", "seq")),
        P(("dp", "seq"), None),
        P(("dp", "seq")),
        P(("dp", "seq")),
        P(("dp", "seq")),
        P(("dp", "seq"), None),
        P(("dp", "seq")),
        P(("dp", "seq"), None),
        P(("dp", "seq")),
        P(("dp", "seq")),
        P(("dp", "seq")),
        P(("dp", "seq"), None),
        P(("dp", "seq")),
        P(("dp", "seq")),
        P(("dp", "seq"), None),
        P(("dp", "seq")),
        P(("dp", "seq")),
        P(("dp", "seq")),
        P(("dp", "seq"), None),
        P("seq", "dp"),
        P(("dp", "seq")),
        P("dp", "seq"),
        P(None, ("dp", "seq")),
    )
    return jax.shard_map(local, mesh=mesh, in_specs=in_specs, out_specs=out_specs, check_vma=False)
```

profile of v0, /device:TPU:9, one launch (start us, length us, event | category | flops | bytes accessed | tf_op | source)
XLA Modules:
  0.0 2248.7 jit_solution(10368945430563189235)
XLA Ops:
  22.7 41.7 %all-reduce.36 = (bf16[768]{0:T(1024)(128)(2,1)S(1)}, bf16[768]{0:T(1024)(128)(2,1)S(1)}, bf16[768]{0:T(1024)(128)(2,1)S(1)}, bf16[768]{0:T(1024)(128)(2,1)S(1)}...) all-reduce(bf16[768]{0:T(1024)(128)(2,1)S(1)} %dynamic-update-slice, ...), channel_id=1, replica_groups=mesh['dp'=8,'seq'=4] {'dp','seq'}, use_global_device_ids=true, to_apply=%add.1 | all-reduce | flops 14592 | bytes 58368
  105.1 13.4 all-gather.15.cloned.1.call-done
  133.8 41.3 %all-gather.19.cloned.1.call-done = bf16[768,768]{1,0:T(8,128)(2,1)} async-done(((bf16[24,768]{1,0:T(8,128)(2,1)}), bf16[768,768]{1,0:T(8,128)(2,1)}) %all-gather.19.cloned.1.call-update) | async-done | bytes 1179664 | tf_op jit(solution)/shard_map/all_gather | solution.py:484
  177.2 65.1 %all-gather.21.cloned.1.call-done = bf16[768,3072]{1,0:T(8,128)(2,1)} async-done(((bf16[24,3072]{1,0:T(8,128)(2,1)}), bf16[768,3072]{1,0:T(8,128)(2,1)}) %all-gather.21.cloned.1.call-update) | async-done | bytes 4718608 | tf_op jit(solution)/shard_map/all_gather | solution.py:488
  253.7 54.5 %all-gather.23.cloned.1.call-done = bf16[3072,768]{1,0:T(8,128)(2,1)} async-done(((bf16[96,768]{1,0:T(8,128)(2,1)}), bf16[3072,768]{1,0:T(8,128)(2,1)}) %all-gather.23.cloned.1.call-update) | async-done | bytes 4718608 | tf_op jit(solution)/shard_map/all_gather | solution.py:490
  312.2 57.3 %all-gather.25.cloned.1.call-done = bf16[768,2304]{1,0:T(8,128)(2,1)} async-done(((bf16[24,2304]{1,0:T(8,128)(2,1)}), bf16[768,2304]{1,0:T(8,128)(2,1)}) %all-gather.25.cloned.1.call-update) | async-done | bytes 3538960 | tf_op jit(solution)/shard_map/all_gather | solution.py:494
  395.5 18.7 all-gather.29.cloned.1.call-done
  427.6 43.0 %all-gather.31.cloned.1.call-done = bf16[768,768]{1,0:T(8,128)(2,1)} async-done(((bf16[24,768]{1,0:T(8,128)(2,1)}), bf16[768,768]{1,0:T(8,128)(2,1)}) %all-gather.31.cloned.1.call-update) | async-done | bytes 1179664 | tf_op jit(solution)/shard_map/all_gather | solution.py:497
  493.6 37.5 %all_gather.132 = bf16[768,32]{1,0:T(8,128)(2,1)S(1)} all-gather(bf16[24,32]{1,0:T(8,128)(2,1)} %convert_element_type.450), channel_id=1, replica_groups=mesh['dp'=8,'seq'=4] {'dp','seq'}, dimensions={0}, use_global_device_ids=true | all-gather | bytes 50688 | tf_op jit(solution)/shard_map/all_gather | solution.py:501
  537.9 56.8 %all-gather.33.cloned.1.call-done = bf16[768,12288]{1,0:T(8,128)(2,1)} async-done(((bf16[192,12288]{1,0:T(8,128)(2,1)}), bf16[768,12288]{1,0:T(8,128)(2,1)}) %all-gather.33.cloned.1.call-update) | async-done | bytes 18874384 | tf_op jit(solution)/shard_map/all_gather | solution.py:505
  594.7 25.2 %copy.218 = bf16[768,12288]{0,1:T(8,128)(2,1)} copy(bf16[768,12288]{1,0:T(8,128)(2,1)} %all-gather.33.cloned.1.call-done) | data formatting | bytes 37748736 | tf_op jit(solution)/shard_map/all_gather | solution.py:505
  625.4 13.4 fusion.33
  638.8 17.4 multiply_convert_fusion.2
  656.2 60.0 %all-gather.35.cloned.1.call-done = bf16[12288,768]{0,1:T(8,128)(2,1)} async-done(((bf16[12288,192]{0,1:T(8,128)(2,1)}), bf16[12288,768]{0,1:T(8,128)(2,1)}) %all-gather.35.cloned.1.call-update) | async-done | bytes 18874384 | tf_op jit(solution)/shard_map/all_gather | solution.py:507
  716.3 24.6 %copy.221 = bf16[12288,768]{1,0:T(8,128)(2,1)} copy(bf16[12288,768]{0,1:T(8,128)(2,1)} %all-gather.35.cloned.1.call-done) | data formatting | bytes 37748736 | tf_op jit(solution)/shard_map/all_gather | solution.py:507
  740.9 16.1 fusion.133
  799.1 48.0 %all_gather.136 = bf16[32,768]{0,1:T(8,128)(2,1)} all-gather(bf16[32,24]{0,1:T(8,128)(2,1)S(1)} %convert_element_type.458), channel_id=1, replica_groups=mesh['dp'=8,'seq'=4] {'dp','seq'}, dimensions={1}, use_global_device_ids=true | all-gather | bytes 50688 | tf_op jit(solution)/shard_map/all_gather | solution.py:502
  908.5 32.0 %reduce-scatter.17.cloned.1.call-done = bf16[256,1536]{0,1:T(8,128)(2,1)} async-done(((bf16[1024,1536]{0,1:T(8,128)(2,1)}), bf16[256,1536]{0,1:T(8,128)(2,1)}) %reduce-scatter.17.cloned.1.call-update) | async-done | bytes 786448 | tf_op jit(solution)/shard_map/reduce_scatter | solution.py:174
  978.3 11.4 convolution_convert_fusion
  989.7 24.8 %copy.239 = bf16[12288,768]{0,1:T(8,128)(2,1)} copy(bf16[12288,768]{1,0:T(8,128)(2,1)} %bitcast.138) | data formatting | bytes 37748736 | tf_op jit(solution)/shard_map/convert_element_type | solution.py:523
  1016.5 12.1 convolution_convert_fusion.1
  1028.6 26.0 %copy.237 = bf16[768,12288]{1,0:T(8,128)(2,1)} copy(bf16[768,12288]{0,1:T(8,128)(2,1)} %bitcast.139) | data formatting | bytes 37748736 | tf_op jit(solution)/shard_map/convert_element_type | solution.py:517
  1113.8 43.4 %all-reduce.35 = (f32[768]{0:T(1024)S(1)}, f32[768]{0:T(1024)S(1)}, f32[768]{0:T(1024)S(1)}, f32[768]{0:T(1024)S(1)}, f32[768]{0:T(1024)S(1)}, /*index=5*/f32[76...) all-reduce(f32[768]{0:T(1024)S(1)} %get-tuple-element.39, ...), channel_id=4, replica_groups=mesh['dp'=8,'seq'=4] {'dp','seq'}, use_global_device_ids=true, to_apply=%region_39.40.clone | all-reduce | flops 14592 | bytes 116736
  1177.2 124.2 %reduce-scatter.33.cloned.1.call-done = bf16[192,12288]{1,0:T(8,128)(2,1)} async-done(((bf16[768,12288]{1,0:T(8,128)(2,1)}), bf16[192,12288]{1,0:T(8,128)(2,1)}) %reduce-scatter.33.cloned.1.call-update) | async-done | bytes 4718608 | tf_op jit(solution)/shard_map/reduce_scatter | solution.py:516
  1308.5 91.0 %reduce-scatter.39.cloned.1.call-done = f32[32,24]{0,1:T(8,128)} async-done(((f32[32,768]{0,1:T(8,128)}), f32[32,24]{0,1:T(8,128)}) %reduce-scatter.39.cloned.1.call-update) | async-done | bytes 3088
  1399.5 100.1 %reduce-scatter.37.cloned.1.call-done = f32[24,32]{1,0:T(8,128)} async-done(((f32[768,32]{1,0:T(8,128)}), f32[24,32]{1,0:T(8,128)}) %reduce-scatter.37.cloned.1.call-update) | async-done | bytes 3088
  1499.6 104.4 %reduce-scatter.31.cloned.1.call-done = f32[24,768]{1,0:T(8,128)} async-done(((f32[768,768]{1,0:T(8,128)}), f32[24,768]{1,0:T(8,128)}) %reduce-scatter.31.cloned.1.call-update) | async-done | bytes 73744 | tf_op jit(solution)/shard_map/reduce_scatter | solution.py:545
  1604.0 104.6 %reduce-scatter.23.cloned.1.call-done = f32[24,768]{1,0:T(8,128)} async-done(((f32[768,768]{1,0:T(8,128)}), f32[24,768]{1,0:T(8,128)}) %reduce-scatter.23.cloned.1.call-update) | async-done | bytes 73744 | tf_op jit(solution)/shard_map/reduce_scatter | solution.py:532
  1708.6 124.3 %reduce-scatter.29.cloned.1.call-done = f32[24,2304]{1,0:T(8,128)} async-done(((f32[768,2304]{1,0:T(8,128)}), f32[24,2304]{1,0:T(8,128)}) %reduce-scatter.29.cloned.1.call-update) | async-done | bytes 221200 | tf_op jit(solution)/shard_map/reduce_scatter | solution.py:542
  1832.9 142.2 %reduce-scatter.25.cloned.1.call-done = f32[24,3072]{1,0:T(8,128)} async-done(((f32[768,3072]{1,0:T(8,128)}), f32[24,3072]{1,0:T(8,128)}) %reduce-scatter.25.cloned.1.call-update) | async-done | bytes 294928 | tf_op jit(solution)/shard_map/reduce_scatter | solution.py:536
  1975.1 141.2 %reduce-scatter.27.cloned.1.call-done = f32[96,768]{1,0:T(8,128)} async-done(((f32[3072,768]{1,0:T(8,128)}), f32[96,768]{1,0:T(8,128)}) %reduce-scatter.27.cloned.1.call-update) | async-done | bytes 294928 | tf_op jit(solution)/shard_map/reduce_scatter | solution.py:538
  2116.2 125.5 %reduce-scatter.21.cloned.1.call-done = f32[24,2304]{1,0:T(8,128)} async-done(((f32[768,2304]{1,0:T(8,128)}), f32[24,2304]{1,0:T(8,128)}) %reduce-scatter.21.cloned.1.call-update) | async-done | bytes 221200 | tf_op jit(solution)/shard_map/reduce_scatter | solution.py:529
  (600 shorter events, 388.9 us)
Async XLA Ops:
  7.2 66.2 %all-gather.13.cloned.1.call-start = ((), (), s32[]{:S(2)}) async-start(), calls=%async_computation.16 | async-start | bytes 3649536 | tf_op jit(solution)/shard_map/all_gather | solution.py:481
  8.9 87.8 %all-gather.17.cloned.1.call-start = ((), (), s32[]{:S(2)}) async-start(), calls=%async_computation.18 | async-start | bytes 1966080 | tf_op jit(solution)/shard_map/all_gather | solution.py:106
  77.6 41.0 %all-gather.15.cloned.1.call-start = ((), (), s32[]{:S(2)}) async-start(), calls=%async_computation.17 | async-start | bytes 1966080 | tf_op jit(solution)/shard_map/all_gather | solution.py:107
  78.5 96.5 %all-gather.19.cloned.1.call-start = ((), (), s32[]{:S(2)}) async-start(), calls=%async_computation.19 | async-start | bytes 1216512 | tf_op jit(solution)/shard_map/all_gather | solution.py:484
  79.2 163.1 %all-gather.21.cloned.1.call-start = ((), (), s32[]{:S(2)}) async-start(), calls=%async_computation.20 | async-start | bytes 4866048 | tf_op jit(solution)/shard_map/all_gather | solution.py:488
  80.0 228.1 %all-gather.23.cloned.1.call-start = ((), (), s32[]{:S(2)}) async-start(), calls=%async_computation.21 | async-start | bytes 4866048 | tf_op jit(solution)/shard_map/all_gather | solution.py:490
  80.8 288.8 %all-gather.25.cloned.1.call-start = ((), (), s32[]{:S(2)}) async-start(), calls=%async_computation.22 | async-start | bytes 3649536 | tf_op jit(solution)/shard_map/all_gather | solution.py:494
  82.4 310.5 %all-gather.27.cloned.1.call-start = ((), (), s32[]{:S(2)}) async-start(), calls=%async_computation.23 | async-start | bytes 1966080 | tf_op jit(solution)/shard_map/all_gather | solution.py:107
  85.9 283.6 %copy-start.68 = (f32[768]{0:T(1024)}, f32[768]{0:T(1024)S(1)}, u32[]{:S(2)}) copy-start(f32[768]{0:T(1024)S(1)} %convert_element_type.426) | copy-start | bytes 9220
  86.0 283.6 %copy-start.75 = (f32[768]{0:T(1024)}, f32[768]{0:T(1024)S(1)}, u32[]{:S(2)}) copy-start(f32[768]{0:T(1024)S(1)} %convert_element_type.428) | copy-start | bytes 9220
  86.3 335.6 %copy-start.30 = (pred[256,1024]{1,0:T(8,128)(4,1)}, pred[256,1024]{1,0:T(8,128)(4,1)S(1)}, u32[]{:S(2)}) copy-start(pred[256,1024]{1,0:T(8,128)(4,1)S(1)} %broadcast_compare_fusion) | copy-start | bytes 786436
  311.9 158.7 %copy-start.11 = (f32[256,768]{1,0:T(8,128)}, f32[256,768]{1,0:T(8,128)S(1)}, u32[]{:S(2)}) copy-start(f32[256,768]{1,0:T(8,128)S(1)} %get-tuple-element.109) | copy-start | bytes 2359300
  373.8 40.4 %all-gather.29.cloned.1.call-start = ((), (), s32[]{:S(2)}) async-start(), calls=%async_computation.24 | async-start | bytes 1966080 | tf_op jit(solution)/shard_map/all_gather | solution.py:106
  374.6 96.0 %all-gather.31.cloned.1.call-start = ((), (), s32[]{:S(2)}) async-start(), calls=%async_computation.25 | async-start | bytes 1216512 | tf_op jit(solution)/shard_map/all_gather | solution.py:497
  375.3 219.4 %all-gather.33.cloned.1.call-start = ((), (), s32[]{:S(2)}) async-start(), calls=%async_computation.26 | async-start | bytes 23592960 | tf_op jit(solution)/shard_map/all_gather | solution.py:505
  381.9 334.4 %all-gather.35.cloned.1.call-start = ((), (), s32[]{:S(2)}) async-start(), calls=%async_computation.27 | async-start | bytes 23592960 | tf_op jit(solution)/shard_map/all_gather | solution.py:507
  479.4 140.5 %all-to-all-start = ((bf16[4,8,17,768]{3,0,2,1:T(4,128)(2,1)}), bf16[4,8,17,768]{3,0,2,1:T(4,128)(2,1)}, u32[]{:S(2)}, u32[]{:S(2)}) async-start(bf16[4,8,17,768]{3,0,2,1:T(4,128)(2,1)} %copy.217), calls=%async_computation | async-start | bytes 1671168 | tf_op jit(solution)/shard_map/all_to_all | solution.py:263
  619.9 121.0 %all-to-all-start.2 = ((bf16[4,8,17,768]{3,0,2,1:T(4,128)(2,1)}), bf16[4,8,17,768]{3,0,2,1:T(4,128)(2,1)}, u32[]{:S(2)}, u32[]{:S(2)}) async-start(bf16[4,8,17,768]{3,0,2,1:T(4,128)(2,1)} %copy.228), calls=%async_computation.2 | async-start | bytes 1671168 | tf_op jit(solution)/shard_map/all_to_all | solution.py:263
  768.4 24.2 %all-to-all-start.3 = ((bf16[4,8,17,768]{3,0,2,1:T(4,128)(2,1)}), bf16[4,8,17,768]{3,0,2,1:T(4,128)(2,1)}, u32[]{:S(2)}, u32[]{:S(2)}) async-start(bf16[4,8,17,768]{3,0,2,1:T(4,128)(2,1)} %bitcast.150), calls=%async_computation.3 | async-start | bytes 1671168 | tf_op jit(solution)/shard_map/all_to_all | solution.py:267
  792.7 64.3 %all-to-all-start.1 = ((bf16[4,8,17,768]{3,0,2,1:T(4,128)(2,1)}), bf16[4,8,17,768]{3,0,2,1:T(4,128)(2,1)}, u32[]{:S(2)}, u32[]{:S(2)}) async-start(bf16[4,8,17,768]{3,0,2,1:T(4,128)(2,1)} %bitcast.18), calls=%async_computation.1 | async-start | bytes 1671168 | tf_op jit(solution)/shard_map/all_to_all | solution.py:267
  799.1 141.4 %reduce-scatter.17.cloned.1.call-start = ((), (), s32[]{:S(2)}) async-start(), calls=%async_computation.28 | async-start | bytes 3932160 | tf_op jit(solution)/shard_map/reduce_scatter | solution.py:174
  902.1 185.7 %reduce-scatter.19.cloned.1.call-start = ((), (), s32[]{:S(2)}) async-start(), calls=%async_computation.29 | async-start | bytes 3932160 | tf_op jit(solution)/shard_map/reduce_scatter | solution.py:174
  977.3 190.6 %reduce-scatter.35.cloned.1.call-start = ((), (), s32[]{:S(2)}) async-start(), calls=%async_computation.37 | async-start | bytes 23592960 | tf_op jit(solution)/shard_map/reduce_scatter | solution.py:522
  1014.5 286.8 %reduce-scatter.33.cloned.1.call-start = ((), (), s32[]{:S(2)}) async-start(), calls=%async_computation.36 | async-start | bytes 23592960 | tf_op jit(solution)/shard_map/reduce_scatter | solution.py:516
  1054.7 344.8 %reduce-scatter.39.cloned.1.call-start = ((), (), s32[]{:S(2)}) async-start(), calls=%async_computation.39 | async-start | bytes 405504
  1057.1 442.4 %reduce-scatter.37.cloned.1.call-start = ((), (), s32[]{:S(2)}) async-start(), calls=%async_computation.38 | async-start | bytes 405504
  1058.3 545.7 %reduce-scatter.31.cloned.1.call-start = ((), (), s32[]{:S(2)}) async-start(), calls=%async_computation.35 | async-start | bytes 2433024 | tf_op jit(solution)/shard_map/reduce_scatter | solution.py:545
  1060.3 648.3 %reduce-scatter.23.cloned.1.call-start = ((), (), s32[]{:S(2)}) async-start(), calls=%async_computation.31 | async-start | bytes 2433024 | tf_op jit(solution)/shard_map/reduce_scatter | solution.py:532
  1062.3 770.6 %reduce-scatter.29.cloned.1.call-start = ((), (), s32[]{:S(2)}) async-start(), calls=%async_computation.34 | async-start | bytes 7299072 | tf_op jit(solution)/shard_map/reduce_scatter | solution.py:542
  1066.6 908.4 %reduce-scatter.25.cloned.1.call-start = ((), (), s32[]{:S(2)}) async-start(), calls=%async_computation.32 | async-start | bytes 9732096 | tf_op jit(solution)/shard_map/reduce_scatter | solution.py:536
  1073.5 1042.7 %reduce-scatter.27.cloned.1.call-start = ((), (), s32[]{:S(2)}) async-start(), calls=%async_computation.33 | async-start | bytes 9732096 | tf_op jit(solution)/shard_map/reduce_scatter | solution.py:538
  1080.3 1161.4 %reduce-scatter.21.cloned.1.call-start = ((), (), s32[]{:S(2)}) async-start(), calls=%async_computation.30 | async-start | bytes 7299072 | tf_op jit(solution)/shard_map/reduce_scatter | solution.py:529
  (146 other events, 2519.5 us)
Sparse Core Ops, SparseCore 0:
  11.5 61.8 all-gather.12
  77.7 18.9 all-gather.16
  98.8 19.6 all-gather.14
  121.9 53.1 all-gather.18
  178.4 63.9 all-gather.20
  245.7 62.4 all-gather.22
  311.6 57.9 all-gather.24
  373.9 18.9 all-gather.26
  394.5 19.6 all-gather.28
  417.5 53.1 all-gather.30
  472.8 121.9 all-gather.32
  596.2 120.0 all-gather.34
  902.3 38.1 reduce-scatter.16
  977.4 37.9 reduce-scatter.18
  1017.8 141.3 reduce-scatter.34
  1161.8 139.4 reduce-scatter.32
  1306.7 92.7 reduce-scatter.38
  1405.6 93.9 reduce-scatter.36
  1505.4 98.5 reduce-scatter.30
  1610.6 97.9 reduce-scatter.22
  1714.8 118.0 reduce-scatter.28
  1840.4 134.6 reduce-scatter.24
  1981.5 134.6 reduce-scatter.26
  2123.3 118.3 reduce-scatter.20
where the time goes:
time: 2260 us; the launch traced here: 2250 us
  waiting for transfers between devices  1530 us (68%)
  matrix products  209 us (9%)
  blocking collectives  188 us (8%)
  local copies, waits for them, and re-layouts  175 us (8%)
  other arithmetic  109 us (5%)
  starting transfers between devices  24.3 us (1%)
    unnamed x26, waiting for transfers between devices  191 us
    reduce_scatter x1, waiting for transfers between devices, local(): lax.psum_scatter(gradients[9], ('dp', 'seq'), scatter_dimension=0, tiled=...  142 us
    reduce_scatter x1, waiting for transfers between devices, local(): lax.psum_scatter(gradients[11], ('dp', 'seq'), scatter_dimension=0, tiled...  141 us
    reduce_scatter x1, waiting for transfers between devices, local(): lax.psum_scatter(gradients[2], ('dp', 'seq'), scatter_dimension=0, tiled=...  125 us
    reduce_scatter x1, waiting for transfers between devices, local(): lax.psum_scatter(gradients[15], ('dp', 'seq'), scatter_dimension=0, tiled...  124 us
    reduce_scatter x1, waiting for transfers between devices, local(): lax.psum_scatter(gradients[23].astype(jnp.bfloat16), 'seq', scatter_dimen...  124 us
    reduce_scatter x1, waiting for transfers between devices, local(): lax.psum_scatter(gradients[5], ('dp', 'seq'), scatter_dimension=0, tiled=...  105 us
    reduce_scatter x1, waiting for transfers between devices, local(): lax.psum_scatter(gradients[18], ('dp', 'seq'), scatter_dimension=0, tiled...  104 us
  transfers between devices with their start and end apart: 28, of which 23 were waited for; matrix products, arithmetic and copies ran while one was open for 16% of the time, Pallas kernels for 0%

commit v1 on v0

v1 whole, which is shorter than its diff:
```python
import functools
import math

import jax
import jax.numpy as jnp
from jax import lax
from jax.experimental import pallas as pl
from jax.experimental.pallas import tpu as pltpu
from jax.sharding import Mesh
from jax.sharding import PartitionSpec as P

HEADS = 12
CAP = 17
LONG = 576
EDGE = 192
MASKED = -1000000000.0
EPSILON = 1e-06
LOWTYPE = jnp.bfloat16
WIDE = jnp.float32
ALL = ("z", "y", "x", "c")
CHIPS = ("z", "y", "x")
SWAP = [(0, 1), (1, 0)]


def dot(left, right, dims):
    return lax.dot_general(left, right, ((dims[0], dims[1]), ((), ())), preferred_element_type=WIDE)


def product(left, right):
    return dot(left, right, ((1,), (0,)))


def over_rows(left, right):
    return dot(left, right, ((0,), (0,)))


def over_features(left, right):
    return dot(left, right, ((1,), (1,)))


def low(values):
    return values.astype(LOWTYPE)


def widen(values):
    return values.astype(WIDE)


def swap_cores(values):
    return lax.ppermute(values, "c", SWAP)


def swap_chips(values):
    return lax.ppermute(values, "x", SWAP)


def in_order(mine, other, index, axis):
    first = jnp.where(index == 0, mine, other)
    second = jnp.where(index == 0, other, mine)
    return jnp.concatenate([first, second], axis=axis)


def norm_parts(values):
    center = values - jnp.mean(values, axis=-1, keepdims=True)
    spread = jnp.mean(center * center, axis=-1, keepdims=True)
    return center, lax.rsqrt(spread + EPSILON)


def layer_norm(values, gain, shift):
    center, scale = norm_parts(values)
    return low(center * scale * gain + shift)


def layer_norm_back(values, gain, grad):
    center, scale = norm_parts(values)
    hat = center * scale
    inner = grad * gain
    dvalues = scale * (
        inner
        - jnp.mean(inner, axis=-1, keepdims=True)
        - hat * jnp.mean(inner * hat, axis=-1, keepdims=True)
    )
    return dvalues, jnp.sum(grad * hat, axis=0), jnp.sum(grad, axis=0)


def gelu_parts(values):
    cdf = 0.5 + 0.5 * lax.erf(values * math.sqrt(0.5))
    pdf = jnp.exp(-0.5 * values * values) * (1.0 / math.sqrt(2.0 * math.pi))
    return values * cdf, cdf + values * pdf


def image_of(places, first_end, second_end):
    return (places >= first_end).astype(jnp.int32) + (places >= second_end).astype(jnp.int32)


def attention_places(scalars, rows, halo):
    x = scalars[0]
    edge_start = pl.multiple_of(x * (rows // 2), 64)
    mid_start = pl.multiple_of((1 - x) * (rows - halo), 64)
    mid_place = rows * x + mid_start
    halo_place = rows + x * ((rows - halo) - rows)
    return edge_start, mid_start, rows * x + edge_start, mid_place, halo_place


def edge_mask(place, count, first_end, second_end):
    row = image_of(place + lax.broadcasted_iota(jnp.int32, (count, 1), 0), first_end, second_end)
    column = image_of(place + lax.broadcasted_iota(jnp.int32, (1, count), 1), first_end, second_end)
    return (row == column) & (column != 1)


def mid_mask(mid_place, halo_place, count, first_end, second_end):
    row_places = mid_place + lax.broadcasted_iota(jnp.int32, (count, 1), 0)
    columns = lax.broadcasted_iota(jnp.int32, (1, 2 * count), 1)
    column_places = jnp.where(columns < count, mid_place + columns, halo_place + columns - count)
    row = image_of(row_places, first_end, second_end) == 1
    column = image_of(column_places, first_end, second_end) == 1
    return row & column, row


def lane_of_head(head, dim, lanes):
    lane = lax.broadcasted_iota(jnp.int32, (1, lanes), 1)
    return (lane >= head * dim) & (lane < (head + 1) * dim)


def only(values, lanes):
    return jnp.where(lanes, values, jnp.zeros_like(values))


def attend_kernel(scalars, packed, out, logs, *, rows, halo, dim):
    share = out.shape[1]
    first_end, second_end = scalars[1], scalars[2]
    edge_start, mid_start, edge_place, mid_place, halo_place = attention_places(scalars, rows, halo)
    half = rows // 2
    scale = 1.0 / math.sqrt(dim)
    mask_edge = edge_mask(edge_place, half, first_end, second_end)
    mask_mid, row_mid = mid_mask(mid_place, halo_place, halo, first_end, second_end)

    def one(queries, keys, values, mask):
        total, log_total = None, None
        for head in range(2):
            lanes = lane_of_head(head, dim, 128)
            scores = jnp.where(mask, over_features(only(queries, lanes), keys) * scale, MASKED)
            highest = jnp.max(scores, axis=-1, keepdims=True)
            raised = jnp.exp(scores - highest)
            sums = jnp.sum(raised, axis=-1, keepdims=True)
            weights = low(raised * (1.0 / sums))
            part = product(weights, only(values, lanes))
            total = part if total is None else total + part
            log_sum = highest + jnp.log(sums)
            log_total = log_sum if head == 0 else jnp.where(lanes, log_sum, log_total)
        return total, log_total

    def pair(index, carry):
        query_lanes = pl.ds(pl.multiple_of(index * 128, 128), 128)
        key_lanes = pl.ds(pl.multiple_of(share + index * 128, 128), 128)
        value_lanes = pl.ds(pl.multiple_of(2 * share + index * 128, 128), 128)
        edge = pl.ds(edge_start, half)
        mid = pl.ds(mid_start, halo)
        far = pl.ds(rows, halo)
        result, log_total = one(
            packed[edge, query_lanes], packed[edge, key_lanes], packed[edge, value_lanes], mask_edge
        )
        out[edge, query_lanes] = low(result)
        logs[edge, query_lanes] = log_total
        keys = jnp.concatenate([packed[mid, key_lanes], packed[far, key_lanes]], axis=0)
        values = jnp.concatenate([packed[mid, value_lanes], packed[far, value_lanes]], axis=0)
        result, log_total = one(packed[mid, query_lanes], keys, values, mask_mid)
        out[mid, query_lanes] = jnp.where(row_mid, low(result), out[mid, query_lanes])
        logs[mid, query_lanes] = jnp.where(row_mid, log_total, logs[mid, query_lanes])
        return carry

    lax.fori_loop(0, share // 128, pair, 0)


def attend_back_kernel(scalars, packed, grads, logs, out, *, rows, halo, dim):
    share = grads.shape[1]
    first_end, second_end = scalars[1], scalars[2]
    edge_start, mid_start, edge_place, mid_place, halo_place = attention_places(scalars, rows, halo)
    half = rows // 2
    scale = 1.0 / math.sqrt(dim)
    mask_edge = edge_mask(edge_place, half, first_end, second_end)
    mask_mid, _ = mid_mask(mid_place, halo_place, halo, first_end, second_end)

    def one(queries, keys, values, grad, log_total, mask):
        dquery, dkey, dvalue = None, None, None
        for head in range(2):
            lanes = lane_of_head(head, dim, 128)
            query, key, dout = only(queries, lanes), only(keys, lanes), only(grad, lanes)
            logs_here = log_total[:, head * dim : head * dim + 1]
            scores = jnp.where(mask, over_features(query, keys) * scale, MASKED)
            probs = jnp.exp(scores - logs_here)
            dprobs = over_features(dout, values)
            delta = jnp.sum(probs * dprobs, axis=-1, keepdims=True)
            dscores = low(probs * (dprobs - delta))
            parts = (
                product(dscores, key) * scale,
                over_rows(dscores, query) * scale,
                over_rows(low(probs), dout),
            )
            if head == 0:
                dquery, dkey, dvalue = parts
            else:
                dquery, dkey, dvalue = dquery + parts[0], dkey + parts[1], dvalue + parts[2]
        return low(dquery), low(dkey), low(dvalue)

    out[...] = jnp.zeros_like(out)

    def pair(index, carry):
        query_lanes = pl.ds(pl.multiple_of(index * 128, 128), 128)
        key_lanes = pl.ds(pl.multiple_of(share + index * 128, 128), 128)
        value_lanes = pl.ds(pl.multiple_of(2 * share + index * 128, 128), 128)
        edge = pl.ds(edge_start, half)
        mid = pl.ds(mid_start, halo)
        far = pl.ds(rows, halo)
        dquery, dkey, dvalue = one(
            packed[edge, query_lanes],
            packed[edge, key_lanes],
            packed[edge, value_lanes],
            grads[edge, query_lanes],
            logs[edge, query_lanes],
            mask_edge,
        )
        out[edge, query_lanes] = dquery
        out[edge, key_lanes] = dkey
        out[edge, value_lanes] = dvalue
        keys = jnp.concatenate([packed[mid, key_lanes], packed[far, key_lanes]], axis=0)
        values = jnp.concatenate([packed[mid, value_lanes], packed[far, value_lanes]], axis=0)
        dquery, dkey, dvalue = one(
            packed[mid, query_lanes],
            keys,
            values,
            grads[mid, query_lanes],
            logs[mid, query_lanes],
            mask_mid,
        )
        out[mid, query_lanes] = out[mid, query_lanes] + dquery
        out[mid, key_lanes] = out[mid, key_lanes] + dkey[:halo]
        out[mid, value_lanes] = out[mid, value_lanes] + dvalue[:halo]
        out[far, key_lanes] = dkey[halo:]
        out[far, value_lanes] = dvalue[halo:]
        return carry

    lax.fori_loop(0, share // 128, pair, 0)


def kernel_call(body, outs, operands, flops):
    return pl.pallas_call(
        body,
        out_shape=outs,
        in_specs=[pl.BlockSpec(memory_space=pltpu.SMEM)]
        + [pl.BlockSpec(memory_space=pltpu.VMEM)] * (len(operands) - 1),
        out_specs=[pl.BlockSpec(memory_space=pltpu.VMEM)] * len(outs),
        compiler_params=pltpu.CompilerParams(vmem_limit_bytes=48 * 1024 * 1024),
        cost_estimate=pl.CostEstimate(flops=flops, bytes_accessed=8_000_000, transcendentals=1_700_000),
    )(*operands)


def attend(scalars, packed, rows, halo, dim):
    share = packed.shape[1] // 3
    return kernel_call(
        functools.partial(attend_kernel, rows=rows, halo=halo, dim=dim),
        [jax.ShapeDtypeStruct((rows, share), LOWTYPE), jax.ShapeDtypeStruct((rows, share), WIDE)],
        [scalars, packed],
        1_700_000_000,
    )


def attend_back(scalars, packed, grads, logs, rows, halo, dim):
    [out] = kernel_call(
        functools.partial(attend_back_kernel, rows=rows, halo=halo, dim=dim),
        [jax.ShapeDtypeStruct(packed.shape, LOWTYPE)],
        [scalars, packed, grads, logs],
        4_000_000_000,
    )
    return out


def pick(block, index):
    return lax.dynamic_index_in_dim(block, index, 0, keepdims=False)


def gather_rows(block, core):
    pair = in_order(pick(block, core), swap_cores(pick(block, 1 - core)), core, 0)
    return lax.all_gather(pair, CHIPS, axis=0, tiled=True)


def scatter_rows(grads, core):
    summed = lax.psum_scatter(low(grads), CHIPS, scatter_dimension=0, tiled=True)
    parts = summed.reshape(2, summed.shape[0] // 2, summed.shape[1])
    mine, other = pick(parts, core), swap_cores(pick(parts, 1 - core))
    return mine, other


def thirds(weight, width):
    rows = weight.shape[0]
    return weight.reshape(rows, 3, 2, width // 2).transpose(2, 0, 1, 3).reshape(2, rows, -1)


def columns(weight):
    rows = weight.shape[0]
    return weight.reshape(rows, 2, -1).transpose(1, 0, 2)


def local(
    patches,
    image_lengths,
    expert_ids,
    lower_norm_gain,
    lower_norm_shift,
    lower_project,
    lower_query_bias,
    lower_value_bias,
    lower_merge,
    lower_merge_bias,
    lower_second_gain,
    lower_second_shift,
    lower_expand,
    lower_expand_bias,
    lower_shrink,
    lower_shrink_bias,
    upper_norm_gain,
    upper_norm_shift,
    upper_project,
    upper_query_bias,
    upper_value_bias,
    upper_merge,
    upper_merge_bias,
    upper_second_gain,
    upper_second_shift,
    router,
    expert_expand,
    expert_expand_bias,
    expert_shrink,
    expert_shrink_bias,
    output_grad,
):
    x, core = lax.axis_index("x"), lax.axis_index("c")
    devices = lax.axis_size(ALL)
    here = lax.axis_index(ALL)
    own, width = patches.shape
    rows = 2 * own
    dim = width // HEADS
    halo = rows - EDGE
    share = width // 2
    experts = router.shape[1]
    copies = devices // experts
    slots = experts * CAP
    part = lower_norm_gain.shape[0]
    hidden_part = lower_expand_bias.shape[0]
    lengths = image_lengths[0]
    scalars = jnp.stack([x, lengths[0], lengths[0] + lengths[1]]).astype(jnp.int32)
    mid_start = (1 - x) * (rows - halo)

    def halo_rows(full):
        count = halo // 2
        piece = lax.dynamic_slice_in_dim(full, mid_start + core * count, count, 0)
        got = swap_chips(piece)
        return in_order(got, swap_cores(got), core, 0)

    vectors = [
        lower_norm_gain,
        lower_norm_shift,
        lower_query_bias,
        lower_value_bias,
        lower_merge_bias,
        lower_second_gain,
        lower_second_shift,
        lower_shrink_bias,
        upper_norm_gain,
        upper_norm_shift,
        upper_query_bias,
        upper_value_bias,
        upper_merge_bias,
        upper_second_gain,
        upper_second_shift,
    ]
    count = len(vectors)
    small = jnp.concatenate(
        [
            jnp.stack(vectors, axis=1),
            lower_expand_bias.reshape(part, hidden_part // part),
            router,
            expert_shrink_bias.T,
        ],
        axis=1,
    )
    extra = hidden_part // part
    small = jnp.pad(small, ((0, 0), (0, 128 - small.shape[1])))
    small = jnp.broadcast_to(low(small)[None], (2, part, 128))
    first = gather_rows(
        jnp.concatenate(
            [thirds(low(lower_project), width), columns(low(lower_merge)), small], axis=2
        ),
        core,
    )
    lower_project_c = first[:, : 3 * share]
    lower_merge_c = first[:, 3 * share : 4 * share]
    lower_merge_full = in_order(lower_merge_c, swap_cores(lower_merge_c), core, 1)
    table = first[:, 4 * share :]
    table_t = widen(table.T)
    (
        ln1_gain,
        ln1_shift,
        lower_qb,
        lower_vb,
        lower_mb,
        ln2_gain,
        ln2_shift,
        shrink_b,
        ln3_gain,
        ln3_shift,
        upper_qb,
        upper_vb,
        upper_mb,
        ln4_gain,
        ln4_shift,
    ) = [table_t[i] for i in range(count)]
    expand_b = widen(table[:, count : count + extra]).reshape(devices, 2, hidden_part // 2)
    expand_b = lax.dynamic_index_in_dim(expand_b, core, 1, keepdims=False).reshape(-1)
    router_w = table[:, count + extra : count + extra + experts]
    router_t = table.T[count + extra : count + extra + experts]
    expert_bias = table.T[count + extra + experts : count + extra + 2 * experts]

    expand_c = gather_rows(
        low(lower_expand)
        .reshape(part, devices, 2, hidden_part // 2)
        .transpose(2, 0, 1, 3)
        .reshape(2, part, -1),
        core,
    )
    shrink_c = gather_rows(low(lower_shrink).reshape(2, hidden_part // 2, width), core)
    third = gather_rows(
        jnp.concatenate([thirds(low(upper_project), width), columns(low(upper_merge))], axis=2),
        core,
    )
    upper_project_c = third[:, : 3 * share]
    upper_merge_c = third[:, 3 * share :]
    upper_merge_full = in_order(upper_merge_c, swap_cores(upper_merge_c), core, 1)

    def whole_expert(weight):
        units = weight.shape[1] // 4
        pieces = low(weight).reshape(weight.shape[0], 4, units).transpose(1, 0, 2)
        return lax.all_to_all(pieces, ("x", "c"), 0, 0, tiled=True).reshape(-1, units)

    def expert_parts(grads):
        pieces = low(grads).reshape(4, grads.shape[0] // 4, grads.shape[1])
        pieces = lax.all_to_all(pieces, ("x", "c"), 0, 0, tiled=True)
        return widen(pieces.transpose(1, 0, 2).reshape(pieces.shape[1], -1))

    expand_e = whole_expert(expert_expand)
    shrink_e = whole_expert(expert_shrink.T)

    order = lax.broadcasted_iota(jnp.int32, (own, own), 0)
    before_it = low(order > lax.broadcasted_iota(jnp.int32, (own, own), 1))
    chosen = [
        low(expert_ids[:, k : k + 1] == jnp.arange(experts, dtype=jnp.int32)[None]) for k in range(2)
    ]
    earlier = product(before_it, chosen[0] + chosen[1])
    places = [
        expert_ids[:, k] * CAP
        + jnp.sum(widen(chosen[k]) * earlier, axis=1).astype(jnp.int32)
        for k in range(2)
    ]
    placed = [
        low(place[:, None] == jnp.arange(slots, dtype=jnp.int32)[None]) for place in places
    ]
    placed_any = placed[0] + placed[1]

    def to_experts(values):
        sent = low(over_rows(placed_any, values)).reshape(experts, CAP, width)
        if copies > 1:
            sent = jnp.repeat(sent, copies, axis=0)
        got = lax.all_to_all(sent, ALL, 0, 0, tiled=True)
        return got.reshape(devices * CAP, width)

    def to_patches(values):
        got = lax.all_to_all(low(values).reshape(devices, CAP, width), ALL, 0, 0, tiled=True)
        if copies > 1:
            got = low(jnp.sum(widen(got.reshape(experts, copies, CAP, width)), axis=1))
        return got.reshape(slots, width)

    grad_rows = to_experts(low(output_grad))

    full = in_order(patches, swap_cores(patches), core, 0)
    x0 = widen(full)

    def half(vector):
        return lax.dynamic_slice_in_dim(vector, core * share, share, 0)

    def attention_forward(residual, normed, project_c, query_bias, value_bias):
        bias = jnp.concatenate([half(query_bias), jnp.zeros((share,), WIDE), half(value_bias)])
        packed = low(product(normed, project_c) + bias)
        attended, logs = attend(scalars, packed, rows, halo, dim)
        attended_full = in_order(attended, swap_cores(attended), core, 1)
        return packed, logs, attended_full

    a1 = layer_norm(jnp.concatenate([x0, widen(halo_rows(full))], axis=0), ln1_gain, ln1_shift)
    packed1, logs1, attended1 = attention_forward(x0, a1, lower_project_c, lower_qb, lower_vb)
    x1 = x0 + product(attended1, lower_merge_full) + lower_mb

    b = layer_norm(x1, ln2_gain, ln2_shift)
    pre = product(b, expand_c) + expand_b
    hidden = low(gelu_parts(pre)[0])
    partial = low(product(hidden, shrink_c))
    x2 = x1 + (widen(partial) + widen(swap_cores(partial))) + shrink_b

    a2_own = layer_norm(x2, ln3_gain, ln3_shift)
    a2 = jnp.concatenate([a2_own, halo_rows(a2_own)], axis=0)
    packed2, logs2, attended2 = attention_forward(x2, a2, upper_project_c, upper_qb, upper_vb)

    def own_rows(values):
        return lax.dynamic_slice_in_dim(values, core * own, own, 0)

    x3 = own_rows(x2) + product(own_rows(attended2), upper_merge_full) + upper_mb
    normed = layer_norm(x3, ln4_gain, ln4_shift)
    rows_in = to_experts(normed)

    def gating(values):
        logits = product(values, router_w)
        raised = jnp.exp(logits - jnp.max(logits, axis=1, keepdims=True))
        return raised / jnp.sum(raised, axis=1, keepdims=True)

    mine = (jnp.arange(experts, dtype=jnp.int32) == here // copies).astype(WIDE)[None]
    probs_in = gating(rows_in)
    gate_in = jnp.sum(probs_in * mine, axis=1, keepdims=True)
    raw = product(grad_rows, shrink_e)
    before = product(rows_in, expand_e) + expert_expand_bias.astype(LOWTYPE).astype(WIDE)
    expert_hidden, slope = gelu_parts(before)
    expert_hidden = low(expert_hidden)
    once = (here % copies == 0).astype(WIDE)
    bias_here = product(low(mine), expert_bias) * once
    delta_gate = jnp.sum(widen(expert_hidden) * raw, axis=1, keepdims=True)
    delta_gate = delta_gate + jnp.sum(widen(grad_rows) * bias_here, axis=1, keepdims=True)
    dbefore = low(gate_in * raw * slope)
    dlogits = low(probs_in * delta_gate * (mine - gate_in))
    drows = over_features(dbefore, expand_e) + product(dlogits, router_t)
    returned_grad = to_patches(drows)
    returned = to_patches(over_features(expert_hidden, shrink_e))
    g_out = low(gate_in * widen(grad_rows))
    delta_expand_e = over_rows(rows_in, dbefore)
    delta_shrink_e = over_rows(g_out, expert_hidden)
    delta_expert_bias = jnp.sum(widen(dbefore), axis=0)
    delta_router = over_rows(rows_in, dlogits)
    delta_shrink_bias = (jnp.sum(widen(g_out), axis=0) * once)[:, None] * mine
    delta_expert_expand = expert_parts(delta_expand_e)
    delta_expert_shrink = expert_parts(delta_shrink_e).T

    probs = gating(normed)
    result = x3
    for k in range(2):
        gate = jnp.sum(widen(chosen[k]) * probs, axis=1, keepdims=True)
        picked = product(placed[k], returned) + product(chosen[k], expert_bias)
        result = result + gate * picked

    delta_normed = product(placed_any, returned_grad)
    dx3, dgain4, dshift4 = layer_norm_back(x3, ln4_gain, delta_normed)
    dx3 = output_grad + dx3
    dx3 = in_order(dx3, swap_cores(dx3), core, 0)
    half_lanes = (jnp.arange(width, dtype=jnp.int32) // share == core).astype(WIDE)

    def columns_of_half(values):
        return lax.dynamic_slice_in_dim(values, core * share, share, 1)

    def spread(vector):
        return lax.dynamic_update_slice_in_dim(jnp.zeros((width,), WIDE), vector, core * share, 0)

    def attention_backward(dresidual, residual, normed, packed, logs, attended, gain, project_c, merge):
        dmerged = low(dresidual)
        delta_merge_bias = jnp.sum(widen(dmerged), axis=0) * half_lanes
        delta_merge = over_rows(attended, columns_of_half(dmerged))
        merge_rows = lax.dynamic_slice_in_dim(merge, core * share, share, 0)
        dattended = low(over_features(dmerged, merge_rows))
        dpacked = attend_back(scalars, packed, dattended, logs, rows, halo, dim)
        dnormed = over_features(dpacked, project_c)
        far = swap_chips(low(dnormed[rows:]))
        delta_project = over_rows(normed, dpacked)
        bias_sums = jnp.sum(widen(dpacked), axis=0)
        mine_part = low(
            dnormed[:rows]
            + lax.dynamic_update_slice_in_dim(jnp.zeros((rows, width), WIDE), widen(far), mid_start, 0)
        )
        dnormed = widen(mine_part) + widen(swap_cores(mine_part))
        dinput, dgain, dshift = layer_norm_back(residual, gain, dnormed)
        sums = (
            dgain * half_lanes,
            dshift * half_lanes,
            spread(bias_sums[:share]),
            spread(bias_sums[2 * share :]),
            delta_merge_bias,
        )
        return dresidual + dinput, jnp.concatenate([delta_project, delta_merge], axis=1), sums

    dx2, upper_grads, upper_sums = attention_backward(
        dx3, x2, a2, packed2, logs2, attended2, ln3_gain, upper_project_c, upper_merge_full
    )
    third_mine, third_other = scatter_rows(upper_grads, core)

    dmlp = low(dx2)
    delta_shrink_b = jnp.sum(widen(dmlp), axis=0) * half_lanes
    delta_shrink = over_rows(hidden, dmlp)
    dpre = low(over_features(dmlp, shrink_c) * gelu_parts(pre)[1])
    shrink_mine, shrink_other = scatter_rows(delta_shrink, core)
    dnormed = low(over_features(dpre, expand_c))
    delta_expand = over_rows(b, dpre)
    delta_expand_b = jnp.sum(widen(dpre), axis=0)
    expand_mine, expand_other = scatter_rows(delta_expand, core)
    dinput, dgain2, dshift2 = layer_norm_back(x1, ln2_gain, widen(dnormed) + widen(swap_cores(dnormed)))
    dx1 = dx2 + dinput

    dx0, lower_grads, lower_sums = attention_backward(
        dx1, x0, a1, packed1, logs1, attended1, ln1_gain, lower_project_c, lower_merge_full
    )
    delta_patches = own_rows(dx0)

    sums = jnp.stack(
        list(lower_sums)
        + [dgain2 * half_lanes, dshift2 * half_lanes, delta_shrink_b]
        + list(upper_sums)
        + [dgain4, dshift4],
        axis=1,
    )
    expand_sums = delta_expand_b.reshape(devices, 1, hidden_part // 2) * (
        jnp.arange(2, dtype=jnp.int32)[None, :, None] == core
    ).astype(WIDE)
    small_grads = jnp.concatenate(
        [sums, expand_sums.reshape(width, extra), delta_router, delta_shrink_bias], axis=1
    )
    small_grads = jnp.pad(small_grads, ((0, 0), (0, 128 - small_grads.shape[1])))
    first_mine, first_other = scatter_rows(jnp.concatenate([lower_grads, small_grads], axis=1), core)

    def halves(mine_part, other_part):
        return jnp.stack(
            [
                jnp.where(core == 0, mine_part, other_part),
                jnp.where(core == 0, other_part, mine_part),
            ]
        )

    def attention_outputs(mine_part, other_part):
        both = widen(halves(mine_part, other_part))
        project = both[:, :, : 3 * share].reshape(2, part, 3, share).transpose(1, 2, 0, 3)
        merge = both[:, :, 3 * share : 4 * share].transpose(1, 0, 2)
        return project.reshape(part, 3 * width), merge.reshape(part, width)

    delta_lower_project, delta_lower_merge = attention_outputs(first_mine, first_other)
    delta_upper_project, delta_upper_merge = attention_outputs(third_mine, third_other)
    delta_lower_expand = (
        widen(halves(expand_mine, expand_other))
        .reshape(2, part, devices, hidden_part // 2)
        .transpose(1, 2, 0, 3)
        .reshape(part, -1)
    )
    delta_lower_shrink = widen(halves(shrink_mine, shrink_other)).reshape(hidden_part, width)
    vector_grads = widen(first_mine[:, 4 * share :]) + widen(first_other[:, 4 * share :])
    vector_t = vector_grads.T
    v = [vector_t[i] for i in range(count)]
    delta_lower_expand_bias = vector_grads[:, count : count + extra].reshape(hidden_part)
    delta_router_out = vector_grads[:, count + extra : count + extra + experts]
    delta_expert_shrink_bias = vector_t[count + extra + experts : count + extra + 2 * experts]
    return (
        result,
        delta_patches,
        v[0],
        v[1],
        delta_lower_project,
        v[2],
        v[3],
        delta_lower_merge,
        v[4],
        v[5],
        v[6],
        delta_lower_expand,
        delta_lower_expand_bias,
        delta_lower_shrink,
        v[7],
        v[8],
        v[9],
        delta_upper_project,
        v[10],
        v[11],
        delta_upper_merge,
        v[12],
        v[13],
        v[14],
        delta_router_out,
        delta_expert_expand,
        delta_expert_bias,
        delta_expert_shrink,
        delta_expert_shrink_bias,
    )


def solution(mesh):
    groups, parts = mesh.devices.shape
    inner = Mesh(mesh.devices.reshape(groups // 2, 2, parts // 2, 2), ALL)
    dp, seq = ("z", "y"), ("x", "c")
    rows, flat = P(ALL, None), P(ALL)
    in_specs = (
        (rows, P(dp, None), rows)
        + (flat, flat, rows, flat, flat, rows, flat)
        + (flat, flat, rows, flat, rows, flat)
        + (flat, flat, rows, flat, flat, rows, flat)
        + (flat, flat, rows, P(seq, dp), flat, P(dp, seq), P(None, ALL), rows)
    )
    out_specs = (
        (rows, rows)
        + (flat, flat, rows, flat, flat, rows, flat)
        + (flat, flat, rows, flat, rows, flat)
        + (flat, flat, rows, flat, flat, rows, flat)
        + (flat, flat, rows, P(seq, dp), flat, P(dp, seq), P(None, ALL))
    )
    return jax.shard_map(local, mesh=inner, in_specs=in_specs, out_specs=out_specs, check_vma=False)
```

time: 2260 us -> 1080 us (0.48)
  waiting for transfers between devices: 1530 us -> 646 us
  blocking collectives: 188 us -> 33.5 us
  matrix products: 209 us -> 110 us
  local copies, waits for them, and re-layouts: 175 us -> 98.7 us
  starting transfers between devices: 24.3 us -> 59.5 us
  other arithmetic: 109 us -> 78.1 us
  Pallas kernels: 0 us -> 29.5 us
    reduce_scatter x10 -> x4, waiting for transfers between devices: 898 us -> 295 us  [scatter_rows(): lax.psum_scatter(low(grads), CHIPS, scatter_dimension=0, tiled=True)]
    all_gather x12 -> x4, waiting for transfers between devices: 427 us -> 180 us  [gather_rows(): return lax.all_gather(pair, CHIPS, axis=0, tiled=True)]
    unnamed x26 -> x8, waiting for transfers between devices: 191 us -> 0.13 us
    all_to_all x4 -> x7, waiting for transfers between devices: 8.23 us -> 134 us  [the longest x2 50.9 us: expert_parts(): pieces = lax.all_to_all(pieces, ('x', 'c'), 0, 0, tiled=True)]
    dot_general x41 -> x37, matrix products: 209 us -> 110 us  [dot(): lax.dot_general(left, right, ((dims[0], dims[1]), ((), ())), preferred_el...]
    unnamed x3 -> x0, blocking collectives: 96.5 us -> none
    all_gather x3 -> x0, blocking collectives: 91.4 us -> none  [the longest x1 48 us: gather_weights(): lax.all_gather(expert_shrink_bias.astype(LOWTYPE), ('dp', 'seq'), axis=1,...]
    all_gather x6 -> x0, local copies, waits for them, and re-layouts: 57.5 us -> none  [the longest x1 25.2 us: gather_weights(): lax.all_gather(expert_expand.astype(LOWTYPE), 'seq', axis=0, tiled=True)]
  transfers between devices with their start and end apart: 28 -> 39, of which waited for: 23 -> 23; matrix products, arithmetic and copies ran while one was open for 16% -> 20% of each run, Pallas kernels for 0% -> 2%
where the time goes in v1:
time: 1080 us; the launch traced here: 1070 us
  waiting for transfers between devices  646 us (60%)
  matrix products  110 us (10%)
  local copies, waits for them, and re-layouts  98.7 us (9%)
  other arithmetic  78.1 us (7%)
  starting transfers between devices  59.5 us (6%)
  blocking collectives  33.5 us (3%)
  Pallas kernels  29.5 us (3%)
  between operations  18.1 us (2%)
    reduce_scatter x4, waiting for transfers between devices, scatter_rows(): lax.psum_scatter(low(grads), CHIPS, scatter_dimension=0, tiled=True)  295 us
    all_gather x4, waiting for transfers between devices, gather_rows(): return lax.all_gather(pair, CHIPS, axis=0, tiled=True)  180 us
    dot_general x37, matrix products, dot(): lax.dot_general(left, right, ((dims[0], dims[1]), ((), ())), preferred_el...  110 us
    all_to_all x2, waiting for transfers between devices, expert_parts(): pieces = lax.all_to_all(pieces, ('x', 'c'), 0, 0, tiled=True)  50.9 us
    all_to_all x2, waiting for transfers between devices, whole_expert(): lax.all_to_all(pieces, ('x', 'c'), 0, 0, tiled=True).reshape(-1, units)  40.7 us
    all_to_all x1, blocking collectives, to_patches(): lax.all_to_all(low(values).reshape(devices, CAP, width), ALL, 0, 0, tiled...  33.5 us
    ppermute x4, waiting for transfers between devices, swap_chips(): return lax.ppermute(values, 'x', SWAP)  30.9 us
    all_to_all x2, waiting for transfers between devices, to_experts(): got = lax.all_to_all(sent, ALL, 0, 0, tiled=True)  30.4 us
  transfers between devices with their start and end apart: 39, of which 23 were waited for; matrix products, arithmetic and copies ran while one was open for 20% of the time, Pallas kernels for 2%

profile of v1, /device:TPU:9, one launch (start us, length us, event | category | flops | bytes accessed | tf_op | source)
XLA Modules:
  0.0 1074.2 jit_solution(7260755169335415884)
XLA Ops:
  33.6 6.3 collective-permute-done.1
  43.5 46.4 %all-gather.5.cloned.1.call-done = bf16[768,1664]{1,0:T(8,128)(2,1)} async-done(((bf16[48,1664]{1,0:T(8,128)(2,1)}), bf16[768,1664]{1,0:T(8,128)(2,1)}) %all-gather.5.cloned.1.call-update) | async-done | bytes 2555920 | tf_op jit(solution)/shard_map/all_gather | solution.py:284
  111.0 43.4 %all-gather.7.cloned.1.call-done = bf16[768,1536]{1,0:T(8,128)(2,1)} async-done(((bf16[48,1536]{1,0:T(8,128)(2,1)}), bf16[768,1536]{1,0:T(8,128)(2,1)}) %all-gather.7.cloned.1.call-update) | async-done | bytes 2359312 | tf_op jit(solution)/shard_map/all_gather | solution.py:284
  159.5 59.5 %all-gather.9.cloned.1.call-done = bf16[1536,768]{1,0:T(8,128)(2,1)} async-done(((bf16[96,768]{1,0:T(8,128)(2,1)}), bf16[1536,768]{1,0:T(8,128)(2,1)}) %all-gather.9.cloned.1.call-update) | async-done | bytes 2359312 | tf_op jit(solution)/shard_map/all_gather | solution.py:284
  230.7 6.4 collective-permute-done.9
  238.9 6.5 convert_bitcast_fusion.2
  245.4 8.2 reshape.501
  253.6 5.9 copy.244
  264.7 31.1 %all-gather.11.cloned.1.call-done = bf16[768,1536]{1,0:T(8,128)(2,1)} async-done(((bf16[48,1536]{1,0:T(8,128)(2,1)}), bf16[768,1536]{1,0:T(8,128)(2,1)}) %all-gather.11.cloned.1.call-update) | async-done | bytes 2359312 | tf_op jit(solution)/shard_map/all_gather | solution.py:284
  316.4 9.7 all-to-all-done.2
  334.6 23.1 %all-to-all-done = bf16[32,17,768]{2,1,0:T(8,128)(2,1)S(1)} async-done(((bf16[32,17,768]{2,1,0:T(8,128)(2,1)}), bf16[32,17,768]{2,1,0:T(8,128)(2,1)S(1)}, u32[]{:S(2)}, u32[]{:S(2)}) %all-to-all-start) | async-done | bytes 835616 | tf_op jit(solution)/shard_map/all_to_all | solution.py:473
  363.4 6.5 convert_element_type.350
  369.9 8.2 reshape.499
  378.1 6.0 copy.243
  384.1 7.4 all-to-all-done.4
  410.3 8.3 fusion.142
  418.5 31.0 %all-to-all-done.1 = bf16[4,192,3072]{2,1,0:T(8,128)(2,1)} async-done(((bf16[4,192,3072]{2,1,0:T(8,128)(2,1)}), bf16[4,192,3072]{2,1,0:T(8,128)(2,1)}, u32[]{:S(2)}, u32[]{:S(2)}) %all-to-all-start.1) | async-done | bytes 4718624 | tf_op jit(solution)/shard_map/all_to_all | solution.py:443
  449.5 10.6 convert_reduce_fusion
  460.1 6.4 fusion.143
  470.0 33.5 %all_to_all.40 = bf16[32,17,768]{2,1,0:T(8,128)(2,1)} all-to-all(bf16[32,17,768]{2,1,0:T(8,128)(2,1)S(1)} %reshape.507), channel_id=1, replica_groups=mesh['z'=4,'y'=2,'x'=2,'c'=2] {'z','y','x','c'}, dimensions={0} | all-to-all | bytes 1671168 | tf_op jit(solution)/shard_map/all_to_all | solution.py:477
  514.1 9.2 shard_map.520
  533.9 13.2 %collective-permute-done.15 = bf16[320,768]{1,0:T(8,128)(2,1)} collective-permute-done((bf16[320,768]{1,0:T(8,128)(2,1)}, bf16[320,768]{1,0:T(8,128)(2,1)}, u32[]{:S(2)}, u32[]{:S(2)}) %collective-permute-start.15) | collective-permute-done | bytes 491552 | tf_op jit(solution)/shard_map/ppermute | solution.py:54
  566.1 7.1 convolution_convert_fusion.8
  581.6 8.4 convolution_convert_fusion.1
  595.9 11.6 %all-to-all-done.3 = bf16[32,17,768]{2,1,0:T(8,128)(2,1)} async-done(((bf16[32,17,768]{2,1,0:T(8,128)(2,1)}), bf16[32,17,768]{2,1,0:T(8,128)(2,1)}, u32[]{:S(2)}, u32[]{:S(2)}) %all-to-all-start.3) | async-done | bytes 835616 | tf_op jit(solution)/shard_map/all_to_all | solution.py:477
  635.5 9.2 shard_map.521
  650.3 18.5 %all-to-all-done.6 = bf16[4,192,3072]{2,1,0:T(8,128)(2,1)} async-done(((bf16[4,192,3072]{2,1,0:T(8,128)(2,1)}), bf16[4,192,3072]{2,1,0:T(8,128)(2,1)}, u32[]{:S(2)}, u32[]{:S(2)}) %all-to-all-start.6) | async-done | bytes 4718624 | tf_op jit(solution)/shard_map/all_to_all | solution.py:447
  668.8 6.3 all-to-all-start.7
  704.7 32.4 %all-to-all-done.7 = bf16[4,192,3072]{2,1,0:T(8,128)(2,1)} async-done(((bf16[4,192,3072]{2,1,0:T(8,128)(2,1)}), bf16[4,192,3072]{2,1,0:T(8,128)(2,1)}, u32[]{:S(2)}, u32[]{:S(2)}) %all-to-all-start.7) | async-done | bytes 4718624 | tf_op jit(solution)/shard_map/all_to_all | solution.py:447
  751.4 38.0 %reduce-scatter.7.cloned.1.call-done = bf16[48,1536]{1,0:T(8,128)(2,1)} async-done(((bf16[768,1536]{1,0:T(8,128)(2,1)}), bf16[48,1536]{1,0:T(8,128)(2,1)}) %reduce-scatter.7.cloned.1.call-update) | async-done | bytes 147472 | tf_op jit(solution)/shard_map/reduce_scatter | solution.py:288
  792.6 129.3 %reduce-scatter.9.cloned.1.call-done = bf16[96,768]{1,0:T(8,128)(2,1)} async-done(((bf16[1536,768]{1,0:T(8,128)(2,1)}), bf16[96,768]{1,0:T(8,128)(2,1)}) %reduce-scatter.9.cloned.1.call-update) | async-done | bytes 147472 | tf_op jit(solution)/shard_map/reduce_scatter | solution.py:288
  928.1 128.0 %reduce-scatter.5.cloned.1.call-done = bf16[48,1664]{1,0:T(8,128)(2,1)} async-done(((bf16[768,1664]{1,0:T(8,128)(2,1)}), bf16[48,1664]{1,0:T(8,128)(2,1)}) %reduce-scatter.5.cloned.1.call-update) | async-done | bytes 159760 | tf_op jit(solution)/shard_map/reduce_scatter | solution.py:288
  (636 shorter events, 280.6 us)
Async XLA Ops:
  7.2 82.7 %all-gather.5.cloned.1.call-start = ((), (), s32[]{:S(2)}) async-start(), calls=%async_computation.12 | async-start | bytes 2715648 | tf_op jit(solution)/shard_map/all_gather | solution.py:284
  25.5 128.9 %all-gather.7.cloned.1.call-start = ((), (), s32[]{:S(2)}) async-start(), calls=%async_computation.13 | async-start | bytes 2506752 | tf_op jit(solution)/shard_map/all_gather | solution.py:284
  28.7 190.3 %all-gather.9.cloned.1.call-start = ((), (), s32[]{:S(2)}) async-start(), calls=%async_computation.14 | async-start | bytes 2506752 | tf_op jit(solution)/shard_map/all_gather | solution.py:284
  29.2 4.4 collective-permute-start.7
  31.6 8.3 collective-permute-start.1
  41.9 253.9 %all-gather.11.cloned.1.call-start = ((), (), s32[]{:S(2)}) async-start(), calls=%async_computation.15 | async-start | bytes 2506752 | tf_op jit(solution)/shard_map/all_gather | solution.py:284
  103.1 3.9 collective-permute-start.4
  222.5 4.2 collective-permute-start.8
  229.4 7.6 collective-permute-start.9
  237.0 61.3 %collective-permute-start.10 = (bf16[160,768]{1,0:T(8,128)(2,1)S(1)}, bf16[160,768]{1,0:T(8,128)(2,1)}, u32[]{:S(2)}, u32[]{:S(2)}) collective-permute-start(bf16[160,768]{1,0:T(8,128)(2,1)S(1)} %collective-permute-done.9), channel_id=1, source_target_pairs={{0,1},{1,0},{2,3},{3,2},{4,5},{5,4},{6,7},{7,6},{8,9},{9,8},{10,11... | collective-permute-start | bytes 737288 | tf_op jit(solution)/shard_map/ppermute | solution.py:50
  259.6 66.5 %all-to-all-start.2 = ((bf16[4,192,3072]{2,1,0:T(8,128)(2,1)}), bf16[4,192,3072]{2,1,0:T(8,128)(2,1)}, u32[]{:S(2)}, u32[]{:S(2)}) async-start(bf16[4,192,3072]{2,1,0:T(8,128)(2,1)} %copy.244), calls=%async_computation.2 | async-start | bytes 9437184 | tf_op jit(solution)/shard_map/all_to_all | solution.py:443
  296.9 12.4 %collective-permute-start.13 = (bf16[768,384]{1,0:T(8,128)(2,1)S(1)}, bf16[768,384]{1,0:T(8,128)(2,1)S(1)}, u32[]{:S(2)}, u32[]{:S(2)}) collective-permute-start(bf16[768,384]{1,0:T(8,128)(2,1)S(1)} %slice.275), channel_id=1, source_target_pairs={{0,1},{1,0},{2,3},{3,2},{4,5},{5,4},{6,7},{7,6},{8,9},{9,8},{10,11... | collective-permute-start | bytes 1769480 | tf_op jit(solution)/shard_map/ppermute | solution.py:50
  326.1 31.6 %all-to-all-start = ((bf16[32,17,768]{2,1,0:T(8,128)(2,1)}), bf16[32,17,768]{2,1,0:T(8,128)(2,1)S(1)}, u32[]{:S(2)}, u32[]{:S(2)}) async-start(bf16[32,17,768]{2,1,0:T(8,128)(2,1)} %reshape.497), calls=%async_computation | async-start | bytes 2359296 | tf_op jit(solution)/shard_map/all_to_all | solution.py:473
  358.7 32.7 %all-to-all-start.4 = ((bf16[32,17,768]{2,1,0:T(8,128)(2,1)}), bf16[32,17,768]{2,1,0:T(8,128)(2,1)S(1)}, u32[]{:S(2)}, u32[]{:S(2)}) async-start(bf16[32,17,768]{2,1,0:T(8,128)(2,1)} %reshape.505), calls=%async_computation.4 | async-start | bytes 2359296 | tf_op jit(solution)/shard_map/all_to_all | solution.py:473
  391.5 58.1 %all-to-all-start.1 = ((bf16[4,192,3072]{2,1,0:T(8,128)(2,1)}), bf16[4,192,3072]{2,1,0:T(8,128)(2,1)}, u32[]{:S(2)}, u32[]{:S(2)}) async-start(bf16[4,192,3072]{2,1,0:T(8,128)(2,1)} %copy.243), calls=%async_computation.1 | async-start | bytes 9437184 | tf_op jit(solution)/shard_map/all_to_all | solution.py:443
  396.5 348.8 %reduce-scatter.11.cloned.1.call-start = ((), (), s32[]{:S(2)}) async-start(), calls=%async_computation.19 | async-start | bytes 2506752 | tf_op jit(solution)/shard_map/reduce_scatter | solution.py:288
  506.8 3.2 collective-permute-start.14
  527.3 262.1 %reduce-scatter.7.cloned.1.call-start = ((), (), s32[]{:S(2)}) async-start(), calls=%async_computation.17 | async-start | bytes 2506752 | tf_op jit(solution)/shard_map/reduce_scatter | solution.py:288
  533.0 14.0 %collective-permute-start.15 = (bf16[320,768]{1,0:T(8,128)(2,1)}, bf16[320,768]{1,0:T(8,128)(2,1)}, u32[]{:S(2)}, u32[]{:S(2)}) collective-permute-start(bf16[320,768]{1,0:T(8,128)(2,1)} %slice.379), channel_id=1, source_target_pairs={{0,2},{2,0},{1,3},{3,1},{4,6},{6,4},{5,7},{7,5},{8,10},{10,8},{9,1... | collective-permute-start | bytes 1474568 | tf_op jit(solution)/shard_map/ppermute | solution.py:54
  548.4 3.2 collective-permute-start.16
  575.5 32.0 %all-to-all-start.3 = ((bf16[32,17,768]{2,1,0:T(8,128)(2,1)}), bf16[32,17,768]{2,1,0:T(8,128)(2,1)}, u32[]{:S(2)}, u32[]{:S(2)}) async-start(bf16[32,17,768]{2,1,0:T(8,128)(2,1)} %reshape.503), calls=%async_computation.3 | async-start | bytes 2359296 | tf_op jit(solution)/shard_map/all_to_all | solution.py:477
  607.6 61.2 %all-to-all-start.6 = ((bf16[4,192,3072]{2,1,0:T(8,128)(2,1)}), bf16[4,192,3072]{2,1,0:T(8,128)(2,1)}, u32[]{:S(2)}, u32[]{:S(2)}) async-start(bf16[4,192,3072]{2,1,0:T(8,128)(2,1)} %bitcast.211), calls=%async_computation.10 | async-start | bytes 9437184 | tf_op jit(solution)/shard_map/all_to_all | solution.py:447
  612.6 309.3 %reduce-scatter.9.cloned.1.call-start = ((), (), s32[]{:S(2)}) async-start(), calls=%async_computation.18 | async-start | bytes 2506752 | tf_op jit(solution)/shard_map/reduce_scatter | solution.py:288
  622.2 5.6 collective-permute-start.17
  648.2 32.2 %collective-permute-start.18 = (bf16[320,768]{1,0:T(8,128)(2,1)S(1)}, bf16[320,768]{1,0:T(8,128)(2,1)S(1)}, u32[]{:S(2)}, u32[]{:S(2)}) collective-permute-start(bf16[320,768]{1,0:T(8,128)(2,1)S(1)} %slice.378), channel_id=1, source_target_pairs={{0,2},{2,0},{1,3},{3,1},{4,6},{6,4},{5,7},{7,5},{8,10},{10,8},{9,1... | collective-permute-start | bytes 1474568 | tf_op jit(solution)/shard_map/ppermute | solution.py:54
  668.8 68.3 %all-to-all-start.7 = ((bf16[4,192,3072]{2,1,0:T(8,128)(2,1)}), bf16[4,192,3072]{2,1,0:T(8,128)(2,1)}, u32[]{:S(2)}, u32[]{:S(2)}) async-start(bf16[4,192,3072]{2,1,0:T(8,128)(2,1)} %bitcast.210), calls=%async_computation.11 | async-start | bytes 9437184 | tf_op jit(solution)/shard_map/all_to_all | solution.py:447
  675.0 381.2 %reduce-scatter.5.cloned.1.call-start = ((), (), s32[]{:S(2)}) async-start(), calls=%async_computation.16 | async-start | bytes 2715648 | tf_op jit(solution)/shard_map/reduce_scatter | solution.py:288
  680.7 5.8 collective-permute-start.19
  746.3 3.2 collective-permute-start.23
  790.2 134.9 %collective-permute-start.21 = (bf16[24,1536]{1,0:T(8,128)(2,1)S(1)}, bf16[24,1536]{1,0:T(8,128)(2,1)S(1)}, u32[]{:S(2)}, u32[]{:S(2)}) collective-permute-start(bf16[24,1536]{1,0:T(8,128)(2,1)S(1)} %dynamic-slice_bitcast_fusion.5), channel_id=1, source_target_pairs={{0,1},{1,0},{2,3},{3,2},{4,5},{5,4},{6,7},{7,6},{8,9},{9,8},{10,11... | collective-permute-start | bytes 221192 | tf_op jit(solution)/shard_map/ppermute | solution.py:50
  922.8 3.7 collective-permute-start.22
  1057.1 5.0 collective-permute-start.20
  (159 other events, 1854.1 us)
Sparse Core Ops, SparseCore 0:
  25.6 64.2 all-gather.4
  93.3 61.1 all-gather.6
  157.8 61.0 all-gather.8
  226.8 68.9 all-gather.10
  527.4 128.4 reduce-scatter.10
  661.4 127.8 reduce-scatter.6
  794.3 127.5 reduce-scatter.8
  927.6 128.5 reduce-scatter.4

commit v2 on v1

--- a/solution.py
+++ b/solution.py
@@ -11,6 +11,7 @@
 
 HEADS = 12
 CAP = 17
+SLOTS = 24
 LONG = 576
 EDGE = 192
 MASKED = -1000000000.0
@@ -275,30 +276,352 @@
     return out
 
 
+def attention_grads_kernel(normed, dpacked, attended, dmerged, *refs):
+    out, width = refs[-1], dmerged.shape[1]
+    for i in range(3):
+        part = over_rows(normed[...], dpacked[:, i * width : (i + 1) * width])
+        out[:, i * width : (i + 1) * width] = low(part)
+    out[:, 3 * width : 4 * width] = low(over_rows(attended[...], dmerged[...]))
+    if len(refs) == 2:
+        out[:, 4 * width :] = low(refs[0][...])
+
+
+def attention_grads(*operands):
+    normed, dpacked, _, dmerged = operands[:4]
+    lanes = dpacked.shape[1] + dmerged.shape[1] + sum(o.shape[1] for o in operands[4:])
+    inside = pl.BlockSpec(memory_space=pltpu.VMEM)
+    return pl.pallas_call(
+        attention_grads_kernel,
+        out_shape=jax.ShapeDtypeStruct((normed.shape[1], lanes), LOWTYPE),
+        in_specs=[inside] * len(operands),
+        out_specs=inside,
+        compiler_params=pltpu.CompilerParams(vmem_limit_bytes=40 * 1024 * 1024),
+        cost_estimate=pl.CostEstimate(
+            flops=2 * normed.shape[0] * normed.shape[1] * lanes,
+            bytes_accessed=8_000_000,
+            transcendentals=0,
+        ),
+    )(*operands)
+
+
 def pick(block, index):
     return lax.dynamic_index_in_dim(block, index, 0, keepdims=False)
 
 
-def gather_rows(block, core):
-    pair = in_order(pick(block, core), swap_cores(pick(block, 1 - core)), core, 0)
-    return lax.all_gather(pair, CHIPS, axis=0, tiled=True)
-
-
-def scatter_rows(grads, core):
-    summed = lax.psum_scatter(low(grads), CHIPS, scatter_dimension=0, tiled=True)
-    parts = summed.reshape(2, summed.shape[0] // 2, summed.shape[1])
-    mine, other = pick(parts, core), swap_cores(pick(parts, 1 - core))
+def xor_pairs(size, flip):
+    return [(i, i ^ flip) for i in range(size)]
+
+
+def assemble_kernel(coords, *refs, parts):
+    blocks, outs = refs[: len(refs) - len(parts)], refs[len(refs) - len(parts) :]
+    count = blocks[0].shape[0]
+    for k, block in enumerate(blocks):
+        chip = (coords[0] ^ (k >> 2)) * 4 + (coords[1] ^ ((k >> 1) & 1)) * 2 + (coords[2] ^ (k & 1))
+        start = 0
+        for out, (width, groups) in zip(outs, parts):
+            for group in range(groups):
+                place = pl.multiple_of((chip * groups + group) * count, 16)
+                out[pl.ds(place, count), :] = block[:, start : start + width]
+                start += width
+
+
+def assemble(coords, blocks, parts):
+    count, width = blocks[0].shape
+    inside = pl.BlockSpec(memory_space=pltpu.VMEM)
+    return pl.pallas_call(
+        functools.partial(assemble_kernel, parts=parts),
+        out_shape=[
+            jax.ShapeDtypeStruct((len(blocks) * count * groups, lanes), LOWTYPE)
+            for lanes, groups in parts
+        ],
+        in_specs=[pl.BlockSpec(memory_space=pltpu.SMEM)] + [inside] * len(blocks),
+        out_specs=[inside] * len(parts),
+        compiler_params=pltpu.CompilerParams(vmem_limit_bytes=40 * 1024 * 1024),
+        cost_estimate=pl.CostEstimate(
+            flops=0, bytes_accessed=4 * len(blocks) * count * width, transcendentals=0
+        ),
+    )(coords, *blocks)
+
+
+def tie(*values):
+    return lax.optimization_barrier(values)
+
+
+def gather_z(pair, after=()):
+    if lax.axis_size("z") != 4:
+        return [lax.all_gather(pair, CHIPS, axis=0, tiled=True), pair]
+    if after:
+        pair, after = tie(pair, after)
+    return [pair] + [lax.ppermute(pair, "z", xor_pairs(4, k)) for k in (1, 2, 3)]
+
+
+def gather_plane(along):
+    if lax.axis_size("z") != 4:
+        return []
+    return [(swap_chips(here), lax.ppermute(here, "y", SWAP)) for here in along]
+
+
+def gather_end(along, plane, parts, x_first):
+    if lax.axis_size("z") != 4:
+        whole, count = along[0], along[1].shape[0]
+        outs, start = [], 0
+        for lanes, groups in parts:
+            piece = whole[:, start : start + lanes * groups]
+            piece = piece.reshape(-1, count, groups, lanes).transpose(0, 2, 1, 3)
+            outs.append(piece.reshape(-1, lanes))
+            start += lanes * groups
+        return outs, ()
+    blocks, across = [], []
+    for k, (here, (by_x, by_y)) in enumerate(zip(along, plane)):
+        if k in x_first:
+            blocks += [here, by_x, by_y, lax.ppermute(by_x, "y", SWAP)]
+            across += [by_x]
+        else:
+            blocks += [here, by_x, by_y, swap_chips(by_y)]
+            across += [by_x, blocks[-1]]
+    coords = jnp.stack([lax.axis_index(name) for name in CHIPS]).astype(jnp.int32)
+    return assemble(coords, blocks, parts), tuple(across)
+
+
+def added(left, right):
+    return low(widen(left) + widen(right))
+
+
+def at(values, index, axis):
+    return lax.dynamic_index_in_dim(values, index, axis, keepdims=False)
+
+
+def pairs_first(grads):
+    if lax.axis_size("z") != 4:
+        return lax.psum_scatter(low(grads), CHIPS, scatter_dimension=0, tiled=True)
+    z, y, x = [lax.axis_index(name) for name in CHIPS]
+    view = low(grads).reshape(2, 2, 2, 2, grads.shape[0] // 16, grads.shape[1])
+    near, far = at(view, z // 2, 0), at(view, 1 - z // 2, 0)
+    from_y, from_x = lax.ppermute(at(near, 1 - y, 1), "y", SWAP), swap_chips(at(far, 1 - x, 2))
+    return at(near, y, 1), from_y, at(far, x, 2), from_x
+
+
+def pairs_second(state):
+    if lax.axis_size("z") != 4:
+        return state
+    y, x = lax.axis_index("y"), lax.axis_index("x")
+    near, far = added(*state[:2]), added(*state[2:])
+    from_x, from_y = swap_chips(at(near, 1 - x, 1)), lax.ppermute(at(far, 1 - y, 1), "y", SWAP)
+    return at(near, x, 1), from_x, at(far, y, 1), from_y
+
+
+def pairs_z(state):
+    if lax.axis_size("z") != 4:
+        return state
+    low_bit = lax.axis_index("z") % 2
+    near, far = added(*state[:2]), added(*state[2:])
+    sent = (at(near, 1 - low_bit, 0), at(far, low_bit, 0), at(far, 1 - low_bit, 0))
+    got = [lax.ppermute(piece, "z", xor_pairs(4, k + 1)) for k, piece in enumerate(sent)]
+    return [at(near, low_bit, 0)] + got
+
+
+def summed_everywhere(values):
+    if lax.axis_size("z") != 4:
+        return lax.psum(values, ALL)
+    for name, pairs in (("c", SWAP), ("x", SWAP), ("y", SWAP), ("z", xor_pairs(4, 1)), ("z", xor_pairs(4, 2))):
+        values = values + lax.ppermute(values, name, pairs)
+    return values
+
+
+def scatter_y(grads):
+    if lax.axis_size("z") != 4:
+        return lax.psum_scatter(low(grads), CHIPS, scatter_dimension=0, tiled=True)
+    y = lax.axis_index("y")
+    view = low(grads).reshape(4, 2, 2, grads.shape[0] // 16, grads.shape[1])
+    return at(view, y, 1), lax.ppermute(at(view, 1 - y, 1), "y", SWAP)
+
+
+def scatter_x(state):
+    if lax.axis_size("z") != 4:
+        return state
+    x, values = lax.axis_index("x"), added(*state)
+    return at(values, x, 1), swap_chips(at(values, 1 - x, 1))
+
+
+def scatter_z(state):
+    if lax.axis_size("z") != 4:
+        return state
+    z, values = lax.axis_index("z"), added(*state)
+    sent = [lax.ppermute(at(values, z ^ k, 0), "z", xor_pairs(4, k)) for k in (1, 2, 3)]
+    return [at(values, z, 0)] + sent
+
+
+def scatter_end(state):
+    if lax.axis_size("z") != 4:
+        return widen(state)
+    return widen(state[0]) + widen(state[1]) + widen(state[2]) + widen(state[3])
+
+
+def exchange_halves(first, second, core):
+    mine = jnp.where(core == 0, first, second)
+    other = widen(swap_cores(low(jnp.where(core == 0, second, first))))
     return mine, other
 
 
-def thirds(weight, width):
-    rows = weight.shape[0]
-    return weight.reshape(rows, 3, 2, width // 2).transpose(2, 0, 1, 3).reshape(2, rows, -1)
-
-
-def columns(weight):
-    rows = weight.shape[0]
-    return weight.reshape(rows, 2, -1).transpose(1, 0, 2)
+def cut_kernel(place, weight, *outs):
+    for k, out in enumerate(outs):
+
+        @pl.when(pl.program_id(0) == k)
+        def _(out=out):
+            out[...] = low(weight[...])
+
+
+def cut_columns(weight, place):
+    rows, units = weight.shape[0], weight.shape[1] // 4
+    return pl.pallas_call(
+        cut_kernel,
+        grid_spec=pltpu.PrefetchScalarGridSpec(
+            num_scalar_prefetch=1,
+            grid=(4,),
+            in_specs=[pl.BlockSpec((rows, units), lambda i, p: (0, p[0] ^ i))],
+            out_specs=[pl.BlockSpec((rows, units), lambda i, p: (0, 0))] * 4,
+        ),
+        out_shape=[jax.ShapeDtypeStruct((rows, units), LOWTYPE)] * 4,
+        compiler_params=pltpu.CompilerParams(vmem_limit_bytes=32 * 1024 * 1024),
+        cost_estimate=pl.CostEstimate(flops=0, bytes_accessed=6 * weight.size, transcendentals=0),
+    )(place, weight)
+
+
+def stack_kernel(place, *refs):
+    blocks, out = refs[:4], refs[4]
+    count = blocks[0].shape[0]
+    for k, block in enumerate(blocks):
+        out[pl.ds(pl.multiple_of((place[0] ^ k) * count, 16), count), :] = block[...]
+
+
+def stack_rows(place, blocks):
+    count, width = blocks[0].shape
+    inside = pl.BlockSpec(memory_space=pltpu.VMEM)
+    return pl.pallas_call(
+        stack_kernel,
+        out_shape=jax.ShapeDtypeStruct((4 * count, width), LOWTYPE),
+        in_specs=[pl.BlockSpec(memory_space=pltpu.SMEM)] + [inside] * 4,
+        out_specs=inside,
+        compiler_params=pltpu.CompilerParams(vmem_limit_bytes=32 * 1024 * 1024),
+        cost_estimate=pl.CostEstimate(flops=0, bytes_accessed=16 * count * width, transcendentals=0),
+    )(place, *blocks)
+
+
+def join_kernel(place, *refs):
+    for k in range(4):
+
+        @pl.when(pl.program_id(0) == k)
+        def _(k=k):
+            refs[4][...] = widen(refs[k][...])
+
+
+def join_columns(place, pieces):
+    rows, units = pieces[0].shape
+    return pl.pallas_call(
+        join_kernel,
+        grid_spec=pltpu.PrefetchScalarGridSpec(
+            num_scalar_prefetch=1,
+            grid=(4,),
+            in_specs=[pl.BlockSpec((rows, units), lambda i, p: (0, 0))] * 4,
+            out_specs=pl.BlockSpec((rows, units), lambda i, p: (0, p[0] ^ i)),
+        ),
+        out_shape=jax.ShapeDtypeStruct((rows, 4 * units), WIDE),
+        compiler_params=pltpu.CompilerParams(vmem_limit_bytes=40 * 1024 * 1024),
+        cost_estimate=pl.CostEstimate(flops=0, bytes_accessed=24 * rows * units, transcendentals=0),
+    )(place, *pieces)
+
+
+def column_sums(values):
+    return product(jnp.ones((8, values.shape[0]), LOWTYPE), values)[0]
+
+
+def halves_of(weight, width):
+    parts = [weight[:, i : i + width] for i in range(0, weight.shape[1], width)]
+    return tuple(
+        jnp.concatenate([p[:, h * width // 2 : (h + 1) * width // 2] for p in parts], axis=1)
+        for h in range(2)
+    )
+
+
+def cut_dense(project, merge, small, expand, shrink, upper_project, upper_merge):
+    width = merge.shape[1]
+    half_rows = shrink.shape[0] // 2
+    project, merge = halves_of(project, width), halves_of(merge, width)
+    upper_project, upper_merge = halves_of(upper_project, width), halves_of(upper_merge, width)
+    expand, shrink = halves_of(expand, expand.shape[1]), halves_of(shrink, width)
+    return [
+        (
+            jnp.concatenate([project[h], merge[h], small], axis=1),
+            jnp.concatenate([expand[h], upper_project[h], upper_merge[h]], axis=1),
+            jnp.concatenate([shrink[h][:half_rows], shrink[h][half_rows:]], axis=1),
+        )
+        for h in range(2)
+    ]
+
+
+def prologue_kernel(core, *refs, count):
+    operands = count + 9
+    sources, outs = refs[:operands], refs[operands : operands + 6]
+    table, small, sems = refs[operands + 6 : operands + 9]
+    inside = refs[operands + 9 :]
+    copies = [
+        pltpu.make_async_copy(source, target, sems.at[i])
+        for i, (source, target) in enumerate(zip(sources, inside))
+    ]
+    for copy in copies:
+        copy.start()
+    for copy in copies:
+        copy.wait()
+    vectors, (expand_bias, router, bias), weights = inside[:count], inside[count : count + 3], inside[count + 3 :]
+    part = router.shape[0]
+    table[...] = jnp.zeros_like(table)
+    for i, vector in enumerate(vectors):
+        table[i : i + 1, 0:part] = vector[...].reshape(1, part)
+    biases = expand_bias[...].reshape(1, 4 * part)
+    for q in range(4):
+        table[16 + q : 17 + q, 0:part] = biases[:, q * part : (q + 1) * part]
+    small[...] = table[...].T
+    small[0:part, 32 : 32 + router.shape[1]] = router[...]
+    small[0:part, 64 : 64 + bias.shape[1]] = bias[...]
+    values = [ref[...] for ref in weights]
+    cut = cut_dense(values[0], values[1], small[0:part, :], *values[2:])
+    first = core[0] == 0
+    for i in range(3):
+        outs[i][...] = low(jnp.where(first, cut[0][i], cut[1][i]))
+        outs[3 + i][...] = low(jnp.where(first, cut[1][i], cut[0][i]))
+
+
+def prologue(core, vectors, expand_bias, router, bias, weights):
+    part = router.shape[0]
+    if lax.axis_size("z") != 4:
+        rows = [jnp.stack(vectors), jnp.zeros((16 - len(vectors), part), WIDE)]
+        rows += [expand_bias.reshape(4, part), jnp.zeros((12, part), WIDE)]
+        small = jnp.concatenate([jnp.concatenate(rows).T, router, bias], axis=1)
+        small = jnp.pad(small, ((0, 0), (0, 128 - small.shape[1])))
+        cut = cut_dense(weights[0], weights[1], small, *weights[2:])
+        picked = [[jnp.where(core == h, a, b) for a, b in zip(*cut)] for h in range(2)]
+        return [low(v) for v in picked[0]], [low(v) for v in picked[1]]
+    lanes = [weights[0].shape[1] // 2 + weights[1].shape[1] // 2 + 128]
+    lanes += [sum(w.shape[1] // 2 for w in (weights[2], weights[4], weights[5]))]
+    shapes = [(part, lanes[0]), (part, lanes[1]), (weights[3].shape[0] // 2, weights[3].shape[1])]
+    inside = pl.BlockSpec(memory_space=pltpu.VMEM)
+    operands = [*vectors, expand_bias, router, bias, *weights]
+    outs = pl.pallas_call(
+        functools.partial(prologue_kernel, count=len(vectors)),
+        out_shape=[jax.ShapeDtypeStruct(shape, LOWTYPE) for shape in shapes * 2],
+        in_specs=[pl.BlockSpec(memory_space=pltpu.SMEM)]
+        + [pl.BlockSpec(memory_space=pl.ANY)] * len(operands),
+        out_specs=[inside] * 6,
+        scratch_shapes=[
+            pltpu.VMEM((128, 128), WIDE),
+            pltpu.VMEM((128, 128), WIDE),
+            pltpu.SemaphoreType.DMA((len(operands),)),
+        ]
+        + [pltpu.VMEM(operand.shape, WIDE) for operand in operands],
+        compiler_params=pltpu.CompilerParams(vmem_limit_bytes=60 * 1024 * 1024),
+        cost_estimate=pl.CostEstimate(flops=0, bytes_accessed=2_500_000, transcendentals=0),
+    )(core.reshape(1).astype(jnp.int32), *operands)
+    return outs[:3], outs[3:]
 
 
 def local(
@@ -344,9 +667,8 @@
     share = width // 2
     experts = router.shape[1]
     copies = devices // experts
-    slots = experts * CAP
+    slots = experts * SLOTS
     part = lower_norm_gain.shape[0]
-    hidden_part = lower_expand_bias.shape[0]
     lengths = image_lengths[0]
     scalars = jnp.stack([x, lengths[0], lengths[0] + lengths[1]]).astype(jnp.int32)
     mid_start = (1 - x) * (rows - halo)
@@ -375,29 +697,40 @@
         upper_second_shift,
     ]
     count = len(vectors)
-    small = jnp.concatenate(
-        [
-            jnp.stack(vectors, axis=1),
-            lower_expand_bias.reshape(part, hidden_part // part),
-            router,
-            expert_shrink_bias.T,
-        ],
-        axis=1,
-    )
-    extra = hidden_part // part
-    small = jnp.pad(small, ((0, 0), (0, 128 - small.shape[1])))
-    small = jnp.broadcast_to(low(small)[None], (2, part, 128))
-    first = gather_rows(
-        jnp.concatenate(
-            [thirds(low(lower_project), width), columns(low(lower_merge)), small], axis=2
-        ),
+    shares, others = prologue(
         core,
-    )
-    lower_project_c = first[:, : 3 * share]
-    lower_merge_c = first[:, 3 * share : 4 * share]
+        vectors,
+        lower_expand_bias,
+        router,
+        expert_shrink_bias.T,
+        [lower_project, lower_merge, lower_expand, lower_shrink, upper_project, upper_merge],
+    )
+    got = [swap_cores(other) for other in others]
+    pair_1 = in_order(shares[0], got[0], core, 0)
+    hidden_half = lower_expand.shape[1] // 2
+    pair_2 = in_order(shares[1], got[1], core, 0)
+    pair_3 = pair_2[:, hidden_half:]
+    pair_2 = jnp.concatenate(
+        [pair_2[:, :hidden_half], in_order(shares[2], got[2], core, 1)], axis=1
+    )
+    along_1 = gather_z(pair_1)
+    (lower_project_c, lower_merge_c, table), _ = gather_end(
+        along_1, gather_plane(along_1), ((3 * share, 1), (share, 1), (128, 1)), (0, 2)
+    )
+    seat = (2 * x + core).reshape(1).astype(jnp.int32)
+    expand_cut, shrink_cut = cut_columns(expert_expand, seat), cut_columns(expert_shrink.T, seat)
+    table, expand_cut, shrink_cut = lax.optimization_barrier((table, expand_cut, shrink_cut))
+    along_2 = gather_z(pair_2, tuple(along_1[1:2]))
+    (expand_c, shrink_half), crossed = gather_end(
+        along_2, gather_plane(along_2), ((hidden_half, 1), (share, 4)), (0, 2)
+    )
+    upper_c = lax.all_gather(pair_3, CHIPS, axis=0, tiled=True)
+    upper_project_c, upper_merge_c = upper_c[:, : 3 * share], upper_c[:, 3 * share :]
     lower_merge_full = in_order(lower_merge_c, swap_cores(lower_merge_c), core, 1)
-    table = first[:, 4 * share :]
-    table_t = widen(table.T)
+    shrink_parts = shrink_half.reshape(2, hidden_half, share)
+    shrink_c = in_order(pick(shrink_parts, core), swap_cores(pick(shrink_parts, 1 - core)), core, 1)
+    table_t = table.T
+    wide_t = widen(table_t[:32])
     (
         ln1_gain,
         ln1_shift,
@@ -414,41 +747,34 @@
         upper_mb,
         ln4_gain,
         ln4_shift,
-    ) = [table_t[i] for i in range(count)]
-    expand_b = widen(table[:, count : count + extra]).reshape(devices, 2, hidden_part // 2)
-    expand_b = lax.dynamic_index_in_dim(expand_b, core, 1, keepdims=False).reshape(-1)
-    router_w = table[:, count + extra : count + extra + experts]
-    router_t = table.T[count + extra : count + extra + experts]
-    expert_bias = table.T[count + extra + experts : count + extra + 2 * experts]
-
-    expand_c = gather_rows(
-        low(lower_expand)
-        .reshape(part, devices, 2, hidden_part // 2)
-        .transpose(2, 0, 1, 3)
-        .reshape(2, part, -1),
-        core,
-    )
-    shrink_c = gather_rows(low(lower_shrink).reshape(2, hidden_part // 2, width), core)
-    third = gather_rows(
-        jnp.concatenate([thirds(low(upper_project), width), columns(low(upper_merge))], axis=2),
-        core,
-    )
-    upper_project_c = third[:, : 3 * share]
-    upper_merge_c = third[:, 3 * share :]
-    upper_merge_full = in_order(upper_merge_c, swap_cores(upper_merge_c), core, 1)
-
-    def whole_expert(weight):
-        units = weight.shape[1] // 4
-        pieces = low(weight).reshape(weight.shape[0], 4, units).transpose(1, 0, 2)
-        return lax.all_to_all(pieces, ("x", "c"), 0, 0, tiled=True).reshape(-1, units)
+    ) = [wide_t[i] for i in range(count)]
+    expand_b = wide_t[16:20].reshape(4, devices, part).transpose(1, 0, 2).reshape(2, hidden_half)
+    expand_b = pick(expand_b, core)
+    router_w = table[:, 32 : 32 + experts]
+    router_t = table_t[32 : 32 + experts]
+    expert_bias = table_t[64 : 64 + experts]
+
+    def between(values, k):
+        return lax.ppermute(values, ("x", "c"), xor_pairs(4, k))
+
+    def whole_expert(pieces):
+        if crossed:
+            pieces, _ = lax.optimization_barrier((pieces, crossed))
+        across = between(pieces[2], 2)
+        last, _ = tie(pieces[3], across)
+        return [pieces[0], between(pieces[1], 1), across, between(last, 3)]
 
     def expert_parts(grads):
-        pieces = low(grads).reshape(4, grads.shape[0] // 4, grads.shape[1])
-        pieces = lax.all_to_all(pieces, ("x", "c"), 0, 0, tiled=True)
-        return widen(pieces.transpose(1, 0, 2).reshape(pieces.shape[1], -1))
-
-    expand_e = whole_expert(expert_expand)
-    shrink_e = whole_expert(expert_shrink.T)
+        count = grads.shape[0] // 4
+        pieces = [
+            lax.dynamic_slice_in_dim(grads, (seat[0] ^ k) * count, count, 0) for k in range(4)
+        ]
+        far_piece = between(pieces[2], 2)
+        last, _ = tie(pieces[3], far_piece)
+        return [pieces[0], between(pieces[1], 1), far_piece, between(last, 3)]
+
+    expand_e = whole_expert(expand_cut)
+    shrink_e = whole_expert(shrink_cut)
 
     order = lax.broadcasted_iota(jnp.int32, (own, own), 0)
     before_it = low(order > lax.broadcasted_iota(jnp.int32, (own, own), 1))
@@ -457,7 +783,7 @@
     ]
     earlier = product(before_it, chosen[0] + chosen[1])
     places = [
-        expert_ids[:, k] * CAP
+        expert_ids[:, k] * SLOTS
         + jnp.sum(widen(chosen[k]) * earlier, axis=1).astype(jnp.int32)
         for k in range(2)
     ]
@@ -467,19 +793,19 @@
     placed_any = placed[0] + placed[1]
 
     def to_experts(values):
-        sent = low(over_rows(placed_any, values)).reshape(experts, CAP, width)
+        sent = low(over_rows(placed_any, values)).reshape(experts, SLOTS, width)
         if copies > 1:
             sent = jnp.repeat(sent, copies, axis=0)
         got = lax.all_to_all(sent, ALL, 0, 0, tiled=True)
-        return got.reshape(devices * CAP, width)
+        return got.reshape(devices * SLOTS, width)
 
     def to_patches(values):
-        got = lax.all_to_all(low(values).reshape(devices, CAP, width), ALL, 0, 0, tiled=True)
+        got = lax.all_to_all(low(values).reshape(devices, SLOTS, width), ALL, 0, 0, tiled=True)
         if copies > 1:
-            got = low(jnp.sum(widen(got.reshape(experts, copies, CAP, width)), axis=1))
+            got = low(jnp.sum(widen(got.reshape(experts, copies, SLOTS, width)), axis=1))
         return got.reshape(slots, width)
 
-    grad_rows = to_experts(low(output_grad))
+    grads_sent = low(output_grad)
 
     full = in_order(patches, swap_cores(patches), core, 0)
     x0 = widen(full)
@@ -501,12 +827,17 @@
     b = layer_norm(x1, ln2_gain, ln2_shift)
     pre = product(b, expand_c) + expand_b
     hidden = low(gelu_parts(pre)[0])
+    upper_merge_full = in_order(upper_merge_c, swap_cores(upper_merge_c), core, 1)
+    hidden_full = in_order(hidden, swap_cores(hidden), core, 1)
     partial = low(product(hidden, shrink_c))
     x2 = x1 + (widen(partial) + widen(swap_cores(partial))) + shrink_b
 
     a2_own = layer_norm(x2, ln3_gain, ln3_shift)
     a2 = jnp.concatenate([a2_own, halo_rows(a2_own)], axis=0)
+    a2, expand_e[2] = tie(a2, expand_e[2])
     packed2, logs2, attended2 = attention_forward(x2, a2, upper_project_c, upper_qb, upper_vb)
+
+    attended2, expand_e[3], grad_rows = tie(attended2, expand_e[3], to_experts(grads_sent))
 
     def own_rows(values):
         return lax.dynamic_slice_in_dim(values, core * own, own, 0)
@@ -514,6 +845,8 @@
     x3 = own_rows(x2) + product(own_rows(attended2), upper_merge_full) + upper_mb
     normed = layer_norm(x3, ln4_gain, ln4_shift)
     rows_in = to_experts(normed)
+    rows_in, expand_e, shrink_e[2] = tie(rows_in, expand_e, shrink_e[2])
+    expand_e, shrink_e = stack_rows(seat, expand_e), stack_rows(seat, shrink_e)
 
     def gating(values):
         logits = product(values, router_w)
@@ -539,18 +872,14 @@
     g_out = low(gate_in * widen(grad_rows))
     delta_expand_e = over_rows(rows_in, dbefore)
     delta_shrink_e = over_rows(g_out, expert_hidden)
-    delta_expert_bias = jnp.sum(widen(dbefore), axis=0)
+    delta_expert_bias = column_sums(dbefore)
     delta_router = over_rows(rows_in, dlogits)
-    delta_shrink_bias = (jnp.sum(widen(g_out), axis=0) * once)[:, None] * mine
-    delta_expert_expand = expert_parts(delta_expand_e)
-    delta_expert_shrink = expert_parts(delta_shrink_e).T
-
-    probs = gating(normed)
-    result = x3
-    for k in range(2):
-        gate = jnp.sum(widen(chosen[k]) * probs, axis=1, keepdims=True)
-        picked = product(placed[k], returned) + product(chosen[k], expert_bias)
-        result = result + gate * picked
+    delta_shrink_e = low(delta_shrink_e)
+    expand_pieces = expert_parts(low(delta_expand_e))
+    returned_grad, expand_pieces[1], expand_pieces[2], delta_shrink_e = tie(
+        returned_grad, expand_pieces[1], expand_pieces[2], delta_shrink_e
+    )
+    delta_shrink_bias = (column_sums(g_out) * once)[:, None] * mine
 
     delta_normed = product(placed_any, returned_grad)
     dx3, dgain4, dshift4 = layer_norm_back(x3, ln4_gain, delta_normed)
@@ -564,17 +893,18 @@
     def spread(vector):
         return lax.dynamic_update_slice_in_dim(jnp.zeros((width,), WIDE), vector, core * share, 0)
 
-    def attention_backward(dresidual, residual, normed, packed, logs, attended, gain, project_c, merge):
+    def attention_backward(
+        dresidual, residual, normed, packed, logs, attended, gain, project_c, merge, waiting
+    ):
         dmerged = low(dresidual)
-        delta_merge_bias = jnp.sum(widen(dmerged), axis=0) * half_lanes
-        delta_merge = over_rows(attended, columns_of_half(dmerged))
+        delta_merge_bias = column_sums(dmerged) * half_lanes
         merge_rows = lax.dynamic_slice_in_dim(merge, core * share, share, 0)
         dattended = low(over_features(dmerged, merge_rows))
         dpacked = attend_back(scalars, packed, dattended, logs, rows, halo, dim)
         dnormed = over_features(dpacked, project_c)
+        dnormed, waiting = tie(dnormed, waiting)
         far = swap_chips(low(dnormed[rows:]))
-        delta_project = over_rows(normed, dpacked)
-        bias_sums = jnp.sum(widen(dpacked), axis=0)
+        bias_sums = column_sums(dpacked)
         mine_part = low(
             dnormed[:rows]
             + lax.dynamic_update_slice_in_dim(jnp.zeros((rows, width), WIDE), widen(far), mid_start, 0)
@@ -588,75 +918,129 @@
             spread(bias_sums[2 * share :]),
             delta_merge_bias,
         )
-        return dresidual + dinput, jnp.concatenate([delta_project, delta_merge], axis=1), sums
-
-    dx2, upper_grads, upper_sums = attention_backward(
-        dx3, x2, a2, packed2, logs2, attended2, ln3_gain, upper_project_c, upper_merge_full
-    )
-    third_mine, third_other = scatter_rows(upper_grads, core)
+        outs = dresidual + dinput, (normed, dpacked, attended, columns_of_half(dmerged)), sums, far
+        return *outs, waiting
+
+    dx2, upper_grads, upper_sums, far, expand_pieces[3] = attention_backward(
+        dx3,
+        x2,
+        a2,
+        packed2,
+        logs2,
+        attended2,
+        ln3_gain,
+        upper_project_c,
+        upper_merge_full,
+        expand_pieces[3],
+    )
+    delta_shrink_e, _ = tie(delta_shrink_e, far)
+    shrink_pieces = expert_parts(delta_shrink_e)
+    third = scatter_y(attention_grads(*upper_grads))
 
     dmlp = low(dx2)
-    delta_shrink_b = jnp.sum(widen(dmlp), axis=0) * half_lanes
-    delta_shrink = over_rows(hidden, dmlp)
+    delta_shrink_b = column_sums(dmlp) * half_lanes
+    delta_shrink = low(over_rows(hidden_full, columns_of_half(dmlp)))
+    delta_shrink = delta_shrink.reshape(-1, 4, 2 * part, share).transpose(0, 2, 1, 3)
     dpre = low(over_features(dmlp, shrink_c) * gelu_parts(pre)[1])
-    shrink_mine, shrink_other = scatter_rows(delta_shrink, core)
+    dpre, shrink_pieces[2] = tie(dpre, shrink_pieces[2])
     dnormed = low(over_features(dpre, expand_c))
-    delta_expand = over_rows(b, dpre)
-    delta_expand_b = jnp.sum(widen(dpre), axis=0)
-    expand_mine, expand_other = scatter_rows(delta_expand, core)
+    delta_expand = low(over_rows(b, dpre))
+    delta_expand_b = column_sums(dpre)
+    second = pairs_first(
+        jnp.concatenate([delta_expand, delta_shrink.reshape(width, 4 * share)], axis=1)
+    )
     dinput, dgain2, dshift2 = layer_norm_back(x1, ln2_gain, widen(dnormed) + widen(swap_cores(dnormed)))
     dx1 = dx2 + dinput
-
-    dx0, lower_grads, lower_sums = attention_backward(
-        dx1, x0, a1, packed1, logs1, attended1, ln1_gain, lower_project_c, lower_merge_full
-    )
+    dx1, third, returned, shrink_pieces[3] = tie(dx1, third, returned, shrink_pieces[3])
+    third = scatter_x(third)
+
+    dx0, lower_grads, lower_sums, _, (third, second) = attention_backward(
+        dx1,
+        x0,
+        a1,
+        packed1,
+        logs1,
+        attended1,
+        ln1_gain,
+        lower_project_c,
+        lower_merge_full,
+        (third, second),
+    )
+    second = pairs_second(second)
+    third = scatter_z(third)
+    dx0, returned = tie(dx0, returned)
+    probs = gating(normed)
+    result = x3
+    for k in range(2):
+        gate = jnp.sum(widen(chosen[k]) * probs, axis=1, keepdims=True)
+        picked = product(placed[k], returned) + product(chosen[k], expert_bias)
+        result = result + gate * picked
+
     delta_patches = own_rows(dx0)
 
-    sums = jnp.stack(
-        list(lower_sums)
-        + [dgain2 * half_lanes, dshift2 * half_lanes, delta_shrink_b]
-        + list(upper_sums)
-        + [dgain4, dshift4],
-        axis=1,
-    )
-    expand_sums = delta_expand_b.reshape(devices, 1, hidden_part // 2) * (
-        jnp.arange(2, dtype=jnp.int32)[None, :, None] == core
-    ).astype(WIDE)
-    small_grads = jnp.concatenate(
-        [sums, expand_sums.reshape(width, extra), delta_router, delta_shrink_bias], axis=1
-    )
+    expand_sums = lax.dynamic_update_slice_in_dim(
+        jnp.zeros((2 * hidden_half,), WIDE), delta_expand_b, core * hidden_half, 0
+    )
+    expand_sums = expand_sums.reshape(devices, 4, part).transpose(1, 0, 2).reshape(4, width)
+    sums = jnp.concatenate(
+        [
+            jnp.stack(
+                [jnp.zeros((width,), WIDE)] * 2
+                + list(lower_sums[2:])
+                + [dgain2 * half_lanes, dshift2 * half_lanes, delta_shrink_b]
+                + list(upper_sums)
+                + [dgain4, dshift4, jnp.zeros((width,), WIDE)]
+            ),
+            expand_sums,
+            jnp.zeros((12, width), WIDE),
+        ]
+    )
+    small_grads = jnp.concatenate([sums.T, delta_router, delta_shrink_bias], axis=1)
     small_grads = jnp.pad(small_grads, ((0, 0), (0, 128 - small_grads.shape[1])))
-    first_mine, first_other = scatter_rows(jnp.concatenate([lower_grads, small_grads], axis=1), core)
-
-    def halves(mine_part, other_part):
-        return jnp.stack(
-            [
-                jnp.where(core == 0, mine_part, other_part),
-                jnp.where(core == 0, other_part, mine_part),
-            ]
-        )
-
-    def attention_outputs(mine_part, other_part):
-        both = widen(halves(mine_part, other_part))
-        project = both[:, :, : 3 * share].reshape(2, part, 3, share).transpose(1, 2, 0, 3)
-        merge = both[:, :, 3 * share : 4 * share].transpose(1, 0, 2)
-        return project.reshape(part, 3 * width), merge.reshape(part, width)
-
-    delta_lower_project, delta_lower_merge = attention_outputs(first_mine, first_other)
-    delta_upper_project, delta_upper_merge = attention_outputs(third_mine, third_other)
-    delta_lower_expand = (
-        widen(halves(expand_mine, expand_other))
-        .reshape(2, part, devices, hidden_part // 2)
-        .transpose(1, 2, 0, 3)
-        .reshape(part, -1)
-    )
-    delta_lower_shrink = widen(halves(shrink_mine, shrink_other)).reshape(hidden_part, width)
-    vector_grads = widen(first_mine[:, 4 * share :]) + widen(first_other[:, 4 * share :])
+    first = pairs_first(attention_grads(*lower_grads, small_grads))
+    first, third, expand_pieces, shrink_pieces = tie(first, third, expand_pieces, shrink_pieces)
+    third = scatter_end(third)
+    delta_expert_expand = join_columns(seat, expand_pieces)
+    delta_expert_shrink = join_columns(seat, shrink_pieces)
+    norm_sums = jnp.concatenate([jnp.stack(lower_sums[:2]), jnp.zeros((6, width), WIDE)])
+    first, second, norm_sums, delta_expert_expand = tie(
+        pairs_second(first), second, norm_sums, delta_expert_expand
+    )
+    first, second, norm_sums = pairs_z(first), pairs_z(second), summed_everywhere(norm_sums)
+    first, second, norm_sums, delta_expert_shrink = tie(
+        first, second, norm_sums, delta_expert_shrink
+    )
+    delta_expert_shrink = delta_expert_shrink.T
+    first, second = scatter_end(first), scatter_end(second)
+    norm_sums = lax.dynamic_slice_in_dim(norm_sums, here * part, part, 1)
+
+    def attention_outputs(pair):
+        mine, other = exchange_halves(pair[:part], pair[part:], core)
+        both = [jnp.where(core == 0, mine, other), jnp.where(core == 0, other, mine)]
+        cut = [[half[:, i * share : (i + 1) * share] for half in both] for i in range(4)]
+        project = jnp.concatenate(cut[0] + cut[1] + cut[2], axis=1)
+        return project, jnp.concatenate(cut[3], axis=1), mine[:, 4 * share :] + other[:, 4 * share :]
+
+    delta_lower_project, delta_lower_merge, vector_grads = attention_outputs(first)
+    delta_upper_project, delta_upper_merge, _ = attention_outputs(third)
+    mine, other = exchange_halves(second[:part, :hidden_half], second[part:, :hidden_half], core)
+    delta_lower_expand = in_order(mine, other, core, 1)
+    mine, other = exchange_halves(
+        second[:, hidden_half : hidden_half + width], second[:, hidden_half + width :], core
+    )
+    both = in_order(mine, other, core, 1)
+    delta_lower_shrink = jnp.concatenate(
+        [
+            jnp.concatenate([both[:, i * share : (i + 1) * share] for i in (row, row + 2)], axis=1)
+            for row in range(2)
+        ],
+        axis=0,
+    )
     vector_t = vector_grads.T
-    v = [vector_t[i] for i in range(count)]
-    delta_lower_expand_bias = vector_grads[:, count : count + extra].reshape(hidden_part)
-    delta_router_out = vector_grads[:, count + extra : count + extra + experts]
-    delta_expert_shrink_bias = vector_t[count + extra + experts : count + extra + 2 * experts]
+    v = [norm_sums[0], norm_sums[1]] + [vector_t[i] for i in range(2, count)]
+    delta_lower_expand_bias = vector_t[16:20].reshape(4 * part)
+    delta_router_out = vector_grads[:, 32 : 32 + experts]
+    delta_expert_shrink_bias = vector_t[64 : 64 + experts]
     return (
         result,
         delta_patches,

time: 1080 us -> 637 us (0.59)
  waiting for transfers between devices: 646 us -> 228 us
  starting transfers between devices: 59.5 us -> 97.9 us
  blocking collectives: 33.5 us -> 0 us
  Pallas kernels: 29.5 us -> 60.7 us
  other arithmetic: 78.1 us -> 51.9 us
  local copies, waits for them, and re-layouts: 98.7 us -> 73.7 us
  matrix products: 110 us -> 95 us
    reduce_scatter x4 -> x0, waiting for transfers between devices: 295 us -> none  [scatter_rows(): lax.psum_scatter(low(grads), CHIPS, scatter_dimension=0, tiled=True)]
    all_gather x4 -> x1, waiting for transfers between devices: 180 us -> 0.02 us  [local(): upper_c = lax.all_gather(pair_3, CHIPS, axis=0, tiled=True)]
    ppermute x0 -> x49, waiting for transfers between devices: none -> 153 us  [the longest x12 83.1 us: between(): return lax.ppermute(values, ('x', 'c'), xor_pairs(4, k))]
    all_to_all x5 -> x2, waiting for transfers between devices: 103 us -> 6.6 us  [to_patches(): lax.all_to_all(low(values).reshape(devices, SLOTS, width), ALL, 0, 0, til...]
    ppermute x0 -> x49, starting transfers between devices: none -> 46.7 us  [the longest x12 11.5 us: between(): return lax.ppermute(values, ('x', 'c'), xor_pairs(4, k))]
    reshape x31 -> x6, local copies, waits for them, and re-layouts: 39.5 us -> 5.14 us  [the longest x1 2.47 us: local(): delta_shrink.reshape(-1, 4, 2 * part, share).transpose(0, 2, 1, 3)]
    ppermute x4 -> x21, waiting for transfers between devices: 30.9 us -> 65.2 us  [swap_chips(): return lax.ppermute(values, 'x', SWAP)]
    all_to_all x1 -> x0, blocking collectives: 33.5 us -> none  [to_patches(): lax.all_to_all(low(values).reshape(devices, CAP, width), ALL, 0, 0, tiled...]
  transfers between devices with their start and end apart: 39 -> 96, of which waited for: 23 -> 32; matrix products, arithmetic and copies ran while one was open for 20% -> 26% of each run, Pallas kernels for 2% -> 9%
where the time goes in v2:
time: 637 us; the launch traced here: 626 us
  waiting for transfers between devices  228 us (36%)
  starting transfers between devices  97.9 us (15%)
  matrix products  95 us (15%)
  local copies, waits for them, and re-layouts  73.7 us (12%)
  Pallas kernels  60.7 us (10%)
  other arithmetic  51.9 us (8%)
  between operations  18.5 us (3%)
    dot_general x41, matrix products, dot(): lax.dot_general(left, right, ((dims[0], dims[1]), ((), ())), preferred_el...  95 us
    ppermute x12, waiting for transfers between devices, between(): return lax.ppermute(values, ('x', 'c'), xor_pairs(4, k))  83.1 us
    ppermute x21, waiting for transfers between devices, swap_chips(): return lax.ppermute(values, 'x', SWAP)  65.2 us
    unnamed x312, local copies, waits for them, and re-layouts  31.5 us
    pallas_call x4, Pallas kernels, kernel_call(): pl.pallas_call(body, out_shape=outs, in_specs=[pl.BlockSpec(memory_space=...  29.5 us
    ppermute x6, waiting for transfers between devices, gather_z(): lax.ppermute(pair, 'z', xor_pairs(4, k))  26.5 us
    ppermute x6, waiting for transfers between devices, pairs_z(): lax.ppermute(piece, 'z', xor_pairs(4, k + 1))  22.7 us
    ppermute x21, starting transfers between devices, swap_cores(): return lax.ppermute(values, 'c', SWAP)  20.7 us
  transfers between devices with their start and end apart: 96, of which 32 were waited for; matrix products, arithmetic and copies ran while one was open for 26% of the time, Pallas kernels for 9%

profile of v2, /device:TPU:9, one launch (start us, length us, event | category | flops | bytes accessed | tf_op | source)
XLA Modules:
  0.0 625.8 jit_solution(5335850339541534932)
XLA Ops:
  39.3 7.9 %collective-permute-done.15.refs_12_ = bf16[48,1664]{1,0:T(8,128)(2,1)S(1)} collective-permute-done((bf16[48,1664]{1,0:T(8,128)(2,1)S(1)}, bf16[48,1664]{1,0:T(8,128)(2,1)S(1)}, u32[]{:S(2)}, u32[]{:S(2)}) %collective-permute-start.15) | collective-permute-done | bytes 159776 | tf_op jit(solution)/shard_map/ppermute | solution.py:355
  59.6 6.0 collective-permute-done.18.refs_15_
  72.5 4.9 collective-permute-start.2
  94.1 15.7 %collective-permute-done.34.refs_12_ = bf16[48,3072]{1,0:T(8,128)(2,1)S(1)} collective-permute-done((bf16[48,3072]{1,0:T(8,128)(2,1)S(1)}, bf16[48,3072]{1,0:T(8,128)(2,1)S(1)}, u32[]{:S(2)}, u32[]{:S(2)}) %collective-permute-start.34) | collective-permute-done | bytes 294944 | tf_op jit(solution)/shard_map/ppermute | solution.py:355
  118.1 6.3 %collective-permute-done.36.refs_14_ = bf16[48,3072]{1,0:T(8,128)(2,1)S(1)} collective-permute-done((bf16[48,3072]{1,0:T(8,128)(2,1)S(1)}, bf16[48,3072]{1,0:T(8,128)(2,1)S(1)}, u32[]{:S(2)}, u32[]{:S(2)}) %collective-permute-start.36) | collective-permute-done | bytes 294944 | tf_op jit(solution)/shard_map/ppermute | solution.py:361
  128.0 5.6 shard_map.522
  158.1 32.2 %collective-permute-done.40 = bf16[160,768]{1,0:T(8,128)(2,1)} collective-permute-done((bf16[160,768]{1,0:T(8,128)(2,1)}, bf16[160,768]{1,0:T(8,128)(2,1)}, u32[]{:S(2)}, u32[]{:S(2)}) %collective-permute-start.40) | collective-permute-done | bytes 245792 | tf_op jit(solution)/shard_map/ppermute | solution.py:55
  198.8 5.3 shard_map.524
  210.2 11.9 %collective-permute-done.44.refs_3_ = bf16[192,3072]{1,0:T(8,128)(2,1)} collective-permute-done((bf16[192,3072]{1,0:T(8,128)(2,1)}, bf16[192,3072]{1,0:T(8,128)(2,1)}, u32[]{:S(2)}, u32[]{:S(2)}) %collective-permute-start.44) | collective-permute-done | bytes 1179680 | tf_op jit(solution)/shard_map/ppermute | solution.py:758
  234.5 19.8 %collective-permute-done.47.refs_2_ = bf16[192,3072]{1,0:T(8,128)(2,1)} collective-permute-done((bf16[192,3072]{1,0:T(8,128)(2,1)}, bf16[192,3072]{1,0:T(8,128)(2,1)}, u32[]{:S(2)}, u32[]{:S(2)}) %collective-permute-start.47) | collective-permute-done | bytes 1179680 | tf_op jit(solution)/shard_map/ppermute | solution.py:758
  274.7 5.1 fusion.158
  287.0 11.0 %multiply_reduce_fusion = (f32[768]{0:T(1024)S(1)}, bf16[768,3072]{1,0:T(8,128)(2,1)}, bf16[768,3072]{1,0:T(8,128)(2,1)S(1)}) fusion(f32[768,3072]{1,0:T(8,128)S(1)} %fusion.158, f32[3072]{0:T(1024)S(1)} %copy-done.122, f32[768]{0:T(1024)S(1)} %multiply_reduce_fusion.15, bf16[768,768]{1,0:T(8,128)(2,1)} %bitcast.22, bf16[768,3072]{1,0:T(8,128)(2,1)S(1)} %shard_map.525), kind=kOutput, calls=%fused_computation.7 | convolution fusion | flops 3663985920 | bytes 24791040 | tf_op jit(solution)/shard_map/dot_general | solution.py:27
  298.9 8.0 %convolution_convert_fusion.1 = bf16[768,3072]{1,0:T(8,128)(2,1)} fusion(bf16[768,768]{1,0:T(8,128)(2,1)} %bitcast.24, bf16[768,3072]{1,0:T(8,128)(2,1)S(1)} %get-tuple-element.311), kind=kOutput, calls=%fused_computation.19 | convolution fusion | flops 3626237952 | bytes 10616832 | tf_op jit(solution)/shard_map/dot_general | solution.py:27
  306.9 4.9 add_convert_fusion.4
  321.1 8.9 %convolution_convert_fusion = bf16[768,3072]{1,0:T(8,128)(2,1)} fusion(bf16[768,3072]{1,0:T(8,128)(2,1)} %get-tuple-element.308, bf16[768,768]{1,0:T(8,128)(2,1)} %bitcast.22, f32[768]{0:T(1024)S(1)} %multiply_reduce_fusion.15), kind=kOutput, calls=%fused_computation.18 | convolution fusion | flops 3628007424 | bytes 10619904 | tf_op jit(solution)/shard_map/dot_general | solution.py:27
  331.8 4.9 convolution_convert_fusion.4
  336.6 6.6 %all-to-all-done.2 = bf16[32,24,768]{2,1,0:T(8,128)(2,1)} async-done(((bf16[32,24,768]{2,1,0:T(8,128)(2,1)}), bf16[32,24,768]{2,1,0:T(8,128)(2,1)}, u32[]{:S(2)}, u32[]{:S(2)}) %all-to-all-start.2) | async-done | bytes 1179680 | tf_op jit(solution)/shard_map/all_to_all | solution.py:803
  343.2 4.8 all-to-all-start.3
  348.0 10.8 %collective-permute-done.51.refs_2_ = bf16[192,3072]{1,0:T(8,128)(2,1)} collective-permute-done((bf16[192,3072]{1,0:T(8,128)(2,1)}, bf16[192,3072]{1,0:T(8,128)(2,1)}, u32[]{:S(2)}, u32[]{:S(2)}) %collective-permute-start.51) | collective-permute-done | bytes 1179680 | tf_op jit(solution)/shard_map/ppermute | solution.py:758
  374.8 9.4 %shard_map.527.dpacked = bf16[832,1152]{1,0:T(8,128)(2,1)S(1)} custom-call(s32[3]{0:T(128)S(1)} %pad_add_fusion.scalars, bf16[832,1152]{1,0:T(8,128)(2,1)S(1)} %copy-done.36, bf16[512,384]{1,0:T(8,128)(2,1)S(1)} %convolution_convert_fusion.9.grads, f32[512,384]{1,0:T(8,128)S(1)} %copy-done.40), custom_call_target="tpu_custom_call" | custom-call | flops 4000000000 | bytes 8000000 | tf_op jit(solution)/shard_map/pallas_call | solution.py:248
  386.0 13.7 %collective-permute-done.53.refs_3_ = bf16[192,3072]{1,0:T(8,128)(2,1)S(1)} collective-permute-done((bf16[192,3072]{1,0:T(8,128)(2,1)S(1)}, bf16[192,3072]{1,0:T(8,128)(2,1)S(1)}, u32[]{:S(2)}, u32[]{:S(2)}) %collective-permute-start.53) | collective-permute-done | bytes 1179680 | tf_op jit(solution)/shard_map/ppermute | solution.py:758
  407.7 5.8 collective-permute-done.54
  425.9 5.0 concatenate.109
  437.4 7.6 %collective-permute-done.56.refs_2_ = bf16[192,3072]{1,0:T(8,128)(2,1)} collective-permute-done((bf16[192,3072]{1,0:T(8,128)(2,1)}, bf16[192,3072]{1,0:T(8,128)(2,1)}, u32[]{:S(2)}, u32[]{:S(2)}) %collective-permute-start.56) | collective-permute-done | bytes 1179680 | tf_op jit(solution)/shard_map/ppermute | solution.py:758
  464.2 14.6 %collective-permute-done.59.refs_3_ = bf16[192,3072]{1,0:T(8,128)(2,1)} collective-permute-done((bf16[192,3072]{1,0:T(8,128)(2,1)}, bf16[192,3072]{1,0:T(8,128)(2,1)}, u32[]{:S(2)}, u32[]{:S(2)}) %collective-permute-start.59) | collective-permute-done | bytes 1179680 | tf_op jit(solution)/shard_map/ppermute | solution.py:758
  485.6 9.2 %shard_map.529.dpacked = bf16[832,1152]{1,0:T(8,128)(2,1)S(1)} custom-call(s32[3]{0:T(128)S(1)} %pad_add_fusion.scalars, bf16[832,1152]{1,0:T(8,128)(2,1)S(1)} %copy-done.34, bf16[512,384]{1,0:T(8,128)(2,1)S(1)} %convolution_convert_fusion.8.grads, f32[512,384]{1,0:T(8,128)S(1)} %copy-done.38), custom_call_target="tpu_custom_call" | custom-call | flops 4000000000 | bytes 8000000 | tf_op jit(solution)/shard_map/pallas_call | solution.py:248
  523.8 5.4 collective-permute-done.67
  536.1 5.6 shard_map.531
  541.7 6.3 %shard_map.532 = f32[192,12288]{1,0:T(8,128)} custom-call(s32[1]{0:T(128)} %bitcast.7.place, bf16[192,3072]{1,0:T(8,128)(2,1)S(1)} %get-tuple-element.240.refs_0_, bf16[192,3072]{1,0:T(8,128)(2,1)} %collective-permute-done.71.refs_1_, bf16[192,3072]{1,0:T(8,128)(2,1)} %collective-permute-done.56.refs_2_, bf16[192,3072]{1,0:T(8,128)(2,1)} %collective-permute-done.59.refs_3_), custom_call_target="tpu_custom_call" | custom-call | bytes 14155776 | tf_op jit(solution)/shard_map/pallas_call | solution.py:520
  553.2 6.0 collective-permute-done.72
  587.5 16.3 %collective-permute-done.80 = bf16[48,3072]{1,0:T(8,128)(2,1)S(1)} collective-permute-done((bf16[48,3072]{1,0:T(8,128)(2,1)S(1)}, bf16[48,3072]{1,0:T(8,128)(2,1)S(1)}, u32[]{:S(2)}, u32[]{:S(2)}) %collective-permute-start.80) | collective-permute-done | bytes 294944 | tf_op jit(solution)/shard_map/ppermute | solution.py:419
  603.9 6.3 %collective-permute-done.81 = bf16[48,3072]{1,0:T(8,128)(2,1)S(1)} collective-permute-done((bf16[48,3072]{1,0:T(8,128)(2,1)S(1)}, bf16[48,3072]{1,0:T(8,128)(2,1)S(1)}, u32[]{:S(2)}, u32[]{:S(2)}) %collective-permute-start.81) | collective-permute-done | bytes 294944 | tf_op jit(solution)/shard_map/ppermute | solution.py:419
  (727 shorter events, 315.5 us)
Async XLA Ops:
  7.2 188.2 %all-gather.2.cloned.1.call-start = ((), (), s32[]{:S(2)}) async-start(), calls=%async_computation.4 | async-start | bytes 2506752 | tf_op jit(solution)/shard_map/all_gather | solution.py:727
  10.7 37.0 %collective-permute-start = (bf16[256,768]{1,0:T(8,128)(2,1)}, bf16[256,768]{1,0:T(8,128)(2,1)S(1)}, u32[]{:S(2)}, u32[]{:S(2)}) collective-permute-start(bf16[256,768]{1,0:T(8,128)(2,1)} %param.31), channel_id=1, source_target_pairs={{0,1},{1,0},{2,3},{3,2},{4,5},{5,4},{6,7},{7,6},{8,9},{9,8},{10,11... | collective-permute-start | bytes 1179656 | tf_op jit(solution)/shard_map/ppermute | solution.py:51
  58.6 29.1 %collective-permute-start.23 = (bf16[48,3072]{1,0:T(8,128)(2,1)S(1)}, bf16[48,3072]{1,0:T(8,128)(2,1)S(1)}, u32[]{:S(2)}, u32[]{:S(2)}) collective-permute-start(bf16[48,3072]{1,0:T(8,128)(2,1)S(1)} %pad_maximum_fusion.17.refs_0_), channel_id=1, source_target_pairs={{0,2},{2,0},{1,3},{3,1},{4,6},{6,4},{5,7},{7,5},{8,10},{10,8},{9,1... | collective-permute-start | bytes 884744 | tf_op jit(solution)/shard_map/ppermute | solution.py:55
  59.6 33.2 %collective-permute-start.24 = (bf16[48,3072]{1,0:T(8,128)(2,1)S(1)}, bf16[48,3072]{1,0:T(8,128)(2,1)S(1)}, u32[]{:S(2)}, u32[]{:S(2)}) collective-permute-start(bf16[48,3072]{1,0:T(8,128)(2,1)S(1)} %pad_maximum_fusion.17.refs_0_), channel_id=1, source_target_pairs={{0,4},{4,0},{1,5},{5,1},{2,6},{6,2},{3,7},{7,3},{8,12},{12,8},{9,1... | collective-permute-start | bytes 884744 | tf_op jit(solution)/shard_map/ppermute | solution.py:361
  59.6 29.6 %collective-permute-start.26 = (bf16[48,3072]{1,0:T(8,128)(2,1)S(1)}, bf16[48,3072]{1,0:T(8,128)(2,1)S(1)}, u32[]{:S(2)}, u32[]{:S(2)}) collective-permute-start(bf16[48,3072]{1,0:T(8,128)(2,1)S(1)} %pad_maximum_fusion.17.refs_0_), channel_id=1, source_target_pairs={{0,8},{8,0},{16,24},{24,16},{1,9},{9,1},{17,25},{25,17},{2,10},{10... | collective-permute-start | bytes 884744 | tf_op jit(solution)/shard_map/ppermute | solution.py:355
  65.6 28.2 %collective-permute-start.30 = (bf16[48,3072]{1,0:T(8,128)(2,1)S(1)}, bf16[48,3072]{1,0:T(8,128)(2,1)}, u32[]{:S(2)}, u32[]{:S(2)}) collective-permute-start(bf16[48,3072]{1,0:T(8,128)(2,1)S(1)} %pad_maximum_fusion.17.refs_0_), channel_id=1, source_target_pairs={{0,16},{8,24},{16,0},{24,8},{1,17},{9,25},{17,1},{25,9},{2,18},{10... | collective-permute-start | bytes 884744 | tf_op jit(solution)/shard_map/ppermute | solution.py:355
  112.4 26.2 %collective-permute-start.20 = (bf16[768,384]{1,0:T(8,128)(2,1)S(1)}, bf16[768,384]{1,0:T(8,128)(2,1)S(1)}, u32[]{:S(2)}, u32[]{:S(2)}) collective-permute-start(bf16[768,384]{1,0:T(8,128)(2,1)S(1)} %get-tuple-element.158), channel_id=1, source_target_pairs={{0,1},{1,0},{2,3},{3,2},{4,5},{5,4},{6,7},{7,6},{8,9},{9,8},{10,11... | collective-permute-start | bytes 1769480 | tf_op jit(solution)/shard_map/ppermute | solution.py:51
  148.1 44.4 %collective-permute-start.42 = (bf16[192,3072]{1,0:T(8,128)(2,1)}, bf16[192,3072]{1,0:T(8,128)(2,1)S(1)}, u32[]{:S(2)}, u32[]{:S(2)}) collective-permute-start(bf16[192,3072]{1,0:T(8,128)(2,1)} %get-tuple-element.170), channel_id=1, source_target_pairs={{0,2},{1,3},{2,0},{3,1},{4,6},{5,7},{6,4},{7,5},{8,10},{9,11},{10,... | collective-permute-start | bytes 3538952 | tf_op jit(solution)/shard_map/ppermute | solution.py:758
  152.3 37.9 %collective-permute-start.40 = (bf16[160,768]{1,0:T(8,128)(2,1)}, bf16[160,768]{1,0:T(8,128)(2,1)}, u32[]{:S(2)}, u32[]{:S(2)}) collective-permute-start(bf16[160,768]{1,0:T(8,128)(2,1)} %constant_dynamic-slice_fusion.12), channel_id=1, source_target_pairs={{0,2},{2,0},{1,3},{3,1},{4,6},{6,4},{5,7},{7,5},{8,10},{10,8},{9,1... | collective-permute-start | bytes 737288 | tf_op jit(solution)/shard_map/ppermute | solution.py:55
  155.0 55.2 %all-to-all-start = ((bf16[32,24,768]{2,1,0:T(8,128)(2,1)}), bf16[32,24,768]{2,1,0:T(8,128)(2,1)}, u32[]{:S(2)}, u32[]{:S(2)}) async-start(bf16[32,24,768]{2,1,0:T(8,128)(2,1)} %bitcast.173), calls=%async_computation | async-start | bytes 2359296 | tf_op jit(solution)/shard_map/all_to_all | solution.py:799
  193.5 28.5 %collective-permute-start.44 = (bf16[192,3072]{1,0:T(8,128)(2,1)}, bf16[192,3072]{1,0:T(8,128)(2,1)}, u32[]{:S(2)}, u32[]{:S(2)}) collective-permute-start(bf16[192,3072]{1,0:T(8,128)(2,1)} %copy-done.32), channel_id=1, source_target_pairs={{0,3},{1,2},{2,1},{3,0},{4,7},{5,6},{6,5},{7,4},{8,11},{9,10},{10,... | collective-permute-start | bytes 3538952 | tf_op jit(solution)/shard_map/ppermute | solution.py:758
  208.6 45.6 %collective-permute-start.47 = (bf16[192,3072]{1,0:T(8,128)(2,1)}, bf16[192,3072]{1,0:T(8,128)(2,1)}, u32[]{:S(2)}, u32[]{:S(2)}) collective-permute-start(bf16[192,3072]{1,0:T(8,128)(2,1)} %copy-done.31), channel_id=1, source_target_pairs={{0,2},{1,3},{2,0},{3,1},{4,6},{5,7},{6,4},{7,5},{8,10},{9,11},{10,... | collective-permute-start | bytes 3538952 | tf_op jit(solution)/shard_map/ppermute | solution.py:758
  209.2 49.1 %collective-permute-start.61 = (bf16[512,1536]{1,0:T(8,128)(2,1)}, bf16[512,1536]{1,0:T(8,128)(2,1)}, u32[]{:S(2)}, u32[]{:S(2)}) collective-permute-start(bf16[512,1536]{1,0:T(8,128)(2,1)} %copy-done.76), channel_id=1, source_target_pairs={{0,1},{1,0},{2,3},{3,2},{4,5},{5,4},{6,7},{7,6},{8,9},{9,8},{10,11... | collective-permute-start | bytes 4718600 | tf_op jit(solution)/shard_map/ppermute | solution.py:51
  227.4 38.4 %all-to-all-start.1 = ((bf16[32,24,768]{2,1,0:T(8,128)(2,1)}), bf16[32,24,768]{2,1,0:T(8,128)(2,1)}, u32[]{:S(2)}, u32[]{:S(2)}) async-start(bf16[32,24,768]{2,1,0:T(8,128)(2,1)} %bitcast.181), calls=%async_computation.1 | async-start | bytes 2359296 | tf_op jit(solution)/shard_map/all_to_all | solution.py:799
  232.8 32.0 %collective-permute-start.46 = (bf16[192,3072]{1,0:T(8,128)(2,1)S(1)}, bf16[192,3072]{1,0:T(8,128)(2,1)S(1)}, u32[]{:S(2)}, u32[]{:S(2)}) collective-permute-start(bf16[192,3072]{1,0:T(8,128)(2,1)S(1)} %copy-done.30), channel_id=1, source_target_pairs={{0,1},{1,0},{2,3},{3,2},{4,5},{5,4},{6,7},{7,6},{8,9},{9,8},{10,11... | collective-permute-start | bytes 3538952 | tf_op jit(solution)/shard_map/ppermute | solution.py:758
  232.9 47.0 %collective-permute-start.48 = (bf16[192,3072]{1,0:T(8,128)(2,1)}, bf16[192,3072]{1,0:T(8,128)(2,1)}, u32[]{:S(2)}, u32[]{:S(2)}) collective-permute-start(bf16[192,3072]{1,0:T(8,128)(2,1)} %get-tuple-element.188), channel_id=1, source_target_pairs={{0,1},{1,0},{2,3},{3,2},{4,5},{5,4},{6,7},{7,6},{8,9},{9,8},{10,11... | collective-permute-start | bytes 3538952 | tf_op jit(solution)/shard_map/ppermute | solution.py:758
  254.3 30.4 %collective-permute-start.49 = (bf16[192,3072]{1,0:T(8,128)(2,1)}, bf16[192,3072]{1,0:T(8,128)(2,1)}, u32[]{:S(2)}, u32[]{:S(2)}) collective-permute-start(bf16[192,3072]{1,0:T(8,128)(2,1)} %get-tuple-element.191), channel_id=1, source_target_pairs={{0,3},{1,2},{2,1},{3,0},{4,7},{5,6},{6,5},{7,4},{8,11},{9,10},{10,... | collective-permute-start | bytes 3538952 | tf_op jit(solution)/shard_map/ppermute | solution.py:758
  311.8 31.4 %all-to-all-start.2 = ((bf16[32,24,768]{2,1,0:T(8,128)(2,1)}), bf16[32,24,768]{2,1,0:T(8,128)(2,1)}, u32[]{:S(2)}, u32[]{:S(2)}) async-start(bf16[32,24,768]{2,1,0:T(8,128)(2,1)} %bitcast.26), calls=%async_computation.2 | async-start | bytes 2359296 | tf_op jit(solution)/shard_map/all_to_all | solution.py:803
  319.6 28.4 %collective-permute-start.50 = (bf16[192,3072]{1,0:T(8,128)(2,1)}, bf16[192,3072]{1,0:T(8,128)(2,1)}, u32[]{:S(2)}, u32[]{:S(2)}) collective-permute-start(bf16[192,3072]{1,0:T(8,128)(2,1)} %get-tuple-element.319), channel_id=1, source_target_pairs={{0,1},{1,0},{2,3},{3,2},{4,5},{5,4},{6,7},{7,6},{8,9},{9,8},{10,11... | collective-permute-start | bytes 3538952 | tf_op jit(solution)/shard_map/ppermute | solution.py:758
  319.9 38.9 %collective-permute-start.51 = (bf16[192,3072]{1,0:T(8,128)(2,1)}, bf16[192,3072]{1,0:T(8,128)(2,1)}, u32[]{:S(2)}, u32[]{:S(2)}) collective-permute-start(bf16[192,3072]{1,0:T(8,128)(2,1)} %get-tuple-element.318), channel_id=1, source_target_pairs={{0,2},{1,3},{2,0},{3,1},{4,6},{5,7},{6,4},{7,5},{8,10},{9,11},{10,... | collective-permute-start | bytes 3538952 | tf_op jit(solution)/shard_map/ppermute | solution.py:758
  343.2 120.9 %all-to-all-start.3 = ((bf16[32,24,768]{2,1,0:T(8,128)(2,1)}), bf16[32,24,768]{2,1,0:T(8,128)(2,1)}, u32[]{:S(2)}, u32[]{:S(2)}) async-start(bf16[32,24,768]{2,1,0:T(8,128)(2,1)} %bitcast.180), calls=%async_computation.3 | async-start | bytes 2359296 | tf_op jit(solution)/shard_map/all_to_all | solution.py:803
  370.6 29.2 %collective-permute-start.53 = (bf16[192,3072]{1,0:T(8,128)(2,1)S(1)}, bf16[192,3072]{1,0:T(8,128)(2,1)S(1)}, u32[]{:S(2)}, u32[]{:S(2)}) collective-permute-start(bf16[192,3072]{1,0:T(8,128)(2,1)S(1)} %copy-done.83), channel_id=1, source_target_pairs={{0,3},{1,2},{2,1},{3,0},{4,7},{5,6},{6,5},{7,4},{8,11},{9,10},{10,... | collective-permute-start | bytes 3538952 | tf_op jit(solution)/shard_map/ppermute | solution.py:758
  406.5 57.7 %collective-permute-start.58 = (bf16[4,2,48,1536]{3,2,1,0:T(8,128)(2,1)}, bf16[4,2,48,1536]{3,2,1,0:T(8,128)(2,1)}, u32[]{:S(2)}, u32[]{:S(2)}) collective-permute-start(bf16[4,2,48,1536]{3,2,1,0:T(8,128)(2,1)} %get-tuple-element.334), channel_id=1, source_target_pairs={{0,4},{4,0},{1,5},{5,1},{2,6},{6,2},{3,7},{7,3},{8,12},{12,8},{9,1... | collective-permute-start | bytes 3538952 | tf_op jit(solution)/shard_map/ppermute | solution.py:436
  417.1 27.9 %collective-permute-start.56 = (bf16[192,3072]{1,0:T(8,128)(2,1)}, bf16[192,3072]{1,0:T(8,128)(2,1)}, u32[]{:S(2)}, u32[]{:S(2)}) collective-permute-start(bf16[192,3072]{1,0:T(8,128)(2,1)} %get-tuple-element.315), channel_id=1, source_target_pairs={{0,2},{1,3},{2,0},{3,1},{4,6},{5,7},{6,4},{7,5},{8,10},{9,11},{10,... | collective-permute-start | bytes 3538952 | tf_op jit(solution)/shard_map/ppermute | solution.py:758
  418.0 104.8 %collective-permute-start.71 = (bf16[192,3072]{1,0:T(8,128)(2,1)}, bf16[192,3072]{1,0:T(8,128)(2,1)}, u32[]{:S(2)}, u32[]{:S(2)}) collective-permute-start(bf16[192,3072]{1,0:T(8,128)(2,1)} %get-tuple-element.312), channel_id=1, source_target_pairs={{0,1},{1,0},{2,3},{3,2},{4,5},{5,4},{6,7},{7,6},{8,9},{9,8},{10,11... | collective-permute-start | bytes 3538952 | tf_op jit(solution)/shard_map/ppermute | solution.py:758
  449.9 28.8 %collective-permute-start.59 = (bf16[192,3072]{1,0:T(8,128)(2,1)}, bf16[192,3072]{1,0:T(8,128)(2,1)}, u32[]{:S(2)}, u32[]{:S(2)}) collective-permute-start(bf16[192,3072]{1,0:T(8,128)(2,1)} %get-tuple-element.203), channel_id=1, source_target_pairs={{0,3},{1,2},{2,1},{3,0},{4,7},{5,6},{6,5},{7,4},{8,11},{9,10},{10,... | collective-permute-start | bytes 3538952 | tf_op jit(solution)/shard_map/ppermute | solution.py:758
  452.4 57.5 %collective-permute-start.62 = (bf16[2,2,48,3072]{3,2,1,0:T(8,128)(2,1)}, bf16[2,2,48,3072]{3,2,1,0:T(8,128)(2,1)}, u32[]{:S(2)}, u32[]{:S(2)}) collective-permute-start(bf16[2,2,48,3072]{3,2,1,0:T(8,128)(2,1)} %get-tuple-element.322), channel_id=1, source_target_pairs={{0,4},{4,0},{1,5},{5,1},{2,6},{6,2},{3,7},{7,3},{8,12},{12,8},{9,1... | collective-permute-start | bytes 3538952 | tf_op jit(solution)/shard_map/ppermute | solution.py:400
  457.5 53.3 %collective-permute-start.63 = (bf16[2,2,48,3072]{3,2,1,0:T(8,128)(2,1)}, bf16[2,2,48,3072]{3,2,1,0:T(8,128)(2,1)}, u32[]{:S(2)}, u32[]{:S(2)}) collective-permute-start(bf16[2,2,48,3072]{3,2,1,0:T(8,128)(2,1)} %get-tuple-element.320), channel_id=1, source_target_pairs={{0,2},{2,0},{1,3},{3,1},{4,6},{6,4},{5,7},{7,5},{8,10},{10,8},{9,1... | collective-permute-start | bytes 3538952 | tf_op jit(solution)/shard_map/ppermute | solution.py:55
  484.8 30.8 %collective-permute-start.60 = (bf16[4,48,1536]{2,1,0:T(8,128)(2,1)}, bf16[4,48,1536]{2,1,0:T(8,128)(2,1)}, u32[]{:S(2)}, u32[]{:S(2)}) collective-permute-start(bf16[4,48,1536]{2,1,0:T(8,128)(2,1)} %get-tuple-element.342), channel_id=1, source_target_pairs={{0,2},{2,0},{1,3},{3,1},{4,6},{6,4},{5,7},{7,5},{8,10},{10,8},{9,1... | collective-permute-start | bytes 1769480 | tf_op jit(solution)/shard_map/ppermute | solution.py:55
  529.1 30.0 %collective-permute-start.74 = (bf16[2,48,3072]{2,1,0:T(8,128)(2,1)S(1)}, bf16[2,48,3072]{2,1,0:T(8,128)(2,1)S(1)}, u32[]{:S(2)}, u32[]{:S(2)}) collective-permute-start(bf16[2,48,3072]{2,1,0:T(8,128)(2,1)S(1)} %get-tuple-element.340), channel_id=1, source_target_pairs={{0,2},{2,0},{1,3},{3,1},{4,6},{6,4},{5,7},{7,5},{8,10},{10,8},{9,1... | collective-permute-start | bytes 1769480 | tf_op jit(solution)/shard_map/ppermute | solution.py:55
  530.0 29.2 %collective-permute-start.75 = (bf16[2,48,3072]{2,1,0:T(8,128)(2,1)S(1)}, bf16[2,48,3072]{2,1,0:T(8,128)(2,1)S(1)}, u32[]{:S(2)}, u32[]{:S(2)}) collective-permute-start(bf16[2,48,3072]{2,1,0:T(8,128)(2,1)S(1)} %get-tuple-element.338), channel_id=1, source_target_pairs={{0,4},{4,0},{1,5},{5,1},{2,6},{6,2},{3,7},{7,3},{8,12},{12,8},{9,1... | collective-permute-start | bytes 1769480 | tf_op jit(solution)/shard_map/ppermute | solution.py:409
  559.7 27.9 %collective-permute-start.77 = (bf16[48,1664]{1,0:T(8,128)(2,1)S(1)}, bf16[48,1664]{1,0:T(8,128)(2,1)S(1)}, u32[]{:S(2)}, u32[]{:S(2)}) collective-permute-start(bf16[48,1664]{1,0:T(8,128)(2,1)S(1)} %get-tuple-element.390), channel_id=1, source_target_pairs={{0,16},{8,24},{16,0},{24,8},{1,17},{9,25},{17,1},{25,9},{2,18},{10... | collective-permute-start | bytes 479240 | tf_op jit(solution)/shard_map/ppermute | solution.py:419
  (217 other events, 2165.9 us)
Sparse Core Ops, SparseCore 0:
  33.4 71.5 all-gather.1

commit v3 on v2

--- a/solution.py
+++ b/solution.py
@@ -867,6 +867,7 @@
     dbefore = low(gate_in * raw * slope)
     dlogits = low(probs_in * delta_gate * (mine - gate_in))
     drows = over_features(dbefore, expand_e) + product(dlogits, router_t)
+    drows, dbefore, expert_hidden = tie(low(drows), dbefore, expert_hidden)
     returned_grad = to_patches(drows)
     returned = to_patches(over_features(expert_hidden, shrink_e))
     g_out = low(gate_in * widen(grad_rows))
@@ -876,8 +877,8 @@
     delta_router = over_rows(rows_in, dlogits)
     delta_shrink_e = low(delta_shrink_e)
     expand_pieces = expert_parts(low(delta_expand_e))
-    returned_grad, expand_pieces[1], expand_pieces[2], delta_shrink_e = tie(
-        returned_grad, expand_pieces[1], expand_pieces[2], delta_shrink_e
+    returned_grad, expand_pieces[1], delta_shrink_e = tie(
+        returned_grad, expand_pieces[1], delta_shrink_e
     )
     delta_shrink_bias = (column_sums(g_out) * once)[:, None] * mine
 
@@ -885,6 +886,7 @@
     dx3, dgain4, dshift4 = layer_norm_back(x3, ln4_gain, delta_normed)
     dx3 = output_grad + dx3
     dx3 = in_order(dx3, swap_cores(dx3), core, 0)
+    dx3, expand_pieces[2] = tie(dx3, expand_pieces[2])
     half_lanes = (jnp.arange(width, dtype=jnp.int32) // share == core).astype(WIDE)
 
     def columns_of_half(values):
@@ -951,10 +953,10 @@
     )
     dinput, dgain2, dshift2 = layer_norm_back(x1, ln2_gain, widen(dnormed) + widen(swap_cores(dnormed)))
     dx1 = dx2 + dinput
-    dx1, third, returned, shrink_pieces[3] = tie(dx1, third, returned, shrink_pieces[3])
+    dx1, third, returned = tie(dx1, third, returned)
     third = scatter_x(third)
 
-    dx0, lower_grads, lower_sums, _, (third, second) = attention_backward(
+    dx0, lower_grads, lower_sums, _, (third, second, shrink_pieces[3]) = attention_backward(
         dx1,
         x0,
         a1,
@@ -964,7 +966,7 @@
         ln1_gain,
         lower_project_c,
         lower_merge_full,
-        (third, second),
+        (third, second, shrink_pieces[3]),
     )
     second = pairs_second(second)
     third = scatter_z(third)

time: 637 us -> 633 us (level)
  starting transfers between devices: 97.9 us -> 105 us
    ppermute x12, waiting for transfers between devices: 83.1 us -> 66.9 us  [between(): return lax.ppermute(values, ('x', 'c'), xor_pairs(4, k))]
    all_to_all x2, starting transfers between devices: 6.56 us -> 15.4 us  [to_experts(): got = lax.all_to_all(sent, ALL, 0, 0, tiled=True)]
    ppermute x21, waiting for transfers between devices: 65.2 us -> 71.9 us  [swap_chips(): return lax.ppermute(values, 'x', SWAP)]
  transfers between devices with their start and end apart: 96 -> 96, of which waited for: 32 -> 34; matrix products, arithmetic and copies ran while one was open for 26% -> 26% of each run, Pallas kernels for 9% -> 9%
where the time goes in v3:
time: 633 us; the launch traced here: 622 us
  waiting for transfers between devices  222 us (35%)
  starting transfers between devices  105 us (17%)
  matrix products  93.6 us (15%)
  local copies, waits for them, and re-layouts  71.4 us (11%)
  Pallas kernels  60.7 us (10%)
  other arithmetic  51.2 us (8%)
  between operations  18.5 us (3%)
    dot_general x41, matrix products, dot(): lax.dot_general(left, right, ((dims[0], dims[1]), ((), ())), preferred_el...  93.6 us
    ppermute x21, waiting for transfers between devices, swap_chips(): return lax.ppermute(values, 'x', SWAP)  71.9 us
    ppermute x12, waiting for transfers between devices, between(): return lax.ppermute(values, ('x', 'c'), xor_pairs(4, k))  66.9 us
    unnamed x312, local copies, waits for them, and re-layouts  32.6 us
    pallas_call x4, Pallas kernels, kernel_call(): pl.pallas_call(body, out_shape=outs, in_specs=[pl.BlockSpec(memory_space=...  29.4 us
    ppermute x6, waiting for transfers between devices, gather_z(): lax.ppermute(pair, 'z', xor_pairs(4, k))  26.5 us
    ppermute x6, waiting for transfers between devices, pairs_z(): lax.ppermute(piece, 'z', xor_pairs(4, k + 1))  23.4 us
    ppermute x21, starting transfers between devices, swap_cores(): return lax.ppermute(values, 'c', SWAP)  20.7 us
  transfers between devices with their start and end apart: 96, of which 34 were waited for; matrix products, arithmetic and copies ran while one was open for 26% of the time, Pallas kernels for 9%

profile of v3, /device:TPU:9, one launch (start us, length us, event | category | flops | bytes accessed | tf_op | source)
XLA Modules:
  0.0 622.2 jit_solution(18297062021217222328)
XLA Ops:
  38.5 7.9 %collective-permute-done.15.refs_12_ = bf16[48,1664]{1,0:T(8,128)(2,1)S(1)} collective-permute-done((bf16[48,1664]{1,0:T(8,128)(2,1)S(1)}, bf16[48,1664]{1,0:T(8,128)(2,1)S(1)}, u32[]{:S(2)}, u32[]{:S(2)}) %collective-permute-start.15) | collective-permute-done | bytes 159776 | tf_op jit(solution)/shard_map/ppermute | solution.py:355
  58.8 6.0 collective-permute-done.18.refs_15_
  71.7 4.9 collective-permute-start.2
  93.3 15.7 %collective-permute-done.34.refs_12_ = bf16[48,3072]{1,0:T(8,128)(2,1)S(1)} collective-permute-done((bf16[48,3072]{1,0:T(8,128)(2,1)S(1)}, bf16[48,3072]{1,0:T(8,128)(2,1)S(1)}, u32[]{:S(2)}, u32[]{:S(2)}) %collective-permute-start.34) | collective-permute-done | bytes 294944 | tf_op jit(solution)/shard_map/ppermute | solution.py:355
  117.3 6.3 %collective-permute-done.36.refs_14_ = bf16[48,3072]{1,0:T(8,128)(2,1)S(1)} collective-permute-done((bf16[48,3072]{1,0:T(8,128)(2,1)S(1)}, bf16[48,3072]{1,0:T(8,128)(2,1)S(1)}, u32[]{:S(2)}, u32[]{:S(2)}) %collective-permute-start.36) | collective-permute-done | bytes 294944 | tf_op jit(solution)/shard_map/ppermute | solution.py:361
  127.1 5.5 shard_map.522
  157.0 32.3 %collective-permute-done.40 = bf16[160,768]{1,0:T(8,128)(2,1)} collective-permute-done((bf16[160,768]{1,0:T(8,128)(2,1)}, bf16[160,768]{1,0:T(8,128)(2,1)}, u32[]{:S(2)}, u32[]{:S(2)}) %collective-permute-start.40) | collective-permute-done | bytes 245792 | tf_op jit(solution)/shard_map/ppermute | solution.py:55
  197.9 5.3 shard_map.524
  209.2 11.9 %collective-permute-done.44.refs_3_ = bf16[192,3072]{1,0:T(8,128)(2,1)} collective-permute-done((bf16[192,3072]{1,0:T(8,128)(2,1)}, bf16[192,3072]{1,0:T(8,128)(2,1)}, u32[]{:S(2)}, u32[]{:S(2)}) %collective-permute-start.44) | collective-permute-done | bytes 1179680 | tf_op jit(solution)/shard_map/ppermute | solution.py:758
  226.5 12.3 %all-to-all-start.1 = ((bf16[32,24,768]{2,1,0:T(8,128)(2,1)}), bf16[32,24,768]{2,1,0:T(8,128)(2,1)}, u32[]{:S(2)}, u32[]{:S(2)}) async-start(bf16[32,24,768]{2,1,0:T(8,128)(2,1)} %bitcast.181), calls=%async_computation.1 | async-start | bytes 2359296 | tf_op jit(solution)/shard_map/all_to_all | solution.py:799
  242.4 6.4 %collective-permute-done.47.refs_2_ = bf16[192,3072]{1,0:T(8,128)(2,1)} collective-permute-done((bf16[192,3072]{1,0:T(8,128)(2,1)}, bf16[192,3072]{1,0:T(8,128)(2,1)}, u32[]{:S(2)}, u32[]{:S(2)}) %collective-permute-start.47) | collective-permute-done | bytes 1179680 | tf_op jit(solution)/shard_map/ppermute | solution.py:758
  260.1 5.8 all-to-all-done.1
  274.8 5.1 fusion.157
  286.0 11.0 %multiply_reduce_fusion = (f32[768]{0:T(1024)S(1)}, bf16[768,3072]{1,0:T(8,128)(2,1)}, bf16[768,3072]{1,0:T(8,128)(2,1)S(1)}) fusion(f32[768,3072]{1,0:T(8,128)S(1)} %fusion.157, f32[3072]{0:T(1024)S(1)} %copy-done.121, f32[768]{0:T(1024)S(1)} %multiply_reduce_fusion.15, bf16[768,768]{1,0:T(8,128)(2,1)} %bitcast.22, bf16[768,3072]{1,0:T(8,128)(2,1)S(1)} %shard_map.525), kind=kOutput, calls=%fused_computation.7 | convolution fusion | flops 3663985920 | bytes 24791040 | tf_op jit(solution)/shard_map/dot_general | solution.py:27
  306.3 6.6 %convolution_convert_fusion.1 = bf16[768,3072]{1,0:T(8,128)(2,1)S(1)} fusion(bf16[768,768]{1,0:T(8,128)(2,1)} %bitcast.24, bf16[768,3072]{1,0:T(8,128)(2,1)} %copy-done.66), kind=kOutput, calls=%fused_computation.19 | convolution fusion | flops 3626237952 | bytes 10616832 | tf_op jit(solution)/shard_map/dot_general | solution.py:27
  315.2 9.1 %convolution_convert_fusion = bf16[768,3072]{1,0:T(8,128)(2,1)} fusion(bf16[768,3072]{1,0:T(8,128)(2,1)} %get-tuple-element.202, bf16[768,768]{1,0:T(8,128)(2,1)} %bitcast.22, f32[768]{0:T(1024)S(1)} %multiply_reduce_fusion.15), kind=kOutput, calls=%fused_computation.18 | convolution fusion | flops 3628007424 | bytes 10619904 | tf_op jit(solution)/shard_map/dot_general | solution.py:27
  334.2 5.3 all-to-all-start.3
  350.5 11.1 %collective-permute-done.52.refs_2_ = bf16[192,3072]{1,0:T(8,128)(2,1)} collective-permute-done((bf16[192,3072]{1,0:T(8,128)(2,1)}, bf16[192,3072]{1,0:T(8,128)(2,1)}, u32[]{:S(2)}, u32[]{:S(2)}) %collective-permute-start.52) | collective-permute-done | bytes 1179680 | tf_op jit(solution)/shard_map/ppermute | solution.py:758
  367.2 9.4 %shard_map.527.dpacked = bf16[832,1152]{1,0:T(8,128)(2,1)S(1)} custom-call(s32[3]{0:T(128)S(1)} %pad_add_fusion.scalars, bf16[832,1152]{1,0:T(8,128)(2,1)S(1)} %copy-done.36, bf16[512,384]{1,0:T(8,128)(2,1)S(1)} %convolution_convert_fusion.9.grads, f32[512,384]{1,0:T(8,128)S(1)} %copy-done.40), custom_call_target="tpu_custom_call" | custom-call | flops 4000000000 | bytes 8000000 | tf_op jit(solution)/shard_map/pallas_call | solution.py:248
  378.4 13.5 %collective-permute-done.53.refs_3_ = bf16[192,3072]{1,0:T(8,128)(2,1)S(1)} collective-permute-done((bf16[192,3072]{1,0:T(8,128)(2,1)S(1)}, bf16[192,3072]{1,0:T(8,128)(2,1)S(1)}, u32[]{:S(2)}, u32[]{:S(2)}) %collective-permute-start.53) | collective-permute-done | bytes 1179680 | tf_op jit(solution)/shard_map/ppermute | solution.py:758
  400.2 5.4 collective-permute-done.54
  417.7 5.0 concatenate.109
  429.2 7.8 %collective-permute-done.56.refs_2_ = bf16[192,3072]{1,0:T(8,128)(2,1)} collective-permute-done((bf16[192,3072]{1,0:T(8,128)(2,1)}, bf16[192,3072]{1,0:T(8,128)(2,1)}, u32[]{:S(2)}, u32[]{:S(2)}) %collective-permute-start.56) | collective-permute-done | bytes 1179680 | tf_op jit(solution)/shard_map/ppermute | solution.py:758
  462.5 9.2 %shard_map.529.dpacked = bf16[832,1152]{1,0:T(8,128)(2,1)S(1)} custom-call(s32[3]{0:T(128)S(1)} %pad_add_fusion.scalars, bf16[832,1152]{1,0:T(8,128)(2,1)S(1)} %copy-done.34, bf16[512,384]{1,0:T(8,128)(2,1)S(1)} %convolution_convert_fusion.8.grads, f32[512,384]{1,0:T(8,128)S(1)} %copy-done.38), custom_call_target="tpu_custom_call" | custom-call | flops 4000000000 | bytes 8000000 | tf_op jit(solution)/shard_map/pallas_call | solution.py:248
  488.3 12.5 %collective-permute-done.63.refs_3_ = bf16[192,3072]{1,0:T(8,128)(2,1)} collective-permute-done((bf16[192,3072]{1,0:T(8,128)(2,1)}, bf16[192,3072]{1,0:T(8,128)(2,1)}, u32[]{:S(2)}, u32[]{:S(2)}) %collective-permute-start.63) | collective-permute-done | bytes 1179680 | tf_op jit(solution)/shard_map/ppermute | solution.py:758
  500.9 11.3 %collective-permute-done.59 = bf16[4,48,1536]{2,1,0:T(8,128)(2,1)} collective-permute-done((bf16[4,48,1536]{2,1,0:T(8,128)(2,1)}, bf16[4,48,1536]{2,1,0:T(8,128)(2,1)}, u32[]{:S(2)}, u32[]{:S(2)}) %collective-permute-start.59) | collective-permute-done | bytes 589856 | tf_op jit(solution)/shard_map/ppermute | solution.py:55
  520.3 5.4 collective-permute-done.67
  532.6 5.6 shard_map.531
  538.1 6.3 %shard_map.532 = f32[192,12288]{1,0:T(8,128)} custom-call(s32[1]{0:T(128)} %bitcast.7.place, bf16[192,3072]{1,0:T(8,128)(2,1)S(1)} %get-tuple-element.248.refs_0_, bf16[192,3072]{1,0:T(8,128)(2,1)} %collective-permute-done.71.refs_1_, bf16[192,3072]{1,0:T(8,128)(2,1)} %collective-permute-done.56.refs_2_, bf16[192,3072]{1,0:T(8,128)(2,1)} %collective-permute-done.63.refs_3_), custom_call_target="tpu_custom_call" | custom-call | bytes 14155776 | tf_op jit(solution)/shard_map/pallas_call | solution.py:520
  549.4 6.3 %collective-permute-done.72 = bf16[2,48,1664]{2,1,0:T(8,128)(2,1)S(1)} collective-permute-done((bf16[2,48,1664]{2,1,0:T(8,128)(2,1)S(1)}, bf16[2,48,1664]{2,1,0:T(8,128)(2,1)S(1)}, u32[]{:S(2)}, u32[]{:S(2)}) %collective-permute-start.72) | collective-permute-done | bytes 319520 | tf_op jit(solution)/shard_map/ppermute | solution.py:55
  582.7 16.6 %collective-permute-done.80 = bf16[48,3072]{1,0:T(8,128)(2,1)S(1)} collective-permute-done((bf16[48,3072]{1,0:T(8,128)(2,1)S(1)}, bf16[48,3072]{1,0:T(8,128)(2,1)S(1)}, u32[]{:S(2)}, u32[]{:S(2)}) %collective-permute-start.80) | collective-permute-done | bytes 294944 | tf_op jit(solution)/shard_map/ppermute | solution.py:419
  599.3 6.8 %collective-permute-done.81 = bf16[48,3072]{1,0:T(8,128)(2,1)S(1)} collective-permute-done((bf16[48,3072]{1,0:T(8,128)(2,1)S(1)}, bf16[48,3072]{1,0:T(8,128)(2,1)S(1)}, u32[]{:S(2)}, u32[]{:S(2)}) %collective-permute-start.81) | collective-permute-done | bytes 294944 | tf_op jit(solution)/shard_map/ppermute | solution.py:419
  (728 shorter events, 314.0 us)
Async XLA Ops:
  7.2 187.3 %all-gather.2.cloned.1.call-start = ((), (), s32[]{:S(2)}) async-start(), calls=%async_computation.4 | async-start | bytes 2506752 | tf_op jit(solution)/shard_map/all_gather | solution.py:727
  10.8 36.1 %collective-permute-start = (bf16[256,768]{1,0:T(8,128)(2,1)}, bf16[256,768]{1,0:T(8,128)(2,1)S(1)}, u32[]{:S(2)}, u32[]{:S(2)}) collective-permute-start(bf16[256,768]{1,0:T(8,128)(2,1)} %param.31), channel_id=1, source_target_pairs={{0,1},{1,0},{2,3},{3,2},{4,5},{5,4},{6,7},{7,6},{8,9},{9,8},{10,11... | collective-permute-start | bytes 1179656 | tf_op jit(solution)/shard_map/ppermute | solution.py:51
  57.8 29.1 %collective-permute-start.23 = (bf16[48,3072]{1,0:T(8,128)(2,1)S(1)}, bf16[48,3072]{1,0:T(8,128)(2,1)S(1)}, u32[]{:S(2)}, u32[]{:S(2)}) collective-permute-start(bf16[48,3072]{1,0:T(8,128)(2,1)S(1)} %pad_maximum_fusion.17.refs_0_), channel_id=1, source_target_pairs={{0,2},{2,0},{1,3},{3,1},{4,6},{6,4},{5,7},{7,5},{8,10},{10,8},{9,1... | collective-permute-start | bytes 884744 | tf_op jit(solution)/shard_map/ppermute | solution.py:55
  58.8 33.1 %collective-permute-start.24 = (bf16[48,3072]{1,0:T(8,128)(2,1)S(1)}, bf16[48,3072]{1,0:T(8,128)(2,1)S(1)}, u32[]{:S(2)}, u32[]{:S(2)}) collective-permute-start(bf16[48,3072]{1,0:T(8,128)(2,1)S(1)} %pad_maximum_fusion.17.refs_0_), channel_id=1, source_target_pairs={{0,4},{4,0},{1,5},{5,1},{2,6},{6,2},{3,7},{7,3},{8,12},{12,8},{9,1... | collective-permute-start | bytes 884744 | tf_op jit(solution)/shard_map/ppermute | solution.py:361
  58.8 29.6 %collective-permute-start.26 = (bf16[48,3072]{1,0:T(8,128)(2,1)S(1)}, bf16[48,3072]{1,0:T(8,128)(2,1)S(1)}, u32[]{:S(2)}, u32[]{:S(2)}) collective-permute-start(bf16[48,3072]{1,0:T(8,128)(2,1)S(1)} %pad_maximum_fusion.17.refs_0_), channel_id=1, source_target_pairs={{0,8},{8,0},{16,24},{24,16},{1,9},{9,1},{17,25},{25,17},{2,10},{10... | collective-permute-start | bytes 884744 | tf_op jit(solution)/shard_map/ppermute | solution.py:355
  64.8 28.2 %collective-permute-start.30 = (bf16[48,3072]{1,0:T(8,128)(2,1)S(1)}, bf16[48,3072]{1,0:T(8,128)(2,1)}, u32[]{:S(2)}, u32[]{:S(2)}) collective-permute-start(bf16[48,3072]{1,0:T(8,128)(2,1)S(1)} %pad_maximum_fusion.17.refs_0_), channel_id=1, source_target_pairs={{0,16},{8,24},{16,0},{24,8},{1,17},{9,25},{17,1},{25,9},{2,18},{10... | collective-permute-start | bytes 884744 | tf_op jit(solution)/shard_map/ppermute | solution.py:355
  111.6 26.1 %collective-permute-start.20 = (bf16[768,384]{1,0:T(8,128)(2,1)S(1)}, bf16[768,384]{1,0:T(8,128)(2,1)S(1)}, u32[]{:S(2)}, u32[]{:S(2)}) collective-permute-start(bf16[768,384]{1,0:T(8,128)(2,1)S(1)} %get-tuple-element.162), channel_id=1, source_target_pairs={{0,1},{1,0},{2,3},{3,2},{4,5},{5,4},{6,7},{7,6},{8,9},{9,8},{10,11... | collective-permute-start | bytes 1769480 | tf_op jit(solution)/shard_map/ppermute | solution.py:51
  147.1 44.4 %collective-permute-start.42 = (bf16[192,3072]{1,0:T(8,128)(2,1)}, bf16[192,3072]{1,0:T(8,128)(2,1)S(1)}, u32[]{:S(2)}, u32[]{:S(2)}) collective-permute-start(bf16[192,3072]{1,0:T(8,128)(2,1)} %get-tuple-element.174), channel_id=1, source_target_pairs={{0,2},{1,3},{2,0},{3,1},{4,6},{5,7},{6,4},{7,5},{8,10},{9,11},{10,... | collective-permute-start | bytes 3538952 | tf_op jit(solution)/shard_map/ppermute | solution.py:758
  151.2 38.0 %collective-permute-start.40 = (bf16[160,768]{1,0:T(8,128)(2,1)}, bf16[160,768]{1,0:T(8,128)(2,1)}, u32[]{:S(2)}, u32[]{:S(2)}) collective-permute-start(bf16[160,768]{1,0:T(8,128)(2,1)} %constant_dynamic-slice_fusion.12), channel_id=1, source_target_pairs={{0,2},{2,0},{1,3},{3,1},{4,6},{6,4},{5,7},{7,5},{8,10},{10,8},{9,1... | collective-permute-start | bytes 737288 | tf_op jit(solution)/shard_map/ppermute | solution.py:55
  153.9 55.4 %all-to-all-start = ((bf16[32,24,768]{2,1,0:T(8,128)(2,1)}), bf16[32,24,768]{2,1,0:T(8,128)(2,1)}, u32[]{:S(2)}, u32[]{:S(2)}) async-start(bf16[32,24,768]{2,1,0:T(8,128)(2,1)} %bitcast.173), calls=%async_computation | async-start | bytes 2359296 | tf_op jit(solution)/shard_map/all_to_all | solution.py:799
  192.6 28.5 %collective-permute-start.44 = (bf16[192,3072]{1,0:T(8,128)(2,1)}, bf16[192,3072]{1,0:T(8,128)(2,1)}, u32[]{:S(2)}, u32[]{:S(2)}) collective-permute-start(bf16[192,3072]{1,0:T(8,128)(2,1)} %copy-done.32), channel_id=1, source_target_pairs={{0,3},{1,2},{2,1},{3,0},{4,7},{5,6},{6,5},{7,4},{8,11},{9,10},{10,... | collective-permute-start | bytes 3538952 | tf_op jit(solution)/shard_map/ppermute | solution.py:758
  207.7 41.1 %collective-permute-start.47 = (bf16[192,3072]{1,0:T(8,128)(2,1)}, bf16[192,3072]{1,0:T(8,128)(2,1)}, u32[]{:S(2)}, u32[]{:S(2)}) collective-permute-start(bf16[192,3072]{1,0:T(8,128)(2,1)} %copy-done.31), channel_id=1, source_target_pairs={{0,2},{1,3},{2,0},{3,1},{4,6},{5,7},{6,4},{7,5},{8,10},{9,11},{10,... | collective-permute-start | bytes 3538952 | tf_op jit(solution)/shard_map/ppermute | solution.py:758
  208.3 44.2 %collective-permute-start.60 = (bf16[512,1536]{1,0:T(8,128)(2,1)}, bf16[512,1536]{1,0:T(8,128)(2,1)}, u32[]{:S(2)}, u32[]{:S(2)}) collective-permute-start(bf16[512,1536]{1,0:T(8,128)(2,1)} %copy-done.75), channel_id=1, source_target_pairs={{0,1},{1,0},{2,3},{3,2},{4,5},{5,4},{6,7},{7,6},{8,9},{9,8},{10,11... | collective-permute-start | bytes 4718600 | tf_op jit(solution)/shard_map/ppermute | solution.py:51
  226.5 39.4 %all-to-all-start.1 = ((bf16[32,24,768]{2,1,0:T(8,128)(2,1)}), bf16[32,24,768]{2,1,0:T(8,128)(2,1)}, u32[]{:S(2)}, u32[]{:S(2)}) async-start(bf16[32,24,768]{2,1,0:T(8,128)(2,1)} %bitcast.181), calls=%async_computation.1 | async-start | bytes 2359296 | tf_op jit(solution)/shard_map/all_to_all | solution.py:799
  240.8 39.2 %collective-permute-start.48 = (bf16[192,3072]{1,0:T(8,128)(2,1)}, bf16[192,3072]{1,0:T(8,128)(2,1)}, u32[]{:S(2)}, u32[]{:S(2)}) collective-permute-start(bf16[192,3072]{1,0:T(8,128)(2,1)} %get-tuple-element.192), channel_id=1, source_target_pairs={{0,1},{1,0},{2,3},{3,2},{4,5},{5,4},{6,7},{7,6},{8,9},{9,8},{10,11... | collective-permute-start | bytes 3538952 | tf_op jit(solution)/shard_map/ppermute | solution.py:758
  248.8 34.8 %collective-permute-start.49 = (bf16[192,3072]{1,0:T(8,128)(2,1)}, bf16[192,3072]{1,0:T(8,128)(2,1)}, u32[]{:S(2)}, u32[]{:S(2)}) collective-permute-start(bf16[192,3072]{1,0:T(8,128)(2,1)} %get-tuple-element.195), channel_id=1, source_target_pairs={{0,3},{1,2},{2,1},{3,0},{4,7},{5,6},{6,5},{7,4},{8,11},{9,10},{10,... | collective-permute-start | bytes 3538952 | tf_op jit(solution)/shard_map/ppermute | solution.py:758
  302.8 31.4 %all-to-all-start.2 = ((bf16[32,24,768]{2,1,0:T(8,128)(2,1)}), bf16[32,24,768]{2,1,0:T(8,128)(2,1)}, u32[]{:S(2)}, u32[]{:S(2)}) async-start(bf16[32,24,768]{2,1,0:T(8,128)(2,1)} %bitcast.26), calls=%async_computation.2 | async-start | bytes 2359296 | tf_op jit(solution)/shard_map/all_to_all | solution.py:803
  324.2 37.3 %collective-permute-start.52 = (bf16[192,3072]{1,0:T(8,128)(2,1)}, bf16[192,3072]{1,0:T(8,128)(2,1)}, u32[]{:S(2)}, u32[]{:S(2)}) collective-permute-start(bf16[192,3072]{1,0:T(8,128)(2,1)} %get-tuple-element.326), channel_id=1, source_target_pairs={{0,2},{1,3},{2,0},{3,1},{4,6},{5,7},{6,4},{7,5},{8,10},{9,11},{10,... | collective-permute-start | bytes 3538952 | tf_op jit(solution)/shard_map/ppermute | solution.py:758
  334.2 120.9 %all-to-all-start.3 = ((bf16[32,24,768]{2,1,0:T(8,128)(2,1)}), bf16[32,24,768]{2,1,0:T(8,128)(2,1)}, u32[]{:S(2)}, u32[]{:S(2)}) async-start(bf16[32,24,768]{2,1,0:T(8,128)(2,1)} %bitcast.180), calls=%async_computation.3 | async-start | bytes 2359296 | tf_op jit(solution)/shard_map/all_to_all | solution.py:803
  361.6 30.3 %collective-permute-start.53 = (bf16[192,3072]{1,0:T(8,128)(2,1)S(1)}, bf16[192,3072]{1,0:T(8,128)(2,1)S(1)}, u32[]{:S(2)}, u32[]{:S(2)}) collective-permute-start(bf16[192,3072]{1,0:T(8,128)(2,1)S(1)} %copy-done.82), channel_id=1, source_target_pairs={{0,3},{1,2},{2,1},{3,0},{4,7},{5,6},{6,5},{7,4},{8,11},{9,10},{10,... | collective-permute-start | bytes 3538952 | tf_op jit(solution)/shard_map/ppermute | solution.py:758
  398.6 56.5 %collective-permute-start.58 = (bf16[4,2,48,1536]{3,2,1,0:T(8,128)(2,1)}, bf16[4,2,48,1536]{3,2,1,0:T(8,128)(2,1)}, u32[]{:S(2)}, u32[]{:S(2)}) collective-permute-start(bf16[4,2,48,1536]{3,2,1,0:T(8,128)(2,1)} %get-tuple-element.342), channel_id=1, source_target_pairs={{0,4},{4,0},{1,5},{5,1},{2,6},{6,2},{3,7},{7,3},{8,12},{12,8},{9,1... | collective-permute-start | bytes 3538952 | tf_op jit(solution)/shard_map/ppermute | solution.py:436
  409.1 27.9 %collective-permute-start.56 = (bf16[192,3072]{1,0:T(8,128)(2,1)}, bf16[192,3072]{1,0:T(8,128)(2,1)}, u32[]{:S(2)}, u32[]{:S(2)}) collective-permute-start(bf16[192,3072]{1,0:T(8,128)(2,1)} %get-tuple-element.323), channel_id=1, source_target_pairs={{0,2},{1,3},{2,0},{3,1},{4,6},{5,7},{6,4},{7,5},{8,10},{9,11},{10,... | collective-permute-start | bytes 3538952 | tf_op jit(solution)/shard_map/ppermute | solution.py:758
  409.7 108.8 %collective-permute-start.71 = (bf16[192,3072]{1,0:T(8,128)(2,1)}, bf16[192,3072]{1,0:T(8,128)(2,1)}, u32[]{:S(2)}, u32[]{:S(2)}) collective-permute-start(bf16[192,3072]{1,0:T(8,128)(2,1)} %get-tuple-element.320), channel_id=1, source_target_pairs={{0,1},{1,0},{2,3},{3,2},{4,5},{5,4},{6,7},{7,6},{8,9},{9,8},{10,11... | collective-permute-start | bytes 3538952 | tf_op jit(solution)/shard_map/ppermute | solution.py:758
  443.7 43.7 %collective-permute-start.61 = (bf16[2,2,48,3072]{3,2,1,0:T(8,128)(2,1)}, bf16[2,2,48,3072]{3,2,1,0:T(8,128)(2,1)}, u32[]{:S(2)}, u32[]{:S(2)}) collective-permute-start(bf16[2,2,48,3072]{3,2,1,0:T(8,128)(2,1)} %get-tuple-element.330), channel_id=1, source_target_pairs={{0,4},{4,0},{1,5},{5,1},{2,6},{6,2},{3,7},{7,3},{8,12},{12,8},{9,1... | collective-permute-start | bytes 3538952 | tf_op jit(solution)/shard_map/ppermute | solution.py:400
  446.6 40.9 %collective-permute-start.62 = (bf16[2,2,48,3072]{3,2,1,0:T(8,128)(2,1)}, bf16[2,2,48,3072]{3,2,1,0:T(8,128)(2,1)}, u32[]{:S(2)}, u32[]{:S(2)}) collective-permute-start(bf16[2,2,48,3072]{3,2,1,0:T(8,128)(2,1)} %get-tuple-element.328), channel_id=1, source_target_pairs={{0,2},{2,0},{1,3},{3,1},{4,6},{6,4},{5,7},{7,5},{8,10},{10,8},{9,1... | collective-permute-start | bytes 3538952 | tf_op jit(solution)/shard_map/ppermute | solution.py:55
  448.3 52.6 %collective-permute-start.63 = (bf16[192,3072]{1,0:T(8,128)(2,1)}, bf16[192,3072]{1,0:T(8,128)(2,1)}, u32[]{:S(2)}, u32[]{:S(2)}) collective-permute-start(bf16[192,3072]{1,0:T(8,128)(2,1)} %get-tuple-element.215), channel_id=1, source_target_pairs={{0,3},{1,2},{2,1},{3,0},{4,7},{5,6},{6,5},{7,4},{8,11},{9,10},{10,... | collective-permute-start | bytes 3538952 | tf_op jit(solution)/shard_map/ppermute | solution.py:758
  461.3 50.8 %collective-permute-start.59 = (bf16[4,48,1536]{2,1,0:T(8,128)(2,1)}, bf16[4,48,1536]{2,1,0:T(8,128)(2,1)}, u32[]{:S(2)}, u32[]{:S(2)}) collective-permute-start(bf16[4,48,1536]{2,1,0:T(8,128)(2,1)} %get-tuple-element.350), channel_id=1, source_target_pairs={{0,2},{2,0},{1,3},{3,1},{4,6},{6,4},{5,7},{7,5},{8,10},{10,8},{9,1... | collective-permute-start | bytes 1769480 | tf_op jit(solution)/shard_map/ppermute | solution.py:55
  487.4 31.7 %collective-permute-start.66 = (bf16[2,2,48,1664]{3,2,1,0:T(8,128)(2,1)S(1)}, bf16[2,2,48,1664]{3,2,1,0:T(8,128)(2,1)S(1)}, u32[]{:S(2)}, u32[]{:S(2)}) collective-permute-start(bf16[2,2,48,1664]{3,2,1,0:T(8,128)(2,1)S(1)} %get-tuple-element.340), channel_id=1, source_target_pairs={{0,4},{4,0},{1,5},{5,1},{2,6},{6,2},{3,7},{7,3},{8,12},{12,8},{9,1... | collective-permute-start | bytes 1916936 | tf_op jit(solution)/shard_map/ppermute | solution.py:400
  487.6 38.1 %collective-permute-start.67 = (bf16[2,2,48,1664]{3,2,1,0:T(8,128)(2,1)S(1)}, bf16[2,2,48,1664]{3,2,1,0:T(8,128)(2,1)S(1)}, u32[]{:S(2)}, u32[]{:S(2)}) collective-permute-start(bf16[2,2,48,1664]{3,2,1,0:T(8,128)(2,1)S(1)} %get-tuple-element.338), channel_id=1, source_target_pairs={{0,2},{2,0},{1,3},{3,1},{4,6},{6,4},{5,7},{7,5},{8,10},{10,8},{9,1... | collective-permute-start | bytes 1916936 | tf_op jit(solution)/shard_map/ppermute | solution.py:55
  525.7 30.0 %collective-permute-start.74 = (bf16[2,48,3072]{2,1,0:T(8,128)(2,1)S(1)}, bf16[2,48,3072]{2,1,0:T(8,128)(2,1)S(1)}, u32[]{:S(2)}, u32[]{:S(2)}) collective-permute-start(bf16[2,48,3072]{2,1,0:T(8,128)(2,1)S(1)} %get-tuple-element.348), channel_id=1, source_target_pairs={{0,2},{2,0},{1,3},{3,1},{4,6},{6,4},{5,7},{7,5},{8,10},{10,8},{9,1... | collective-permute-start | bytes 1769480 | tf_op jit(solution)/shard_map/ppermute | solution.py:55
  526.9 28.9 %collective-permute-start.75 = (bf16[2,48,3072]{2,1,0:T(8,128)(2,1)S(1)}, bf16[2,48,3072]{2,1,0:T(8,128)(2,1)S(1)}, u32[]{:S(2)}, u32[]{:S(2)}) collective-permute-start(bf16[2,48,3072]{2,1,0:T(8,128)(2,1)S(1)} %get-tuple-element.346), channel_id=1, source_target_pairs={{0,4},{4,0},{1,5},{5,1},{2,6},{6,2},{3,7},{7,3},{8,12},{12,8},{9,1... | collective-permute-start | bytes 1769480 | tf_op jit(solution)/shard_map/ppermute | solution.py:409
  529.5 26.2 %collective-permute-start.72 = (bf16[2,48,1664]{2,1,0:T(8,128)(2,1)S(1)}, bf16[2,48,1664]{2,1,0:T(8,128)(2,1)S(1)}, u32[]{:S(2)}, u32[]{:S(2)}) collective-permute-start(bf16[2,48,1664]{2,1,0:T(8,128)(2,1)S(1)} %get-tuple-element.366), channel_id=1, source_target_pairs={{0,2},{2,0},{1,3},{3,1},{4,6},{6,4},{5,7},{7,5},{8,10},{10,8},{9,1... | collective-permute-start | bytes 958472 | tf_op jit(solution)/shard_map/ppermute | solution.py:55
  (217 other events, 2122.7 us)
Sparse Core Ops, SparseCore 0:
  32.6 71.6 all-gather.1

commit v4 on v3

--- a/solution.py
+++ b/solution.py
@@ -956,7 +956,7 @@
     dx1, third, returned = tie(dx1, third, returned)
     third = scatter_x(third)
 
-    dx0, lower_grads, lower_sums, _, (third, second, shrink_pieces[3]) = attention_backward(
+    dx0, lower_grads, lower_sums, _, (third, second) = attention_backward(
         dx1,
         x0,
         a1,
@@ -966,7 +966,7 @@
         ln1_gain,
         lower_project_c,
         lower_merge_full,
-        (third, second, shrink_pieces[3]),
+        (third, second),
     )
     second = pairs_second(second)
     third = scatter_z(third)

time: 633 us -> 633 us (level)
    ppermute x12, waiting for transfers between devices: 66.9 us -> 54.7 us  [between(): return lax.ppermute(values, ('x', 'c'), xor_pairs(4, k))]
    ppermute x21, waiting for transfers between devices: 71.9 us -> 82 us  [swap_chips(): return lax.ppermute(values, 'x', SWAP)]
where the time goes in v4:
time: 633 us; the launch traced here: 622 us
  waiting for transfers between devices  222 us (35%)
  starting transfers between devices  105 us (17%)
  matrix products  93.6 us (15%)
  local copies, waits for them, and re-layouts  71.4 us (11%)
  Pallas kernels  60.7 us (10%)
  other arithmetic  50.9 us (8%)
  between operations  18.5 us (3%)
    dot_general x41, matrix products, dot(): lax.dot_general(left, right, ((dims[0], dims[1]), ((), ())), preferred_el...  93.6 us
    ppermute x21, waiting for transfers between devices, swap_chips(): return lax.ppermute(values, 'x', SWAP)  82 us
    ppermute x12, waiting for transfers between devices, between(): return lax.ppermute(values, ('x', 'c'), xor_pairs(4, k))  54.7 us
    unnamed x312, local copies, waits for them, and re-layouts  32.7 us
    pallas_call x4, Pallas kernels, kernel_call(): pl.pallas_call(body, out_shape=outs, in_specs=[pl.BlockSpec(memory_space=...  29.4 us
    ppermute x6, waiting for transfers between devices, gather_z(): lax.ppermute(pair, 'z', xor_pairs(4, k))  26.5 us
    ppermute x6, waiting for transfers between devices, pairs_z(): lax.ppermute(piece, 'z', xor_pairs(4, k + 1))  23.3 us
    ppermute x21, starting transfers between devices, swap_cores(): return lax.ppermute(values, 'c', SWAP)  21.1 us
  transfers between devices with their start and end apart: 96, of which 34 were waited for; matrix products, arithmetic and copies ran while one was open for 26% of the time, Pallas kernels for 9%

profile of v4, /device:TPU:9, one launch (start us, length us, event | category | flops | bytes accessed | tf_op | source)
XLA Modules:
  0.0 622.3 jit_solution(7275731536485522963)
XLA Ops:
  38.5 7.9 %collective-permute-done.15.refs_12_ = bf16[48,1664]{1,0:T(8,128)(2,1)S(1)} collective-permute-done((bf16[48,1664]{1,0:T(8,128)(2,1)S(1)}, bf16[48,1664]{1,0:T(8,128)(2,1)S(1)}, u32[]{:S(2)}, u32[]{:S(2)}) %collective-permute-start.15) | collective-permute-done | bytes 159776 | tf_op jit(solution)/shard_map/ppermute | solution.py:355
  58.7 6.0 collective-permute-done.18.refs_15_
  71.6 4.9 collective-permute-start.2
  93.2 15.7 %collective-permute-done.34.refs_12_ = bf16[48,3072]{1,0:T(8,128)(2,1)S(1)} collective-permute-done((bf16[48,3072]{1,0:T(8,128)(2,1)S(1)}, bf16[48,3072]{1,0:T(8,128)(2,1)S(1)}, u32[]{:S(2)}, u32[]{:S(2)}) %collective-permute-start.34) | collective-permute-done | bytes 294944 | tf_op jit(solution)/shard_map/ppermute | solution.py:355
  117.2 6.3 %collective-permute-done.36.refs_14_ = bf16[48,3072]{1,0:T(8,128)(2,1)S(1)} collective-permute-done((bf16[48,3072]{1,0:T(8,128)(2,1)S(1)}, bf16[48,3072]{1,0:T(8,128)(2,1)S(1)}, u32[]{:S(2)}, u32[]{:S(2)}) %collective-permute-start.36) | collective-permute-done | bytes 294944 | tf_op jit(solution)/shard_map/ppermute | solution.py:361
  127.0 5.5 shard_map.522
  157.2 32.2 %collective-permute-done.40 = bf16[160,768]{1,0:T(8,128)(2,1)} collective-permute-done((bf16[160,768]{1,0:T(8,128)(2,1)}, bf16[160,768]{1,0:T(8,128)(2,1)}, u32[]{:S(2)}, u32[]{:S(2)}) %collective-permute-start.40) | collective-permute-done | bytes 245792 | tf_op jit(solution)/shard_map/ppermute | solution.py:55
  197.9 5.3 shard_map.524
  209.3 11.9 %collective-permute-done.44.refs_3_ = bf16[192,3072]{1,0:T(8,128)(2,1)} collective-permute-done((bf16[192,3072]{1,0:T(8,128)(2,1)}, bf16[192,3072]{1,0:T(8,128)(2,1)}, u32[]{:S(2)}, u32[]{:S(2)}) %collective-permute-start.44) | collective-permute-done | bytes 1179680 | tf_op jit(solution)/shard_map/ppermute | solution.py:758
  226.5 12.3 %all-to-all-start.1 = ((bf16[32,24,768]{2,1,0:T(8,128)(2,1)}), bf16[32,24,768]{2,1,0:T(8,128)(2,1)}, u32[]{:S(2)}, u32[]{:S(2)}) async-start(bf16[32,24,768]{2,1,0:T(8,128)(2,1)} %bitcast.181), calls=%async_computation.1 | async-start | bytes 2359296 | tf_op jit(solution)/shard_map/all_to_all | solution.py:799
  242.4 6.6 %collective-permute-done.47.refs_2_ = bf16[192,3072]{1,0:T(8,128)(2,1)} collective-permute-done((bf16[192,3072]{1,0:T(8,128)(2,1)}, bf16[192,3072]{1,0:T(8,128)(2,1)}, u32[]{:S(2)}, u32[]{:S(2)}) %collective-permute-start.47) | collective-permute-done | bytes 1179680 | tf_op jit(solution)/shard_map/ppermute | solution.py:758
  260.0 5.9 all-to-all-done.1
  274.8 5.1 fusion.157
  286.0 11.0 %multiply_reduce_fusion = (f32[768]{0:T(1024)S(1)}, bf16[768,3072]{1,0:T(8,128)(2,1)}, bf16[768,3072]{1,0:T(8,128)(2,1)S(1)}) fusion(f32[768,3072]{1,0:T(8,128)S(1)} %fusion.157, f32[3072]{0:T(1024)S(1)} %copy-done.121, f32[768]{0:T(1024)S(1)} %multiply_reduce_fusion.15, bf16[768,768]{1,0:T(8,128)(2,1)} %bitcast.22, bf16[768,3072]{1,0:T(8,128)(2,1)S(1)} %shard_map.525), kind=kOutput, calls=%fused_computation.7 | convolution fusion | flops 3663985920 | bytes 24791040 | tf_op jit(solution)/shard_map/dot_general | solution.py:27
  298.0 4.9 add_convert_fusion.4
  306.3 6.6 %convolution_convert_fusion.1 = bf16[768,3072]{1,0:T(8,128)(2,1)S(1)} fusion(bf16[768,768]{1,0:T(8,128)(2,1)} %bitcast.24, bf16[768,3072]{1,0:T(8,128)(2,1)} %copy-done.66), kind=kOutput, calls=%fused_computation.19 | convolution fusion | flops 3626237952 | bytes 10616832 | tf_op jit(solution)/shard_map/dot_general | solution.py:27
  315.2 9.1 %convolution_convert_fusion = bf16[768,3072]{1,0:T(8,128)(2,1)} fusion(bf16[768,3072]{1,0:T(8,128)(2,1)} %get-tuple-element.201, bf16[768,768]{1,0:T(8,128)(2,1)} %bitcast.22, f32[768]{0:T(1024)S(1)} %multiply_reduce_fusion.15), kind=kOutput, calls=%fused_computation.18 | convolution fusion | flops 3628007424 | bytes 10619904 | tf_op jit(solution)/shard_map/dot_general | solution.py:27
  327.2 4.9 convolution_convert_fusion.4
  334.2 5.3 all-to-all-start.3
  350.5 11.1 %collective-permute-done.52.refs_2_ = bf16[192,3072]{1,0:T(8,128)(2,1)} collective-permute-done((bf16[192,3072]{1,0:T(8,128)(2,1)}, bf16[192,3072]{1,0:T(8,128)(2,1)}, u32[]{:S(2)}, u32[]{:S(2)}) %collective-permute-start.52) | collective-permute-done | bytes 1179680 | tf_op jit(solution)/shard_map/ppermute | solution.py:758
  367.1 9.4 %shard_map.527.dpacked = bf16[832,1152]{1,0:T(8,128)(2,1)S(1)} custom-call(s32[3]{0:T(128)S(1)} %pad_add_fusion.scalars, bf16[832,1152]{1,0:T(8,128)(2,1)S(1)} %copy-done.36, bf16[512,384]{1,0:T(8,128)(2,1)S(1)} %convolution_convert_fusion.9.grads, f32[512,384]{1,0:T(8,128)S(1)} %copy-done.40), custom_call_target="tpu_custom_call" | custom-call | flops 4000000000 | bytes 8000000 | tf_op jit(solution)/shard_map/pallas_call | solution.py:248
  378.4 13.5 %collective-permute-done.53.refs_3_ = bf16[192,3072]{1,0:T(8,128)(2,1)S(1)} collective-permute-done((bf16[192,3072]{1,0:T(8,128)(2,1)S(1)}, bf16[192,3072]{1,0:T(8,128)(2,1)S(1)}, u32[]{:S(2)}, u32[]{:S(2)}) %collective-permute-start.53) | collective-permute-done | bytes 1179680 | tf_op jit(solution)/shard_map/ppermute | solution.py:758
  400.1 5.5 collective-permute-done.54
  417.8 5.0 concatenate.109
  429.3 7.9 %collective-permute-done.56.refs_2_ = bf16[192,3072]{1,0:T(8,128)(2,1)} collective-permute-done((bf16[192,3072]{1,0:T(8,128)(2,1)}, bf16[192,3072]{1,0:T(8,128)(2,1)}, u32[]{:S(2)}, u32[]{:S(2)}) %collective-permute-start.56) | collective-permute-done | bytes 1179680 | tf_op jit(solution)/shard_map/ppermute | solution.py:758
  462.5 9.2 %shard_map.529.dpacked = bf16[832,1152]{1,0:T(8,128)(2,1)S(1)} custom-call(s32[3]{0:T(128)S(1)} %pad_add_fusion.scalars, bf16[832,1152]{1,0:T(8,128)(2,1)S(1)} %copy-done.34, bf16[512,384]{1,0:T(8,128)(2,1)S(1)} %convolution_convert_fusion.8.grads, f32[512,384]{1,0:T(8,128)S(1)} %copy-done.38), custom_call_target="tpu_custom_call" | custom-call | flops 4000000000 | bytes 8000000 | tf_op jit(solution)/shard_map/pallas_call | solution.py:248
  488.4 23.9 %collective-permute-done.59 = bf16[4,48,1536]{2,1,0:T(8,128)(2,1)} collective-permute-done((bf16[4,48,1536]{2,1,0:T(8,128)(2,1)}, bf16[4,48,1536]{2,1,0:T(8,128)(2,1)}, u32[]{:S(2)}, u32[]{:S(2)}) %collective-permute-start.59) | collective-permute-done | bytes 589856 | tf_op jit(solution)/shard_map/ppermute | solution.py:55
  520.3 5.5 collective-permute-done.66
  535.3 5.6 shard_map.531
  540.9 6.3 %shard_map.532 = f32[192,12288]{1,0:T(8,128)} custom-call(s32[1]{0:T(128)} %bitcast.7.place, bf16[192,3072]{1,0:T(8,128)(2,1)S(1)} %get-tuple-element.246.refs_0_, bf16[192,3072]{1,0:T(8,128)(2,1)} %collective-permute-done.70.refs_1_, bf16[192,3072]{1,0:T(8,128)(2,1)} %collective-permute-done.56.refs_2_, bf16[192,3072]{1,0:T(8,128)(2,1)} %collective-permute-done.71.refs_3_), custom_call_target="tpu_custom_call" | custom-call | bytes 14155776 | tf_op jit(solution)/shard_map/pallas_call | solution.py:520
  582.8 16.4 %collective-permute-done.80 = bf16[48,3072]{1,0:T(8,128)(2,1)S(1)} collective-permute-done((bf16[48,3072]{1,0:T(8,128)(2,1)S(1)}, bf16[48,3072]{1,0:T(8,128)(2,1)S(1)}, u32[]{:S(2)}, u32[]{:S(2)}) %collective-permute-start.80) | collective-permute-done | bytes 294944 | tf_op jit(solution)/shard_map/ppermute | solution.py:419
  599.3 6.9 %collective-permute-done.81 = bf16[48,3072]{1,0:T(8,128)(2,1)S(1)} collective-permute-done((bf16[48,3072]{1,0:T(8,128)(2,1)S(1)}, bf16[48,3072]{1,0:T(8,128)(2,1)S(1)}, u32[]{:S(2)}, u32[]{:S(2)}) %collective-permute-start.81) | collective-permute-done | bytes 294944 | tf_op jit(solution)/shard_map/ppermute | solution.py:419
  (728 shorter events, 310.4 us)
Async XLA Ops:
  7.2 187.3 %all-gather.2.cloned.1.call-start = ((), (), s32[]{:S(2)}) async-start(), calls=%async_computation.4 | async-start | bytes 2506752 | tf_op jit(solution)/shard_map/all_gather | solution.py:727
  10.8 36.1 %collective-permute-start = (bf16[256,768]{1,0:T(8,128)(2,1)}, bf16[256,768]{1,0:T(8,128)(2,1)S(1)}, u32[]{:S(2)}, u32[]{:S(2)}) collective-permute-start(bf16[256,768]{1,0:T(8,128)(2,1)} %param.31), channel_id=1, source_target_pairs={{0,1},{1,0},{2,3},{3,2},{4,5},{5,4},{6,7},{7,6},{8,9},{9,8},{10,11... | collective-permute-start | bytes 1179656 | tf_op jit(solution)/shard_map/ppermute | solution.py:51
  57.7 29.1 %collective-permute-start.23 = (bf16[48,3072]{1,0:T(8,128)(2,1)S(1)}, bf16[48,3072]{1,0:T(8,128)(2,1)S(1)}, u32[]{:S(2)}, u32[]{:S(2)}) collective-permute-start(bf16[48,3072]{1,0:T(8,128)(2,1)S(1)} %pad_maximum_fusion.17.refs_0_), channel_id=1, source_target_pairs={{0,2},{2,0},{1,3},{3,1},{4,6},{6,4},{5,7},{7,5},{8,10},{10,8},{9,1... | collective-permute-start | bytes 884744 | tf_op jit(solution)/shard_map/ppermute | solution.py:55
  58.7 33.1 %collective-permute-start.24 = (bf16[48,3072]{1,0:T(8,128)(2,1)S(1)}, bf16[48,3072]{1,0:T(8,128)(2,1)S(1)}, u32[]{:S(2)}, u32[]{:S(2)}) collective-permute-start(bf16[48,3072]{1,0:T(8,128)(2,1)S(1)} %pad_maximum_fusion.17.refs_0_), channel_id=1, source_target_pairs={{0,4},{4,0},{1,5},{5,1},{2,6},{6,2},{3,7},{7,3},{8,12},{12,8},{9,1... | collective-permute-start | bytes 884744 | tf_op jit(solution)/shard_map/ppermute | solution.py:361
  58.7 29.6 %collective-permute-start.26 = (bf16[48,3072]{1,0:T(8,128)(2,1)S(1)}, bf16[48,3072]{1,0:T(8,128)(2,1)S(1)}, u32[]{:S(2)}, u32[]{:S(2)}) collective-permute-start(bf16[48,3072]{1,0:T(8,128)(2,1)S(1)} %pad_maximum_fusion.17.refs_0_), channel_id=1, source_target_pairs={{0,8},{8,0},{16,24},{24,16},{1,9},{9,1},{17,25},{25,17},{2,10},{10... | collective-permute-start | bytes 884744 | tf_op jit(solution)/shard_map/ppermute | solution.py:355
  64.8 28.2 %collective-permute-start.30 = (bf16[48,3072]{1,0:T(8,128)(2,1)S(1)}, bf16[48,3072]{1,0:T(8,128)(2,1)}, u32[]{:S(2)}, u32[]{:S(2)}) collective-permute-start(bf16[48,3072]{1,0:T(8,128)(2,1)S(1)} %pad_maximum_fusion.17.refs_0_), channel_id=1, source_target_pairs={{0,16},{8,24},{16,0},{24,8},{1,17},{9,25},{17,1},{25,9},{2,18},{10... | collective-permute-start | bytes 884744 | tf_op jit(solution)/shard_map/ppermute | solution.py:355
  111.5 26.2 %collective-permute-start.20 = (bf16[768,384]{1,0:T(8,128)(2,1)S(1)}, bf16[768,384]{1,0:T(8,128)(2,1)S(1)}, u32[]{:S(2)}, u32[]{:S(2)}) collective-permute-start(bf16[768,384]{1,0:T(8,128)(2,1)S(1)} %get-tuple-element.161), channel_id=1, source_target_pairs={{0,1},{1,0},{2,3},{3,2},{4,5},{5,4},{6,7},{7,6},{8,9},{9,8},{10,11... | collective-permute-start | bytes 1769480 | tf_op jit(solution)/shard_map/ppermute | solution.py:51
  147.2 44.4 %collective-permute-start.42 = (bf16[192,3072]{1,0:T(8,128)(2,1)}, bf16[192,3072]{1,0:T(8,128)(2,1)S(1)}, u32[]{:S(2)}, u32[]{:S(2)}) collective-permute-start(bf16[192,3072]{1,0:T(8,128)(2,1)} %get-tuple-element.173), channel_id=1, source_target_pairs={{0,2},{1,3},{2,0},{3,1},{4,6},{5,7},{6,4},{7,5},{8,10},{9,11},{10,... | collective-permute-start | bytes 3538952 | tf_op jit(solution)/shard_map/ppermute | solution.py:758
  151.4 37.9 %collective-permute-start.40 = (bf16[160,768]{1,0:T(8,128)(2,1)}, bf16[160,768]{1,0:T(8,128)(2,1)}, u32[]{:S(2)}, u32[]{:S(2)}) collective-permute-start(bf16[160,768]{1,0:T(8,128)(2,1)} %constant_dynamic-slice_fusion.12), channel_id=1, source_target_pairs={{0,2},{2,0},{1,3},{3,1},{4,6},{6,4},{5,7},{7,5},{8,10},{10,8},{9,1... | collective-permute-start | bytes 737288 | tf_op jit(solution)/shard_map/ppermute | solution.py:55
  154.0 55.2 %all-to-all-start = ((bf16[32,24,768]{2,1,0:T(8,128)(2,1)}), bf16[32,24,768]{2,1,0:T(8,128)(2,1)}, u32[]{:S(2)}, u32[]{:S(2)}) async-start(bf16[32,24,768]{2,1,0:T(8,128)(2,1)} %bitcast.173), calls=%async_computation | async-start | bytes 2359296 | tf_op jit(solution)/shard_map/all_to_all | solution.py:799
  192.6 28.5 %collective-permute-start.44 = (bf16[192,3072]{1,0:T(8,128)(2,1)}, bf16[192,3072]{1,0:T(8,128)(2,1)}, u32[]{:S(2)}, u32[]{:S(2)}) collective-permute-start(bf16[192,3072]{1,0:T(8,128)(2,1)} %copy-done.32), channel_id=1, source_target_pairs={{0,3},{1,2},{2,1},{3,0},{4,7},{5,6},{6,5},{7,4},{8,11},{9,10},{10,... | collective-permute-start | bytes 3538952 | tf_op jit(solution)/shard_map/ppermute | solution.py:758
  207.7 41.2 %collective-permute-start.47 = (bf16[192,3072]{1,0:T(8,128)(2,1)}, bf16[192,3072]{1,0:T(8,128)(2,1)}, u32[]{:S(2)}, u32[]{:S(2)}) collective-permute-start(bf16[192,3072]{1,0:T(8,128)(2,1)} %copy-done.31), channel_id=1, source_target_pairs={{0,2},{1,3},{2,0},{3,1},{4,6},{5,7},{6,4},{7,5},{8,10},{9,11},{10,... | collective-permute-start | bytes 3538952 | tf_op jit(solution)/shard_map/ppermute | solution.py:758
  208.3 44.2 %collective-permute-start.60 = (bf16[512,1536]{1,0:T(8,128)(2,1)}, bf16[512,1536]{1,0:T(8,128)(2,1)}, u32[]{:S(2)}, u32[]{:S(2)}) collective-permute-start(bf16[512,1536]{1,0:T(8,128)(2,1)} %copy-done.75), channel_id=1, source_target_pairs={{0,1},{1,0},{2,3},{3,2},{4,5},{5,4},{6,7},{7,6},{8,9},{9,8},{10,11... | collective-permute-start | bytes 4718600 | tf_op jit(solution)/shard_map/ppermute | solution.py:51
  226.5 39.4 %all-to-all-start.1 = ((bf16[32,24,768]{2,1,0:T(8,128)(2,1)}), bf16[32,24,768]{2,1,0:T(8,128)(2,1)}, u32[]{:S(2)}, u32[]{:S(2)}) async-start(bf16[32,24,768]{2,1,0:T(8,128)(2,1)} %bitcast.181), calls=%async_computation.1 | async-start | bytes 2359296 | tf_op jit(solution)/shard_map/all_to_all | solution.py:799
  240.8 39.2 %collective-permute-start.48 = (bf16[192,3072]{1,0:T(8,128)(2,1)}, bf16[192,3072]{1,0:T(8,128)(2,1)}, u32[]{:S(2)}, u32[]{:S(2)}) collective-permute-start(bf16[192,3072]{1,0:T(8,128)(2,1)} %get-tuple-element.191), channel_id=1, source_target_pairs={{0,1},{1,0},{2,3},{3,2},{4,5},{5,4},{6,7},{7,6},{8,9},{9,8},{10,11... | collective-permute-start | bytes 3538952 | tf_op jit(solution)/shard_map/ppermute | solution.py:758
  248.9 34.8 %collective-permute-start.49 = (bf16[192,3072]{1,0:T(8,128)(2,1)}, bf16[192,3072]{1,0:T(8,128)(2,1)}, u32[]{:S(2)}, u32[]{:S(2)}) collective-permute-start(bf16[192,3072]{1,0:T(8,128)(2,1)} %get-tuple-element.194), channel_id=1, source_target_pairs={{0,3},{1,2},{2,1},{3,0},{4,7},{5,6},{6,5},{7,4},{8,11},{9,10},{10,... | collective-permute-start | bytes 3538952 | tf_op jit(solution)/shard_map/ppermute | solution.py:758
  302.9 31.3 %all-to-all-start.2 = ((bf16[32,24,768]{2,1,0:T(8,128)(2,1)}), bf16[32,24,768]{2,1,0:T(8,128)(2,1)}, u32[]{:S(2)}, u32[]{:S(2)}) async-start(bf16[32,24,768]{2,1,0:T(8,128)(2,1)} %bitcast.26), calls=%async_computation.2 | async-start | bytes 2359296 | tf_op jit(solution)/shard_map/all_to_all | solution.py:803
  324.2 37.3 %collective-permute-start.52 = (bf16[192,3072]{1,0:T(8,128)(2,1)}, bf16[192,3072]{1,0:T(8,128)(2,1)}, u32[]{:S(2)}, u32[]{:S(2)}) collective-permute-start(bf16[192,3072]{1,0:T(8,128)(2,1)} %get-tuple-element.324), channel_id=1, source_target_pairs={{0,2},{1,3},{2,0},{3,1},{4,6},{5,7},{6,4},{7,5},{8,10},{9,11},{10,... | collective-permute-start | bytes 3538952 | tf_op jit(solution)/shard_map/ppermute | solution.py:758
  334.2 121.0 %all-to-all-start.3 = ((bf16[32,24,768]{2,1,0:T(8,128)(2,1)}), bf16[32,24,768]{2,1,0:T(8,128)(2,1)}, u32[]{:S(2)}, u32[]{:S(2)}) async-start(bf16[32,24,768]{2,1,0:T(8,128)(2,1)} %bitcast.180), calls=%async_computation.3 | async-start | bytes 2359296 | tf_op jit(solution)/shard_map/all_to_all | solution.py:803
  361.6 30.4 %collective-permute-start.53 = (bf16[192,3072]{1,0:T(8,128)(2,1)S(1)}, bf16[192,3072]{1,0:T(8,128)(2,1)S(1)}, u32[]{:S(2)}, u32[]{:S(2)}) collective-permute-start(bf16[192,3072]{1,0:T(8,128)(2,1)S(1)} %copy-done.82), channel_id=1, source_target_pairs={{0,3},{1,2},{2,1},{3,0},{4,7},{5,6},{6,5},{7,4},{8,11},{9,10},{10,... | collective-permute-start | bytes 3538952 | tf_op jit(solution)/shard_map/ppermute | solution.py:758
  398.6 56.6 %collective-permute-start.58 = (bf16[4,2,48,1536]{3,2,1,0:T(8,128)(2,1)}, bf16[4,2,48,1536]{3,2,1,0:T(8,128)(2,1)}, u32[]{:S(2)}, u32[]{:S(2)}) collective-permute-start(bf16[4,2,48,1536]{3,2,1,0:T(8,128)(2,1)} %get-tuple-element.340), channel_id=1, source_target_pairs={{0,4},{4,0},{1,5},{5,1},{2,6},{6,2},{3,7},{7,3},{8,12},{12,8},{9,1... | collective-permute-start | bytes 3538952 | tf_op jit(solution)/shard_map/ppermute | solution.py:436
  409.3 27.9 %collective-permute-start.56 = (bf16[192,3072]{1,0:T(8,128)(2,1)}, bf16[192,3072]{1,0:T(8,128)(2,1)}, u32[]{:S(2)}, u32[]{:S(2)}) collective-permute-start(bf16[192,3072]{1,0:T(8,128)(2,1)} %get-tuple-element.321), channel_id=1, source_target_pairs={{0,2},{1,3},{2,0},{3,1},{4,6},{5,7},{6,4},{7,5},{8,10},{9,11},{10,... | collective-permute-start | bytes 3538952 | tf_op jit(solution)/shard_map/ppermute | solution.py:758
  409.9 107.0 %collective-permute-start.70 = (bf16[192,3072]{1,0:T(8,128)(2,1)}, bf16[192,3072]{1,0:T(8,128)(2,1)}, u32[]{:S(2)}, u32[]{:S(2)}) collective-permute-start(bf16[192,3072]{1,0:T(8,128)(2,1)} %get-tuple-element.319), channel_id=1, source_target_pairs={{0,1},{1,0},{2,3},{3,2},{4,5},{5,4},{6,7},{7,6},{8,9},{9,8},{10,11... | collective-permute-start | bytes 3538952 | tf_op jit(solution)/shard_map/ppermute | solution.py:758
  443.7 43.7 %collective-permute-start.61 = (bf16[2,2,48,3072]{3,2,1,0:T(8,128)(2,1)}, bf16[2,2,48,3072]{3,2,1,0:T(8,128)(2,1)}, u32[]{:S(2)}, u32[]{:S(2)}) collective-permute-start(bf16[2,2,48,3072]{3,2,1,0:T(8,128)(2,1)} %get-tuple-element.328), channel_id=1, source_target_pairs={{0,4},{4,0},{1,5},{5,1},{2,6},{6,2},{3,7},{7,3},{8,12},{12,8},{9,1... | collective-permute-start | bytes 3538952 | tf_op jit(solution)/shard_map/ppermute | solution.py:400
  446.8 40.9 %collective-permute-start.62 = (bf16[2,2,48,3072]{3,2,1,0:T(8,128)(2,1)}, bf16[2,2,48,3072]{3,2,1,0:T(8,128)(2,1)}, u32[]{:S(2)}, u32[]{:S(2)}) collective-permute-start(bf16[2,2,48,3072]{3,2,1,0:T(8,128)(2,1)} %get-tuple-element.326), channel_id=1, source_target_pairs={{0,2},{2,0},{1,3},{3,1},{4,6},{6,4},{5,7},{7,5},{8,10},{10,8},{9,1... | collective-permute-start | bytes 3538952 | tf_op jit(solution)/shard_map/ppermute | solution.py:55
  448.3 70.4 %collective-permute-start.71 = (bf16[192,3072]{1,0:T(8,128)(2,1)}, bf16[192,3072]{1,0:T(8,128)(2,1)}, u32[]{:S(2)}, u32[]{:S(2)}) collective-permute-start(bf16[192,3072]{1,0:T(8,128)(2,1)} %get-tuple-element.224), channel_id=1, source_target_pairs={{0,3},{1,2},{2,1},{3,0},{4,7},{5,6},{6,5},{7,4},{8,11},{9,10},{10,... | collective-permute-start | bytes 3538952 | tf_op jit(solution)/shard_map/ppermute | solution.py:758
  461.4 50.9 %collective-permute-start.59 = (bf16[4,48,1536]{2,1,0:T(8,128)(2,1)}, bf16[4,48,1536]{2,1,0:T(8,128)(2,1)}, u32[]{:S(2)}, u32[]{:S(2)}) collective-permute-start(bf16[4,48,1536]{2,1,0:T(8,128)(2,1)} %get-tuple-element.348), channel_id=1, source_target_pairs={{0,2},{2,0},{1,3},{3,1},{4,6},{6,4},{5,7},{7,5},{8,10},{10,8},{9,1... | collective-permute-start | bytes 1769480 | tf_op jit(solution)/shard_map/ppermute | solution.py:55
  487.4 31.8 %collective-permute-start.65 = (bf16[2,2,48,1664]{3,2,1,0:T(8,128)(2,1)S(1)}, bf16[2,2,48,1664]{3,2,1,0:T(8,128)(2,1)S(1)}, u32[]{:S(2)}, u32[]{:S(2)}) collective-permute-start(bf16[2,2,48,1664]{3,2,1,0:T(8,128)(2,1)S(1)} %get-tuple-element.338), channel_id=1, source_target_pairs={{0,4},{4,0},{1,5},{5,1},{2,6},{6,2},{3,7},{7,3},{8,12},{12,8},{9,1... | collective-permute-start | bytes 1916936 | tf_op jit(solution)/shard_map/ppermute | solution.py:400
  487.7 38.2 %collective-permute-start.66 = (bf16[2,2,48,1664]{3,2,1,0:T(8,128)(2,1)S(1)}, bf16[2,2,48,1664]{3,2,1,0:T(8,128)(2,1)S(1)}, u32[]{:S(2)}, u32[]{:S(2)}) collective-permute-start(bf16[2,2,48,1664]{3,2,1,0:T(8,128)(2,1)S(1)} %get-tuple-element.336), channel_id=1, source_target_pairs={{0,2},{2,0},{1,3},{3,1},{4,6},{6,4},{5,7},{7,5},{8,10},{10,8},{9,1... | collective-permute-start | bytes 1916936 | tf_op jit(solution)/shard_map/ppermute | solution.py:55
  519.2 28.4 %collective-permute-start.63 = (bf16[320,768]{1,0:T(8,128)(2,1)S(1)}, bf16[320,768]{1,0:T(8,128)(2,1)S(1)}, u32[]{:S(2)}, u32[]{:S(2)}) collective-permute-start(bf16[320,768]{1,0:T(8,128)(2,1)S(1)} %slice.588), channel_id=1, source_target_pairs={{0,2},{2,0},{1,3},{3,1},{4,6},{6,4},{5,7},{7,5},{8,10},{10,8},{9,1... | collective-permute-start | bytes 1474568 | tf_op jit(solution)/shard_map/ppermute | solution.py:55
  525.8 30.0 %collective-permute-start.74 = (bf16[2,48,3072]{2,1,0:T(8,128)(2,1)S(1)}, bf16[2,48,3072]{2,1,0:T(8,128)(2,1)S(1)}, u32[]{:S(2)}, u32[]{:S(2)}) collective-permute-start(bf16[2,48,3072]{2,1,0:T(8,128)(2,1)S(1)} %get-tuple-element.346), channel_id=1, source_target_pairs={{0,2},{2,0},{1,3},{3,1},{4,6},{6,4},{5,7},{7,5},{8,10},{10,8},{9,1... | collective-permute-start | bytes 1769480 | tf_op jit(solution)/shard_map/ppermute | solution.py:55
  527.0 28.9 %collective-permute-start.75 = (bf16[2,48,3072]{2,1,0:T(8,128)(2,1)S(1)}, bf16[2,48,3072]{2,1,0:T(8,128)(2,1)S(1)}, u32[]{:S(2)}, u32[]{:S(2)}) collective-permute-start(bf16[2,48,3072]{2,1,0:T(8,128)(2,1)S(1)} %get-tuple-element.344), channel_id=1, source_target_pairs={{0,4},{4,0},{1,5},{5,1},{2,6},{6,2},{3,7},{7,3},{8,12},{12,8},{9,1... | collective-permute-start | bytes 1769480 | tf_op jit(solution)/shard_map/ppermute | solution.py:409
  (217 other events, 2115.8 us)
Sparse Core Ops, SparseCore 0:
  32.5 71.6 all-gather.1
